TPU v7x, 32 devices: a whole 2x2x4 slice. The times are simulated.
32 devices in a mesh: group: 2 (over y), ep: 8 (over z, core), dp: 2 (over x).
Axes of the slice: x: 2, y: 2, z: 4, core: 2. Of those that a mesh axis runs over, the one named last changes fastest.
Arguments:
- tokens: bfloat16 [256, 7168], P(('group', 'ep', 'dp')), parts along dimension 0, may hold values from -6 to 6
- expert_ids: int32 [256, 2], P(('group', 'ep', 'dp')), parts along dimension 0, may hold values from 0 to 7, all different within a row; in each aligned block of 8 rows (0 to 7, 8 to 15, ...) at most 3 rows name the same one
- gate_weights: float32 [256, 2], P(('group', 'ep', 'dp')), parts along dimension 0, may hold values from 0.5 to 2.5
- w_gate: bfloat16 [8, 7168, 2048], P('ep', None, 'dp'), may hold values from -0.0625 to 0.0625
- w_up: bfloat16 [8, 7168, 2048], P('ep', None, 'dp'), may hold values from -0.0625 to 0.0625
- w_down: bfloat16 [8, 2048, 7168], P('ep', 'dp'), may hold values from -0.125 to 0.125
- queries: bfloat16 [64, 128, 576], P(('group', 'ep', 'dp')), parts along dimension 0
- cache: bfloat16 [64, 512, 576], P(('group', 'ep', 'dp')), parts along dimension 0
- lengths: int32 [64], P(('group', 'ep', 'dp')), parts along dimension 0, may hold values from 1 to 512, 8192 in all
Outputs:
- moe_out: bfloat16 [256, 7168], P(('group', 'ep', 'dp')), parts along dimension 0
- attn_out: bfloat16 [64, 128, 512], P(('group', 'ep', 'dp')), parts along dimension 0
There are 2 independent parts, one for each index of `group`. A program takes and returns all parts, laid end to end along the dimension named above; an argument that names none is the same for every part. Nothing has to cross between parts.
Inputs may be any that keep to these rules, and one draw needn't show every extreme that they name: `expert_ids`: in the rows of one device no expert is named by more than 3 routes, and some device reaches 3.
All inputs are finite; a program needn't handle non-finite values. No bound on the sum of `lengths` on one device may be relied on, other than what follows from the above.
Results may differ from a plain program's by a relative error of at most 0.009.
Values may be sent and summed in bfloat16 or wider, within the bound.
No kernel may reach another device: no remote copies, remote signals or barrier semaphores. Data moves between devices by JAX's collectives and lax.ppermute only.
A program may use at most 128 MiB of HBM per device.

v0:
```python
import jax
import jax.numpy as jnp
from jax import lax
from jax.sharding import PartitionSpec as P

ROPE = 64


softmax_scale = 1.0 / 192.0**0.5


def expert_rows(inputs, w_gate, w_up, w_down):
    gate = jnp.dot(inputs, w_gate[0], preferred_element_type=jnp.float32)
    upper = jnp.dot(inputs, w_up[0], preferred_element_type=jnp.float32)
    hidden = (jax.nn.silu(gate) * upper).astype(jnp.bfloat16)
    return jnp.dot(hidden, w_down[0], preferred_element_type=jnp.float32)


def attend(queries, cache, lengths):
    width = cache.shape[1]
    latent = cache.shape[2] - ROPE
    scores = (
        jnp.einsum("rhc,rlc->rhl", queries, cache, preferred_element_type=jnp.float32)
        * softmax_scale
    )
    valid = jnp.arange(width, dtype=jnp.int32)[None, None, :] < lengths[:, None, None]
    scores = jnp.where(valid, scores, -jnp.inf)
    probs = jax.nn.softmax(scores, axis=-1).astype(jnp.bfloat16)
    return jnp.einsum(
        "rhl,rlc->rhc", probs, cache[:, :, :latent], preferred_element_type=jnp.float32
    ).astype(jnp.bfloat16)


def per_device(tokens, expert_ids, gate_weights, w_gate, w_up, w_down, queries, cache, lengths):
    n_ep = lax.axis_size("ep")
    n_dp = lax.axis_size("dp")
    tok_rows = tokens.shape[0]
    width = tokens.shape[1]
    top = expert_ids.shape[1]
    capacity = (3 * tok_rows * top + 2 * n_ep - 1) // (2 * n_ep)
    flat_ids = expert_ids.reshape(-1)
    onehot = (flat_ids[:, None] == jnp.arange(n_ep, dtype=jnp.int32)[None, :]).astype(jnp.int32)
    slots = jnp.sum((jnp.cumsum(onehot, axis=0) - 1) * onehot, axis=1)
    target = (flat_ids * capacity + slots).reshape(tok_rows, top)
    places = jnp.arange(n_ep * capacity, dtype=jnp.int32)[:, None, None]
    selector = jnp.sum((places == target[None, :, :]).astype(jnp.bfloat16), axis=2)
    buffer = jnp.dot(selector, tokens, preferred_element_type=jnp.float32).astype(jnp.bfloat16)
    spread = jnp.broadcast_to(
        buffer.reshape(n_ep, 1, capacity, width), (n_ep, n_dp, capacity, width)
    )
    arrived = lax.all_to_all(
        spread.reshape(n_ep * n_dp, capacity, width),
        ("ep", "dp"),
        split_axis=0,
        concat_axis=0,
        tiled=True,
    )
    partial_out = expert_rows(arrived.reshape(-1, width), w_gate, w_up, w_down).astype(jnp.bfloat16)
    returned = lax.all_to_all(
        partial_out.reshape(arrived.shape), ("ep", "dp"), split_axis=0, concat_axis=0, tiled=True
    )
    combined = jnp.sum(returned.reshape(n_ep, n_dp, capacity, width), axis=1, dtype=jnp.float32)
    picked = combined.reshape(n_ep * capacity, width)[target]
    moe_out = jnp.sum(gate_weights[:, :, None] * picked, axis=1).astype(jnp.bfloat16)
    attn_out = attend(queries, cache, lengths)
    return (moe_out, attn_out)


def solution(mesh):
    placed = (
        P(("group", "ep", "dp"), None),
        P(("group", "ep", "dp"), None),
        P(("group", "ep", "dp"), None),
        P("ep", None, "dp"),
        P("ep", None, "dp"),
        P("ep", "dp", None),
        P(("group", "ep", "dp"), None, None),
        P(("group", "ep", "dp"), None, None),
        P(("group", "ep", "dp")),
    )
    return jax.shard_map(
        per_device,
        mesh=mesh,
        in_specs=placed,
        out_specs=(P(("group", "ep", "dp"), None), P(("group", "ep", "dp"), None, None)),
        check_vma=False,
    )
```

profile of v0, /device:TPU:0, one launch (start us, length us, event | category | flops | bytes accessed | tf_op | source)
XLA Modules:
  0.0 87.1 jit_solution(17117968551570698455)
XLA Ops:
  0.6 0.0 copy-start
  0.6 0.8 copy.20
  1.4 0.1 eq.29
  1.5 0.1 fusion.29
  1.6 0.2 select_reduce_fusion
  1.8 0.1 reduce_sum.51
  1.9 0.1 copy.22
  2.0 0.1 fusion.31
  2.1 1.2 %convolution_convert_fusion = bf16[24,7168]{1,0:T(8,128)(2,1)S(1)} fusion(bf16[24,8]{0,1:T(8,128)(2,1)S(1)} %fusion.31, bf16[8,7168]{1,0:T(8,128)(2,1)} %param.9), kind=kOutput, calls=%fused_computation.9 | convolution fusion | flops 2924544 | bytes 459136 | tf_op jit(solution)/shard_map/dot_general | solution.py:47
  3.3 0.2 broadcast_in_dim.18
  3.5 0.2 broadcast_in_dim.30
  3.7 30.7 %all_to_all.10 = bf16[16,3,7168]{2,1,0:T(4,128)(2,1)S(1)} all-to-all(bf16[16,3,7168]{2,1,0:T(4,128)(2,1)S(1)} %bitcast.29), channel_id=1, replica_groups=mesh['group'=2,'ep'=8,'dp'=2] {'ep','dp'}, dimensions={0} | all-to-all | bytes 1376256 | tf_op jit(solution)/shard_map/all_to_all | solution.py:51
  34.4 0.6 reshape.56
  35.0 7.8 %fusion.5 = f32[48,1024]{1,0:T(8,128)S(1)} fusion(bf16[48,7168]{1,0:T(8,128)(2,1)S(1)} %reshape.56, bf16[1,7168,1024]{2,1,0:T(8,128)(2,1)} %param.12), kind=kOutput, calls=%fused_computation.6 | convolution fusion | flops 704643072 | bytes 15564800 | tf_op jit(solution)/shard_map/dot_general | solution.py:13
  42.8 0.0 copy-start.2
  42.9 0.0 copy-start.3
  42.9 0.0 copy-start.1
  42.9 14.7 %fusion.7 = bf16[48,7168]{1,0:T(8,128)(2,1)S(1)} fusion(bf16[1,1024,7168]{2,1,0:T(8,128)(2,1)} %param.14, bf16[48,7168]{1,0:T(8,128)(2,1)S(1)} %reshape.56, bf16[1,7168,1024]{2,1,0:T(8,128)(2,1)} %param.13, f32[48,1024]{1,0:T(8,128)S(1)} %fusion.5), kind=kOutput, calls=%fused_computation.8 | convolution fusion | flops 1409925120 | bytes 30932992 | tf_op jit(solution)/shard_map/dot_general | solution.py:16
  57.6 1.2 %reshape.57 = bf16[16,3,7168]{2,1,0:T(4,128)(2,1)} reshape(bf16[48,7168]{1,0:T(8,128)(2,1)S(1)} %fusion.7) | data formatting | bytes 1376256 | tf_op jit(solution)/shard_map/reshape | solution.py:60
  58.8 3.7 %all-to-all-start.1 = ((bf16[16,3,7168]{2,1,0:T(4,128)(2,1)}), bf16[16,3,7168]{2,1,0:T(4,128)(2,1)S(1)}, u32[]{:S(2)}, u32[]{:S(2)}) async-start(bf16[16,3,7168]{2,1,0:T(4,128)(2,1)} %reshape.57), calls=%async_computation.1 | async-start | bytes 1835008 | tf_op jit(solution)/shard_map/all_to_all | solution.py:59
  62.5 0.1 reshape.62
  62.6 0.0 copy-done.2
  62.6 0.1 copy.19
  62.6 0.0 copy-done.3
  62.6 0.1 iota_compare_fusion.2
  62.7 0.0 copy-done
  62.7 0.0 copy-done.1
  62.7 0.4 fusion.11
  63.2 0.2 fusion.34
  63.4 1.3 %convolution_convert_fusion.1 = bf16[2,128,512]{2,1,0:T(8,128)(2,1)} fusion(bf16[2,512,576]{1,2,0:T(8,128)(2,1)S(1)} %copy-done.1, f32[2,128]{1,0:T(2,128)S(1)} %fusion.34, f32[2,128,512]{2,1,0:T(8,128)S(1)} %fusion.11), kind=kOutput, calls=%fused_computation.15 | convolution fusion | flops 134742784 | bytes 2360320 | tf_op jit(solution)/shard_map/rhl,rlc->rhc/dot_general | solution.py:29
  64.7 19.2 %all-to-all-done.1 = bf16[16,3,7168]{2,1,0:T(4,128)(2,1)S(1)} async-done(((bf16[16,3,7168]{2,1,0:T(4,128)(2,1)}), bf16[16,3,7168]{2,1,0:T(4,128)(2,1)S(1)}, u32[]{:S(2)}, u32[]{:S(2)}) %all-to-all-start.1) | async-done | bytes 688160 | tf_op jit(solution)/shard_map/all_to_all | solution.py:59
  83.9 0.5 convert_reduce_fusion
  84.4 0.3 reshape.58
  84.8 0.7 gather_fusion
  85.5 0.3 reshape.61
  85.8 1.3 %multiply_reduce_fusion = bf16[8,7168]{1,0:T(8,128)(2,1)} fusion(f32[8,2,7168]{2,1,0:T(2,128)S(1)} %reshape.61, f32[8,2]{1,0:T(8,128)S(1)} %copy.19), kind=kLoop, calls=%fused_computation.20 | loop fusion | flops 172032 | bytes 573504 | tf_op jit(solution)/shard_map/reduce_sum | solution.py:64
  (3 shorter events, 0.1 us)
Async XLA Ops:
  0.6 62.1 %copy-start = (bf16[2,128,576]{1,2,0:T(8,128)(2,1)S(1)}, bf16[2,128,576]{1,2,0:T(8,128)(2,1)}, u32[]{:S(2)}) copy-start(bf16[2,128,576]{1,2,0:T(8,128)(2,1)} %param.15) | copy-start | bytes 884740
  42.8 19.7 %copy-start.2 = (f32[8,2]{0,1:T(2,128)S(1)}, f32[8,2]{0,1:T(2,128)}, u32[]{:S(2)}) copy-start(f32[8,2]{0,1:T(2,128)} %param.11) | copy-start | bytes 196
  42.9 19.8 %copy-start.3 = (s32[2]{0:T(128)S(1)}, s32[2]{0:T(128)}, u32[]{:S(2)}) copy-start(s32[2]{0:T(128)} %param.17) | copy-start | bytes 28
  42.9 19.9 %copy-start.1 = (bf16[2,512,576]{1,2,0:T(8,128)(2,1)S(1)}, bf16[2,512,576]{1,2,0:T(8,128)(2,1)}, u32[]{:S(2)}) copy-start(bf16[2,512,576]{1,2,0:T(8,128)(2,1)} %param.16) | copy-start | bytes 3538948
  58.8 25.1 %all-to-all-start.1 = ((bf16[16,3,7168]{2,1,0:T(4,128)(2,1)}), bf16[16,3,7168]{2,1,0:T(4,128)(2,1)S(1)}, u32[]{:S(2)}, u32[]{:S(2)}) async-start(bf16[16,3,7168]{2,1,0:T(4,128)(2,1)} %reshape.57), calls=%async_computation.1 | async-start | bytes 1835008 | tf_op jit(solution)/shard_map/all_to_all | solution.py:59
where the time goes:
time: 88.1 us; the launch traced here: 87.1 us
  blocking collectives  30.7 us (35%)
  matrix products  25.5 us (29%)
  waiting for transfers between devices  19.2 us (22%)
  local copies, waits for them, and re-layouts  4.81 us (5%)
  starting transfers between devices  3.66 us (4%)
  other arithmetic  2.51 us (3%)
    all_to_all x1, blocking collectives, per_device(): lax.all_to_all(spread.reshape(n_ep * n_dp, capacity, width), ('ep', 'dp')...  30.7 us
    all_to_all x1, waiting for transfers between devices, per_device(): lax.all_to_all(partial_out.reshape(arrived.shape), ('ep', 'dp'), split_ax...  19.2 us
    dot_general x1, matrix products, expert_rows(): return jnp.dot(hidden, w_down[0], preferred_element_type=jnp.float32)  14.7 us
    dot_general x1, matrix products, expert_rows(): gate = jnp.dot(inputs, w_gate[0], preferred_element_type=jnp.float32)  7.83 us
    all_to_all x1, starting transfers between devices, per_device(): lax.all_to_all(partial_out.reshape(arrived.shape), ('ep', 'dp'), split_ax...  3.66 us
  transfers between devices with their start and end apart: 1, of which 1 were waited for; matrix products, arithmetic and copies ran while one was open for 3% of the time, Pallas kernels for 0%

commit v1 on v0

--- a/solution.py
+++ b/solution.py
@@ -1,10 +1,15 @@
+import functools
+
 import jax
 import jax.numpy as jnp
 from jax import lax
+from jax.experimental import pallas as pl
+from jax.experimental.pallas import tpu as pltpu
 from jax.sharding import PartitionSpec as P
 
 ROPE = 64
-
+CORES = 2
+MIB = 1 << 20
 
 softmax_scale = 1.0 / 192.0**0.5
 
@@ -31,13 +36,13 @@
     ).astype(jnp.bfloat16)
 
 
-def per_device(tokens, expert_ids, gate_weights, w_gate, w_up, w_down, queries, cache, lengths):
+def plain(tokens, expert_ids, gate_weights, w_gate, w_up, w_down, queries, cache, lengths):
     n_ep = lax.axis_size("ep")
     n_dp = lax.axis_size("dp")
     tok_rows = tokens.shape[0]
     width = tokens.shape[1]
     top = expert_ids.shape[1]
-    capacity = (3 * tok_rows * top + 2 * n_ep - 1) // (2 * n_ep)
+    capacity = slots_per_expert(tok_rows, top, n_ep)
     flat_ids = expert_ids.reshape(-1)
     onehot = (flat_ids[:, None] == jnp.arange(n_ep, dtype=jnp.int32)[None, :]).astype(jnp.int32)
     slots = jnp.sum((jnp.cumsum(onehot, axis=0) - 1) * onehot, axis=1)
@@ -64,6 +69,314 @@
     moe_out = jnp.sum(gate_weights[:, :, None] * picked, axis=1).astype(jnp.bfloat16)
     attn_out = attend(queries, cache, lengths)
     return (moe_out, attn_out)
+
+
+def slots_per_expert(tok_rows, top, n_ep):
+    return (3 * tok_rows * top + 2 * n_ep - 1) // (2 * n_ep)
+
+
+def iota(shape, dim):
+    return lax.broadcasted_iota(jnp.int32, shape, dim)
+
+
+def split(value, *sizes):
+    digits = []
+    for size in reversed(sizes):
+        digits.append(lax.rem(value, size))
+        value = lax.div(value, size)
+    return [value] + digits[::-1]
+
+
+def ones(mask):
+    return jnp.where(mask, 1.0, 0.0).astype(jnp.bfloat16)
+
+
+def dot(a, b):
+    return jnp.dot(a, b, preferred_element_type=jnp.float32)
+
+
+def slot_table(ids_ref, chip, chips, pieces, capacity, which=None):
+    rows = chips * pieces * CORES * capacity
+    top, toks = ids_ref.shape
+    away, piece, core, slot = split(iota((rows, toks), 0), pieces, CORES, capacity)
+    expert = (chip ^ away) * CORES + core
+    named = [ids_ref[k : k + 1, :] == expert for k in range(top)]
+    any_named = functools.reduce(jnp.logical_or, named)
+    before = ones(iota((toks, toks), 0) < iota((toks, toks), 1))
+    rank = dot(ones(any_named), before)
+    return (any_named if which is None else named[which]) & (rank == slot.astype(jnp.float32))
+
+
+def spread_pieces(table, chips, pieces, capacity):
+    rows, toks = table.shape
+    repeat = ones(iota((toks, pieces * toks), 0) == lax.rem(iota((toks, pieces * toks), 1), toks))
+    wide = dot(ones(table), repeat)
+    _, piece, _, _ = split(iota(wide.shape, 0), pieces, CORES, capacity)
+    return jnp.where(piece == lax.div(iota(wide.shape, 1), toks), wide, 0.0).astype(jnp.bfloat16)
+
+
+def chip_index():
+    return lax.div(lax.axis_index("ep"), CORES)
+
+
+def core_index():
+    return lax.rem(lax.axis_index("ep"), CORES)
+
+
+def pack_kernel(pieces, capacity, ids_ref, tok_ref, *outs):
+    chips = len(outs)
+    wide = tok_ref.shape[1] // pieces
+    table = slot_table(ids_ref, chip_index(), chips, pieces, capacity)
+    select = spread_pieces(table, chips, pieces, capacity)
+    toks = tok_ref[...].astype(jnp.float32)
+    stacked = jnp.concatenate(
+        [toks[:, k * wide : (k + 1) * wide] for k in range(pieces)], axis=0
+    ).astype(jnp.bfloat16)
+    packed = dot(select, stacked).astype(jnp.bfloat16)
+    rows = outs[0].shape[0]
+    for d, out in enumerate(outs):
+        out[...] = packed[d * rows : (d + 1) * rows]
+
+
+def near_kernel(far_pieces, near_pieces, capacity, chips, *refs):
+    ins, (same, other, stack) = refs[:chips], refs[chips:]
+    rows = ins[0].shape[0]
+    for d, ref in enumerate(ins):
+        stack[d * rows : (d + 1) * rows] = ref[...]
+    ratio = far_pieces // near_pieces
+    wide = ins[0].shape[1]
+    shape = (same.shape[0], stack.shape[0])
+    piece, away, slot = split(iota(shape, 0), chips, capacity)
+    from_away, from_piece, from_core, from_slot = split(iota(shape, 1), far_pieces, CORES, capacity)
+    match = (away == from_away) & (slot == from_slot)
+    for out, core in ((same, core_index()), (other, 1 - core_index())):
+        for h in range(ratio):
+            pick = ones(match & (from_core == core) & (from_piece == piece * ratio + h))
+            out[:, h * wide : (h + 1) * wide] = dot(pick, stack[...]).astype(jnp.bfloat16)
+
+
+def expert_kernel(pieces, *refs):
+    ins, (w_gate, w_up, w_down), outs, (stack, hidden) = refs[:4], refs[4:7], refs[7:11], refs[11:]
+    rows, wide = ins[0].shape
+    part = rows // pieces
+    total = 4 * part
+    for s, ref in enumerate(ins):
+        stack[s * rows : (s + 1) * rows] = ref[...]
+    shape = (total, 4 * rows)
+    who, which = split(iota(shape, 0), part)
+    from_who, from_piece, from_which = split(iota(shape, 1), pieces, part)
+    match = (who == from_who) & (which == from_which)
+    gate = up = None
+    for k in range(pieces):
+        x = dot(ones(match & (from_piece == k)), stack[...]).astype(jnp.bfloat16)
+        g = dot(x, w_gate[k * wide : (k + 1) * wide, :])
+        u = dot(x, w_up[k * wide : (k + 1) * wide, :])
+        gate, up = (g, u) if gate is None else (gate + g, up + u)
+    hidden[...] = (gate / (1.0 + jnp.exp(-gate)) * up).astype(jnp.bfloat16)
+    for k in range(pieces):
+        stack[k * total : (k + 1) * total] = dot(
+            hidden[...], w_down[:, k * wide : (k + 1) * wide]
+        ).astype(jnp.bfloat16)
+    shape = (4 * rows, pieces * total)
+    who, piece, which = split(iota(shape, 0), pieces, part)
+    from_piece, from_who, from_which = split(iota(shape, 1), 4, part)
+    back = dot(
+        ones((who == from_who) & (piece == from_piece) & (which == from_which)), stack[...]
+    ).astype(jnp.bfloat16)
+    for s, out in enumerate(outs):
+        out[...] = back[s * rows : (s + 1) * rows]
+
+
+def sum_kernel(far_pieces, near_pieces, capacity, chips, own, along, core_ref, across, *refs):
+    outs, (stack,) = refs[:chips], refs[chips:]
+    rows = own.shape[0]
+    ratio = far_pieces // near_pieces
+    wide = outs[0].shape[1]
+    f32 = jnp.float32
+    stack[:rows] = (own[...].astype(f32) + along[...].astype(f32)).astype(jnp.bfloat16)
+    stack[rows:] = (core_ref[...].astype(f32) + across[...].astype(f32)).astype(jnp.bfloat16)
+    far_rows = outs[0].shape[0]
+    shape = (chips * far_rows, 2 * rows)
+    away, piece, core, slot = split(iota(shape, 0), far_pieces, CORES, capacity)
+    from_other, from_piece, from_away, from_slot = split(
+        iota(shape, 1), near_pieces, chips, capacity
+    )
+    match = (
+        (away == from_away)
+        & (slot == from_slot)
+        & ((core != core_index()) == (from_other == 1))
+        & (lax.div(piece, ratio) == from_piece)
+    )
+    sent = None
+    for h in range(ratio):
+        term = dot(
+            ones(match & (lax.rem(piece, ratio) == h)), stack[:, h * wide : (h + 1) * wide]
+        )
+        sent = term if sent is None else sent + term
+    sent = sent.astype(jnp.bfloat16)
+    for d, out in enumerate(outs):
+        out[...] = sent[d * far_rows : (d + 1) * far_rows]
+
+
+def combine_kernel(pieces, capacity, chips, ids_ref, gains_ref, *refs):
+    ins, (out, stack) = refs[:chips], refs[chips:]
+    rows, wide = ins[0].shape
+    top, toks = ids_ref.shape
+    for d, ref in enumerate(ins):
+        stack[d * rows : (d + 1) * rows] = ref[...]
+    eye = iota((toks, toks), 0) == iota((toks, toks), 1)
+    total = None
+    for k in range(top):
+        table = slot_table(ids_ref, chip_index(), chips, pieces, capacity, k)
+        select = spread_pieces(table, chips, pieces, capacity)
+        picked = lax.dot_general(
+            select, stack[...], (((0,), (0,)), ((), ())), preferred_element_type=jnp.float32
+        )
+        gain = jnp.sum(jnp.where(eye, gains_ref[k : k + 1, :], 0.0), axis=1, keepdims=True)
+        terms = [picked[p * toks : (p + 1) * toks] * gain for p in range(pieces)]
+        total = terms if total is None else [a + b for a, b in zip(total, terms)]
+    for p in range(pieces):
+        out[:, p * wide : (p + 1) * wide] = total[p].astype(jnp.bfloat16)
+
+
+def start_copies(pairs, sems, cuts):
+    copies = []
+    for i, (src, dst) in enumerate(pairs):
+        rows = src.shape[0] // cuts
+        for j in range(cuts):
+            span = pl.ds(j * rows, rows)
+            copy = pltpu.make_async_copy(src.at[span], dst.at[span], sems.at[i * cuts + j])
+            copy.start()
+            copies.append(copy)
+    return copies
+
+
+def fetch_kernel(cuts, after, w_gate, w_up, got_gate, got_up, sems):
+    del after
+    for copy in start_copies([(w_gate, got_gate), (w_up, got_up)], sems, cuts):
+        copy.wait()
+
+
+def attend_kernel(cuts, latent, after, lengths, w_down, queries, cache, got_down, out, sems):
+    del after
+    copies = start_copies([(w_down, got_down)], sems, cuts)
+    requests, _, heads = queries.shape
+    width = cache.shape[2]
+    for r in range(requests):
+        scores = (
+            lax.dot_general(
+                queries[r], cache[r], (((0,), (0,)), ((), ())), preferred_element_type=jnp.float32
+            )
+            * softmax_scale
+        )
+        scores = jnp.where(iota((heads, width), 1) < lengths[r], scores, -jnp.inf)
+        weights = jnp.exp(scores - jnp.max(scores, axis=1, keepdims=True))
+        probs = (weights / jnp.sum(weights, axis=1, keepdims=True)).astype(jnp.bfloat16)
+        out[r] = lax.dot_general(
+            probs,
+            cache[r, :latent, :],
+            (((1,), (1,)), ((), ())),
+            preferred_element_type=jnp.float32,
+        ).astype(jnp.bfloat16)
+    for copy in copies:
+        copy.wait()
+
+
+VMEM = pl.BlockSpec(memory_space=pltpu.VMEM)
+HBM = pl.BlockSpec(memory_space=pltpu.HBM)
+SMEM = pl.BlockSpec(memory_space=pltpu.SMEM)
+
+
+def call(kernel, name, out_shape, in_specs, out_specs, scratch, limit, args, flops=0, moved=0):
+    return pl.pallas_call(
+        kernel,
+        name=name,
+        out_shape=out_shape,
+        in_specs=in_specs,
+        out_specs=out_specs,
+        scratch_shapes=scratch,
+        compiler_params=pltpu.CompilerParams(vmem_limit_bytes=limit),
+        cost_estimate=pl.CostEstimate(flops=flops, bytes_accessed=moved, transcendentals=0),
+    )(*args)
+
+
+def paired(n_ep, tokens, expert_ids, gate_weights, w_gate, w_up, w_down, queries, cache, lengths):
+    chips = n_ep // CORES
+    toks, width = tokens.shape
+    top = expert_ids.shape[1]
+    bf16 = jnp.bfloat16
+    capacity = slots_per_expert(toks, top, n_ep)
+    far_pieces, near_pieces = 8, 4
+    far_rows, near_rows = far_pieces * CORES * capacity, near_pieces * chips * capacity
+    far = jax.ShapeDtypeStruct((far_rows, width // far_pieces), bf16)
+    near = jax.ShapeDtypeStruct((near_rows, width // near_pieces), bf16)
+    w_gate, w_up, w_down = w_gate[0], w_up[0], w_down[0]
+    units = w_gate.shape[1]
+    ids, gains = expert_ids.T, gate_weights.T
+
+    def to_chip(x, d):
+        return lax.ppermute(x, "ep", [(i, i ^ (CORES * d)) for i in range(n_ep)])
+
+    def to_core(x):
+        return lax.ppermute(x, "ep", [(i, i ^ 1) for i in range(n_ep)])
+
+    def along_dp(x):
+        return lax.ppermute(x, "dp", [(0, 1), (1, 0)])
+
+    def across(x):
+        return lax.ppermute(x, ("ep", "dp"), [(i, i ^ 3) for i in range(2 * n_ep)])
+
+    packed = call(
+        functools.partial(pack_kernel, far_pieces, capacity),
+        "pack", (far,) * chips, [VMEM] * 2, (VMEM,) * chips, [], 4 * MIB, (ids, tokens),
+    )
+    landed = [packed[0]] + [to_chip(packed[d], d) for d in range(1, chips)]
+    cuts = 8
+    got_gate, got_up = call(
+        functools.partial(fetch_kernel, cuts),
+        "fetch",
+        (pltpu.VMEM(w_gate.shape, bf16), pltpu.VMEM(w_up.shape, bf16)),
+        [HBM] * 3, (VMEM, VMEM), [pltpu.SemaphoreType.DMA((2 * cuts,))], 1 * MIB,
+        (packed[0], w_gate, w_up), moved=2 * 2 * w_gate.size,
+    )
+    same, other = call(
+        functools.partial(near_kernel, far_pieces, near_pieces, capacity, chips),
+        "near", (near,) * 2, [VMEM] * chips, (VMEM,) * 2,
+        [pltpu.VMEM((chips * far_rows, width // far_pieces), bf16)], 4 * MIB, landed,
+    )
+    arrived = [same, along_dp(same), to_core(other), across(other)]
+    latent = cache.shape[2] - ROPE
+    got_down, attn_out = call(
+        functools.partial(attend_kernel, cuts, latent),
+        "attend",
+        (
+            pltpu.VMEM(w_down.shape, bf16),
+            jax.ShapeDtypeStruct(queries.shape[:2] + (latent,), bf16),
+        ),
+        [HBM, SMEM, HBM, VMEM, VMEM], (VMEM, VMEM), [pltpu.SemaphoreType.DMA((cuts,))], 8 * MIB,
+        (same, lengths, w_down, queries.swapaxes(1, 2), cache.swapaxes(1, 2)),
+        moved=2 * w_down.size,
+    )
+    rows = 4 * near_rows // near_pieces
+    parts = call(
+        functools.partial(expert_kernel, near_pieces),
+        "experts", (near,) * 4, [VMEM] * 7, (VMEM,) * 4,
+        [pltpu.VMEM((4 * near_rows, width // near_pieces), bf16), pltpu.VMEM((rows, units), bf16)],
+        8 * MIB, (*arrived, got_gate, got_up, got_down), flops=6 * rows * width * units,
+    )
+    sums = call(
+        functools.partial(sum_kernel, far_pieces, near_pieces, capacity, chips),
+        "sums", (far,) * chips, [VMEM] * 4, (VMEM,) * chips,
+        [pltpu.VMEM((2 * near_rows, width // near_pieces), bf16)], 6 * MIB,
+        (parts[0], along_dp(parts[1]), to_core(parts[2]), across(parts[3])),
+    )
+    back = [sums[0]] + [to_chip(sums[d], d) for d in range(1, chips)]
+    moe_out = call(
+        functools.partial(combine_kernel, far_pieces, capacity, chips),
+        "combine", jax.ShapeDtypeStruct(tokens.shape, bf16), [VMEM] * (2 + chips), VMEM,
+        [pltpu.VMEM((chips * far_rows, width // far_pieces), bf16)], 4 * MIB, (ids, gains, *back),
+    )
+    return moe_out, attn_out
 
 
 def solution(mesh):
@@ -78,8 +391,10 @@
         P(("group", "ep", "dp"), None, None),
         P(("group", "ep", "dp")),
     )
+    n_ep, n_dp = mesh.shape["ep"], mesh.shape["dp"]
+    fits = n_dp == 2 and n_ep == 8
     return jax.shard_map(
-        per_device,
+        functools.partial(paired, n_ep) if fits else plain,
         mesh=mesh,
         in_specs=placed,
         out_specs=(P(("group", "ep", "dp"), None), P(("group", "ep", "dp"), None, None)),

time: 88.1 us -> 97.8 us (1.11)
  local copies, waits for them, and re-layouts: 4.81 us -> 40 us
  blocking collectives: 30.7 us -> 0 us
  matrix products: 25.5 us -> 0 us
  Pallas kernels: 0 us -> 21.8 us
  starting transfers between devices: 3.66 us -> 14.5 us
  other arithmetic: 2.51 us -> 0 us
  waiting for transfers between devices: 19.2 us -> 20.5 us
    unnamed x10 -> x30, local copies, waits for them, and re-layouts: 0.91 us -> 40 us
    all_to_all x1 -> x0, blocking collectives: 30.7 us -> none  [per_device(): lax.all_to_all(spread.reshape(n_ep * n_dp, capacity, width), ('ep', 'dp')...]
    dot_general x5 -> x0, matrix products: 25.5 us -> none  [the longest x1 14.7 us: expert_rows(): return jnp.dot(hidden, w_down[0], preferred_element_type=jnp.float32)]
    pallas_call x0 -> x7, Pallas kernels: none -> 21.8 us  [call(): pl.pallas_call(kernel, name=name, out_shape=out_shape, in_specs=in_specs,...]
    ppermute x0 -> x12, waiting for transfers between devices: none -> 20.5 us  [the longest x6 13.9 us: to_chip(): return lax.ppermute(x, 'ep', [(i, i ^ CORES * d) for i in range(n_ep)])]
    all_to_all x1 -> x0, waiting for transfers between devices: 19.2 us -> none  [per_device(): lax.all_to_all(partial_out.reshape(arrived.shape), ('ep', 'dp'), split_ax...]
    ppermute x0 -> x12, starting transfers between devices: none -> 14.5 us  [the longest x6 10.1 us: to_chip(): return lax.ppermute(x, 'ep', [(i, i ^ CORES * d) for i in range(n_ep)])]
    all_to_all x1 -> x0, starting transfers between devices: 3.66 us -> none  [per_device(): lax.all_to_all(partial_out.reshape(arrived.shape), ('ep', 'dp'), split_ax...]
  transfers between devices with their start and end apart: 1 -> 12, of which waited for: 1 -> 5; matrix products, arithmetic and copies ran while one was open for 3% -> 0% of each run, Pallas kernels for 0% -> 11%
where the time goes in v1:
time: 97.8 us; the launch traced here: 97.5 us
  local copies, waits for them, and re-layouts  40 us (41%)
  Pallas kernels  21.8 us (22%)
  waiting for transfers between devices  20.5 us (21%)
  starting transfers between devices  14.5 us (15%)
    unnamed x30, local copies, waits for them, and re-layouts  40 us
    pallas_call x7, Pallas kernels, call(): pl.pallas_call(kernel, name=name, out_shape=out_shape, in_specs=in_specs,...  21.8 us
    ppermute x6, waiting for transfers between devices, to_chip(): return lax.ppermute(x, 'ep', [(i, i ^ CORES * d) for i in range(n_ep)])  13.9 us
    ppermute x6, starting transfers between devices, to_chip(): return lax.ppermute(x, 'ep', [(i, i ^ CORES * d) for i in range(n_ep)])  10.1 us
    ppermute x2, waiting for transfers between devices, along_dp(): return lax.ppermute(x, 'dp', [(0, 1), (1, 0)])  5.14 us
    ppermute x2, starting transfers between devices, along_dp(): return lax.ppermute(x, 'dp', [(0, 1), (1, 0)])  2.1 us
  transfers between devices with their start and end apart: 12, of which 5 were waited for; matrix products, arithmetic and copies ran while one was open for 0% of the time, Pallas kernels for 11%

profile of v1, /device:TPU:0, one launch (start us, length us, event | category | flops | bytes accessed | tf_op | source)
XLA Modules:
  0.0 97.5 jit_solution(7585050841870006284)
XLA Ops:
  0.6 0.0 copy-start.10
  0.6 0.9 copy-done.10
  1.5 0.7 copy-done.11
  2.2 0.5 pack.1
  2.7 3.1 %collective-permute-start = (bf16[48,896]{1,0:T(8,128)(2,1)S(1)}, bf16[48,896]{1,0:T(8,128)(2,1)S(1)}, u32[]{:S(2)}, u32[]{:S(2)}) collective-permute-start(bf16[48,896]{1,0:T(8,128)(2,1)S(1)} %get-tuple-element.21), channel_id=1, source_target_pairs={{0,4},{2,6},{4,0},{6,2},{8,12},{10,14},{12,8},{14,10},{1,5},{3,7},... | collective-permute-start | bytes 258056 | tf_op jit(solution)/shard_map/ppermute | solution.py:318
  5.8 2.6 %collective-permute-start.1 = (bf16[48,896]{1,0:T(8,128)(2,1)S(1)}, bf16[48,896]{1,0:T(8,128)(2,1)S(1)}, u32[]{:S(2)}, u32[]{:S(2)}) collective-permute-start(bf16[48,896]{1,0:T(8,128)(2,1)S(1)} %get-tuple-element.22), channel_id=1, source_target_pairs={{0,8},{2,10},{4,12},{6,14},{8,0},{10,2},{12,4},{14,6},{1,9},{3,11}... | collective-permute-start | bytes 258056 | tf_op jit(solution)/shard_map/ppermute | solution.py:318
  8.4 0.0 collective-permute-start.2
  8.4 0.0 collective-permute-done.refs_1_
  8.4 6.9 %collective-permute-done.1.refs_2_ = bf16[48,896]{1,0:T(8,128)(2,1)S(1)} collective-permute-done((bf16[48,896]{1,0:T(8,128)(2,1)S(1)}, bf16[48,896]{1,0:T(8,128)(2,1)S(1)}, u32[]{:S(2)}, u32[]{:S(2)}) %collective-permute-start.1) | collective-permute-done | bytes 86048 | tf_op jit(solution)/shard_map/ppermute | solution.py:318
  15.3 0.0 collective-permute-done.2.refs_3_
  15.3 0.4 near.1
  15.7 0.1 collective-permute-start.5
  15.8 1.6 %collective-permute-start.4 = (bf16[48,1792]{1,0:T(8,128)(2,1)S(1)}, bf16[48,1792]{1,0:T(8,128)(2,1)S(1)}, u32[]{:S(2)}, u32[]{:S(2)}) collective-permute-start(bf16[48,1792]{1,0:T(8,128)(2,1)S(1)} %get-tuple-element.25), channel_id=1, source_target_pairs={{0,2},{2,0},{4,6},{6,4},{8,10},{10,8},{12,14},{14,12},{1,3},{3,1},... | collective-permute-start | bytes 516104 | tf_op jit(solution)/shard_map/ppermute | solution.py:321
  17.4 0.5 collective-permute-start.3
  17.9 5.2 %copy-done = bf16[1,7168,1024]{2,1,0:T(8,128)(2,1)S(1)} copy-done((bf16[1,7168,1024]{2,1,0:T(8,128)(2,1)S(1)}, bf16[1,7168,1024]{2,1,0:T(8,128)(2,1)}, u32[]{:S(2)}) %copy-start) | copy-done | bytes 14680088
  23.1 6.8 %fetch.1 = (bf16[7168,1024]{1,0:T(8,128)(2,1)S(1)}, bf16[7168,1024]{1,0:T(8,128)(2,1)S(1)}) custom-call(bf16[48,896]{1,0:T(8,128)(2,1)S(1)} %get-tuple-element.20.refs_0_.after, bf16[7168,1024]{1,0:T(8,128)(2,1)S(1)} %bitcast.7, bf16[7168,1024]{1,0:T(8,128)(2,1)} %bitcast.14), custom_call_target="tpu_custom_call" | custom-call | bytes 29360128 | tf_op jit(solution)/shard_map/fetch/pallas_call | solution.py:291
  29.9 0.0 copy-start.2
  29.9 7.4 %copy-done.2 = bf16[7168,1024]{1,0:T(8,128)(2,1)} copy-done((bf16[7168,1024]{1,0:T(8,128)(2,1)}, bf16[7168,1024]{1,0:T(8,128)(2,1)S(1)}, u32[]{:S(2)}) %copy-start.2) | copy-done | bytes 14680088
  37.2 5.1 %copy-done.4 = bf16[7168,1024]{1,0:T(8,128)(2,1)} copy-done((bf16[7168,1024]{1,0:T(8,128)(2,1)}, bf16[7168,1024]{1,0:T(8,128)(2,1)S(1)}, u32[]{:S(2)}) %copy-start.4) | copy-done | bytes 14680088
  42.4 0.0 copy-done.1
  42.4 0.0 copy-done.8
  42.4 0.0 copy-done.9
  42.4 3.5 %attend.1 = (bf16[1024,7168]{1,0:T(8,128)(2,1)S(1)}, bf16[2,128,512]{2,1,0:T(8,128)(2,1)}) custom-call(bf16[48,1792]{1,0:T(8,128)(2,1)S(1)} %get-tuple-element.24.after.refs_0_, s32[2]{0:T(128)S(1)} %copy-done.14, bf16[1024,7168]{1,0:T(8,128)(2,1)S(1)} %bitcast.8, bf16[2,576,128]{2,1,0:T(8,128)(2,1)S(1)} %bitcast.10, bf16[2,576,512]{2,1,0:T(8,128)(2,1)S(1)} %bitcast.9), custom_call_target="tpu_custom_call" | custom-call | bytes 14680064 | tf_op jit(solution)/shard_map/attend/pallas_call | solution.py:291
  45.9 0.0 copy-start.6
  46.0 5.2 %copy-done.6 = bf16[1024,7168]{1,0:T(8,128)(2,1)} copy-done((bf16[1024,7168]{1,0:T(8,128)(2,1)}, bf16[1024,7168]{1,0:T(8,128)(2,1)S(1)}, u32[]{:S(2)}) %copy-start.6) | copy-done | bytes 14680088
  51.1 0.0 collective-permute-done.5.refs_3_
  51.1 0.0 collective-permute-done.4.refs_2_
  51.1 0.0 collective-permute-done.3.refs_1_
  51.1 0.0 copy-start.3
  51.1 5.2 %copy-done.3 = bf16[7168,1024]{1,0:T(8,128)(2,1)S(1)} copy-done((bf16[7168,1024]{1,0:T(8,128)(2,1)S(1)}, bf16[7168,1024]{1,0:T(8,128)(2,1)}, u32[]{:S(2)}) %copy-start.3) | copy-done | bytes 14680088
  56.3 5.2 %copy-done.5 = bf16[7168,1024]{1,0:T(8,128)(2,1)S(1)} copy-done((bf16[7168,1024]{1,0:T(8,128)(2,1)S(1)}, bf16[7168,1024]{1,0:T(8,128)(2,1)}, u32[]{:S(2)}) %copy-start.5) | copy-done | bytes 14680088
  61.5 5.2 %copy-done.7 = bf16[1024,7168]{1,0:T(8,128)(2,1)S(1)} copy-done((bf16[1024,7168]{1,0:T(8,128)(2,1)S(1)}, bf16[1024,7168]{1,0:T(8,128)(2,1)}, u32[]{:S(2)}) %copy-start.7) | copy-done | bytes 14680088
  66.7 8.6 %experts.1 = (bf16[48,1792]{1,0:T(8,128)(2,1)S(1)}, bf16[48,1792]{1,0:T(8,128)(2,1)S(1)}, bf16[48,1792]{1,0:T(8,128)(2,1)S(1)}, bf16[48,1792]{1,0:T(8,128)(2,1)S(1)}) custom-call(bf16[48,1792]{1,0:T(8,128)(2,1)S(1)} %get-tuple-element.24.after.refs_0_, bf16[48,1792]{1,0:T(8,128)(2,1)S(1)} %collective-permute-done.3.refs_1_, ...), custom_call_target="tpu_custom_call" | custom-call | flops 2113929216 | tf_op jit(solution)/shard_map/experts/pallas_call | solution.py:291
  75.3 1.6 %collective-permute-start.6 = (bf16[48,1792]{1,0:T(8,128)(2,1)S(1)}, bf16[48,1792]{1,0:T(8,128)(2,1)S(1)}, u32[]{:S(2)}, u32[]{:S(2)}) collective-permute-start(bf16[48,1792]{1,0:T(8,128)(2,1)S(1)} %get-tuple-element.30), channel_id=1, source_target_pairs={{0,1},{1,0},{2,3},{3,2},{4,5},{5,4},{6,7},{7,6},{8,9},{9,8},{10,11... | collective-permute-start | bytes 516104 | tf_op jit(solution)/shard_map/ppermute | solution.py:324
  76.9 0.0 collective-permute-start.7
  76.9 0.6 collective-permute-start.8
  77.5 5.1 %collective-permute-done.6.along = bf16[48,1792]{1,0:T(8,128)(2,1)S(1)} collective-permute-done((bf16[48,1792]{1,0:T(8,128)(2,1)S(1)}, bf16[48,1792]{1,0:T(8,128)(2,1)S(1)}, u32[]{:S(2)}, u32[]{:S(2)}) %collective-permute-start.6) | collective-permute-done | bytes 172064 | tf_op jit(solution)/shard_map/ppermute | solution.py:324
  82.6 0.0 collective-permute-done.7.core_ref
  82.6 1.4 %collective-permute-done.8.across = bf16[48,1792]{1,0:T(8,128)(2,1)S(1)} collective-permute-done((bf16[48,1792]{1,0:T(8,128)(2,1)S(1)}, bf16[48,1792]{1,0:T(8,128)(2,1)S(1)}, u32[]{:S(2)}, u32[]{:S(2)}) %collective-permute-start.8) | collective-permute-done | bytes 172064 | tf_op jit(solution)/shard_map/ppermute | solution.py:327
  84.0 0.5 sums.1
  84.6 1.6 %collective-permute-start.9 = (bf16[48,896]{1,0:T(8,128)(2,1)S(1)}, bf16[48,896]{1,0:T(8,128)(2,1)S(1)}, u32[]{:S(2)}, u32[]{:S(2)}) collective-permute-start(bf16[48,896]{1,0:T(8,128)(2,1)S(1)} %get-tuple-element.34), channel_id=1, source_target_pairs={{0,4},{2,6},{4,0},{6,2},{8,12},{10,14},{12,8},{14,10},{1,5},{3,7},... | collective-permute-start | bytes 258056 | tf_op jit(solution)/shard_map/ppermute | solution.py:318
  86.1 1.6 %collective-permute-start.10 = (bf16[48,896]{1,0:T(8,128)(2,1)S(1)}, bf16[48,896]{1,0:T(8,128)(2,1)S(1)}, u32[]{:S(2)}, u32[]{:S(2)}) collective-permute-start(bf16[48,896]{1,0:T(8,128)(2,1)S(1)} %get-tuple-element.35), channel_id=1, source_target_pairs={{0,8},{2,10},{4,12},{6,14},{8,0},{10,2},{12,4},{14,6},{1,9},{3,11}... | collective-permute-start | bytes 258056 | tf_op jit(solution)/shard_map/ppermute | solution.py:318
  87.7 1.3 %collective-permute-start.11 = (bf16[48,896]{1,0:T(8,128)(2,1)S(1)}, bf16[48,896]{1,0:T(8,128)(2,1)S(1)}, u32[]{:S(2)}, u32[]{:S(2)}) collective-permute-start(bf16[48,896]{1,0:T(8,128)(2,1)S(1)} %get-tuple-element.36), channel_id=1, source_target_pairs={{0,12},{2,14},{4,8},{6,10},{8,4},{10,6},{12,0},{14,2},{1,13},{3,15... | collective-permute-start | bytes 258056 | tf_op jit(solution)/shard_map/ppermute | solution.py:318
  89.0 0.9 collective-permute-done.9.refs_1_
  89.9 6.1 %collective-permute-done.10.refs_2_ = bf16[48,896]{1,0:T(8,128)(2,1)S(1)} collective-permute-done((bf16[48,896]{1,0:T(8,128)(2,1)S(1)}, bf16[48,896]{1,0:T(8,128)(2,1)S(1)}, u32[]{:S(2)}, u32[]{:S(2)}) %collective-permute-start.10) | collective-permute-done | bytes 86048 | tf_op jit(solution)/shard_map/ppermute | solution.py:318
  96.0 0.0 collective-permute-done.11.refs_3_
  96.0 0.0 copy-done.13
  96.0 1.5 %combine.1 = bf16[8,7168]{1,0:T(8,128)(2,1)} custom-call(s32[2,8]{1,0:T(2,128)S(1)} %bitcast.12, f32[2,8]{1,0:T(2,128)S(1)} %bitcast.13, bf16[48,896]{1,0:T(8,128)(2,1)S(1)} %get-tuple-element.33.refs_0_, bf16[48,896]{1,0:T(8,128)(2,1)S(1)} %collective-permute-done.9.refs_1_, bf16[48,896]{1,0:T(8,128)(2,1)S(1)} %collective-permute-done.10.refs_2_, ...), custom_call_target="tpu_custom_call" | custom-call | tf_op jit(solution)/shard_map/combine/pallas_call | solution.py:291
  (13 shorter events, 0.0 us)
Async XLA Ops:
  0.6 0.9 copy-start.10
  1.5 0.7 copy-start.11
  2.7 5.7 %collective-permute-start = (bf16[48,896]{1,0:T(8,128)(2,1)S(1)}, bf16[48,896]{1,0:T(8,128)(2,1)S(1)}, u32[]{:S(2)}, u32[]{:S(2)}) collective-permute-start(bf16[48,896]{1,0:T(8,128)(2,1)S(1)} %get-tuple-element.21), channel_id=1, source_target_pairs={{0,4},{2,6},{4,0},{6,2},{8,12},{10,14},{12,8},{14,10},{1,5},{3,7},... | collective-permute-start | bytes 258056 | tf_op jit(solution)/shard_map/ppermute | solution.py:318
  5.8 9.5 %collective-permute-start.1 = (bf16[48,896]{1,0:T(8,128)(2,1)S(1)}, bf16[48,896]{1,0:T(8,128)(2,1)S(1)}, u32[]{:S(2)}, u32[]{:S(2)}) collective-permute-start(bf16[48,896]{1,0:T(8,128)(2,1)S(1)} %get-tuple-element.22), channel_id=1, source_target_pairs={{0,8},{2,10},{4,12},{6,14},{8,0},{10,2},{12,4},{14,6},{1,9},{3,11}... | collective-permute-start | bytes 258056 | tf_op jit(solution)/shard_map/ppermute | solution.py:318
  8.4 6.9 %collective-permute-start.2 = (bf16[48,896]{1,0:T(8,128)(2,1)S(1)}, bf16[48,896]{1,0:T(8,128)(2,1)S(1)}, u32[]{:S(2)}, u32[]{:S(2)}) collective-permute-start(bf16[48,896]{1,0:T(8,128)(2,1)S(1)} %get-tuple-element.23), channel_id=1, source_target_pairs={{0,12},{2,14},{4,8},{6,10},{8,4},{10,6},{12,0},{14,2},{1,13},{3,15... | collective-permute-start | bytes 258056 | tf_op jit(solution)/shard_map/ppermute | solution.py:318
  15.7 35.4 %collective-permute-start.5 = (bf16[48,1792]{1,0:T(8,128)(2,1)S(1)}, bf16[48,1792]{1,0:T(8,128)(2,1)S(1)}, u32[]{:S(2)}, u32[]{:S(2)}) collective-permute-start(bf16[48,1792]{1,0:T(8,128)(2,1)S(1)} %get-tuple-element.25), channel_id=1, source_target_pairs={{0,3},{1,2},{2,1},{3,0},{4,7},{5,6},{6,5},{7,4},{8,11},{9,10},{10,... | collective-permute-start | bytes 516104 | tf_op jit(solution)/shard_map/ppermute | solution.py:327
  15.8 35.3 %collective-permute-start.4 = (bf16[48,1792]{1,0:T(8,128)(2,1)S(1)}, bf16[48,1792]{1,0:T(8,128)(2,1)S(1)}, u32[]{:S(2)}, u32[]{:S(2)}) collective-permute-start(bf16[48,1792]{1,0:T(8,128)(2,1)S(1)} %get-tuple-element.25), channel_id=1, source_target_pairs={{0,2},{2,0},{4,6},{6,4},{8,10},{10,8},{12,14},{14,12},{1,3},{3,1},... | collective-permute-start | bytes 516104 | tf_op jit(solution)/shard_map/ppermute | solution.py:321
  17.4 33.8 %collective-permute-start.3 = (bf16[48,1792]{1,0:T(8,128)(2,1)S(1)}, bf16[48,1792]{1,0:T(8,128)(2,1)S(1)}, u32[]{:S(2)}, u32[]{:S(2)}) collective-permute-start(bf16[48,1792]{1,0:T(8,128)(2,1)S(1)} %get-tuple-element.24.after.refs_0_), channel_id=1, source_target_pairs={{0,1},{1,0},{2,3},{3,2},{4,5},{5,4},{6,7},{7,6},{8,9},{9,8},{10,11... | collective-permute-start | bytes 516104 | tf_op jit(solution)/shard_map/ppermute | solution.py:324
  17.9 5.2 %copy-start = (bf16[1,7168,1024]{2,1,0:T(8,128)(2,1)S(1)}, bf16[1,7168,1024]{2,1,0:T(8,128)(2,1)}, u32[]{:S(2)}) copy-start(bf16[1,7168,1024]{2,1,0:T(8,128)(2,1)} %param.12) | copy-start | bytes 44040196
  23.1 19.3 %copy-start.1 = (bf16[1,1024,7168]{2,1,0:T(8,128)(2,1)S(1)}, bf16[1,1024,7168]{2,1,0:T(8,128)(2,1)}, u32[]{:S(2)}) copy-start(bf16[1,1024,7168]{2,1,0:T(8,128)(2,1)} %param.14) | copy-start | bytes 44040196
  23.1 19.3 %copy-start.8 = (bf16[2,512,576]{1,2,0:T(8,128)(2,1)S(1)}, bf16[2,512,576]{1,2,0:T(8,128)(2,1)}, u32[]{:S(2)}) copy-start(bf16[2,512,576]{1,2,0:T(8,128)(2,1)} %param.16) | copy-start | bytes 3538948
  23.1 19.3 %copy-start.9 = (bf16[2,128,576]{1,2,0:T(8,128)(2,1)S(1)}, bf16[2,128,576]{1,2,0:T(8,128)(2,1)}, u32[]{:S(2)}) copy-start(bf16[2,128,576]{1,2,0:T(8,128)(2,1)} %param.15) | copy-start | bytes 884740
  23.1 19.3 %copy-start.14 = (s32[2]{0:T(128)S(1)}, s32[2]{0:T(128)}, u32[]{:S(2)}) copy-start(s32[2]{0:T(128)} %lengths.1) | copy-start | bytes 28
  29.9 7.4 %copy-start.2 = (bf16[7168,1024]{1,0:T(8,128)(2,1)}, bf16[7168,1024]{1,0:T(8,128)(2,1)S(1)}, u32[]{:S(2)}) copy-start(bf16[7168,1024]{1,0:T(8,128)(2,1)S(1)} %get-tuple-element.26.refs_4_) | copy-start | bytes 44040196
  37.2 5.1 %copy-start.4 = (bf16[7168,1024]{1,0:T(8,128)(2,1)}, bf16[7168,1024]{1,0:T(8,128)(2,1)S(1)}, u32[]{:S(2)}) copy-start(bf16[7168,1024]{1,0:T(8,128)(2,1)S(1)} %get-tuple-element.27.refs_5_) | copy-start | bytes 44040196
  45.9 5.2 %copy-start.6 = (bf16[1024,7168]{1,0:T(8,128)(2,1)}, bf16[1024,7168]{1,0:T(8,128)(2,1)S(1)}, u32[]{:S(2)}) copy-start(bf16[1024,7168]{1,0:T(8,128)(2,1)S(1)} %get-tuple-element.28.refs_6_) | copy-start | bytes 44040196
  51.1 5.2 %copy-start.3 = (bf16[7168,1024]{1,0:T(8,128)(2,1)S(1)}, bf16[7168,1024]{1,0:T(8,128)(2,1)}, u32[]{:S(2)}) copy-start(bf16[7168,1024]{1,0:T(8,128)(2,1)} %copy-done.2) | copy-start | bytes 44040196
  56.3 5.2 %copy-start.5 = (bf16[7168,1024]{1,0:T(8,128)(2,1)S(1)}, bf16[7168,1024]{1,0:T(8,128)(2,1)}, u32[]{:S(2)}) copy-start(bf16[7168,1024]{1,0:T(8,128)(2,1)} %copy-done.4) | copy-start | bytes 44040196
  61.5 5.2 %copy-start.7 = (bf16[1024,7168]{1,0:T(8,128)(2,1)S(1)}, bf16[1024,7168]{1,0:T(8,128)(2,1)}, u32[]{:S(2)}) copy-start(bf16[1024,7168]{1,0:T(8,128)(2,1)} %copy-done.6) | copy-start | bytes 44040196
  66.7 29.4 %copy-start.12 = (s32[8,2]{0,1:T(2,128)S(1)}, s32[8,2]{0,1:T(2,128)}, u32[]{:S(2)}) copy-start(s32[8,2]{0,1:T(2,128)} %param.10) | copy-start | bytes 196
  66.7 29.4 %copy-start.13 = (f32[8,2]{0,1:T(2,128)S(1)}, f32[8,2]{0,1:T(2,128)}, u32[]{:S(2)}) copy-start(f32[8,2]{0,1:T(2,128)} %param.11) | copy-start | bytes 196
  75.3 7.3 %collective-permute-start.6 = (bf16[48,1792]{1,0:T(8,128)(2,1)S(1)}, bf16[48,1792]{1,0:T(8,128)(2,1)S(1)}, u32[]{:S(2)}, u32[]{:S(2)}) collective-permute-start(bf16[48,1792]{1,0:T(8,128)(2,1)S(1)} %get-tuple-element.30), channel_id=1, source_target_pairs={{0,1},{1,0},{2,3},{3,2},{4,5},{5,4},{6,7},{7,6},{8,9},{9,8},{10,11... | collective-permute-start | bytes 516104 | tf_op jit(solution)/shard_map/ppermute | solution.py:324
  76.9 5.8 %collective-permute-start.7 = (bf16[48,1792]{1,0:T(8,128)(2,1)S(1)}, bf16[48,1792]{1,0:T(8,128)(2,1)S(1)}, u32[]{:S(2)}, u32[]{:S(2)}) collective-permute-start(bf16[48,1792]{1,0:T(8,128)(2,1)S(1)} %get-tuple-element.31), channel_id=1, source_target_pairs={{0,2},{2,0},{4,6},{6,4},{8,10},{10,8},{12,14},{14,12},{1,3},{3,1},... | collective-permute-start | bytes 516104 | tf_op jit(solution)/shard_map/ppermute | solution.py:321
  76.9 7.2 %collective-permute-start.8 = (bf16[48,1792]{1,0:T(8,128)(2,1)S(1)}, bf16[48,1792]{1,0:T(8,128)(2,1)S(1)}, u32[]{:S(2)}, u32[]{:S(2)}) collective-permute-start(bf16[48,1792]{1,0:T(8,128)(2,1)S(1)} %get-tuple-element.32), channel_id=1, source_target_pairs={{0,3},{1,2},{2,1},{3,0},{4,7},{5,6},{6,5},{7,4},{8,11},{9,10},{10,... | collective-permute-start | bytes 516104 | tf_op jit(solution)/shard_map/ppermute | solution.py:327
  84.6 5.3 %collective-permute-start.9 = (bf16[48,896]{1,0:T(8,128)(2,1)S(1)}, bf16[48,896]{1,0:T(8,128)(2,1)S(1)}, u32[]{:S(2)}, u32[]{:S(2)}) collective-permute-start(bf16[48,896]{1,0:T(8,128)(2,1)S(1)} %get-tuple-element.34), channel_id=1, source_target_pairs={{0,4},{2,6},{4,0},{6,2},{8,12},{10,14},{12,8},{14,10},{1,5},{3,7},... | collective-permute-start | bytes 258056 | tf_op jit(solution)/shard_map/ppermute | solution.py:318
  86.1 9.9 %collective-permute-start.10 = (bf16[48,896]{1,0:T(8,128)(2,1)S(1)}, bf16[48,896]{1,0:T(8,128)(2,1)S(1)}, u32[]{:S(2)}, u32[]{:S(2)}) collective-permute-start(bf16[48,896]{1,0:T(8,128)(2,1)S(1)} %get-tuple-element.35), channel_id=1, source_target_pairs={{0,8},{2,10},{4,12},{6,14},{8,0},{10,2},{12,4},{14,6},{1,9},{3,11}... | collective-permute-start | bytes 258056 | tf_op jit(solution)/shard_map/ppermute | solution.py:318
  87.7 8.3 %collective-permute-start.11 = (bf16[48,896]{1,0:T(8,128)(2,1)S(1)}, bf16[48,896]{1,0:T(8,128)(2,1)S(1)}, u32[]{:S(2)}, u32[]{:S(2)}) collective-permute-start(bf16[48,896]{1,0:T(8,128)(2,1)S(1)} %get-tuple-element.36), channel_id=1, source_target_pairs={{0,12},{2,14},{4,8},{6,10},{8,4},{10,6},{12,0},{14,2},{1,13},{3,15... | collective-permute-start | bytes 258056 | tf_op jit(solution)/shard_map/ppermute | solution.py:318

commit v2 on v1

--- a/solution.py
+++ b/solution.py
@@ -310,7 +310,9 @@
     far_rows, near_rows = far_pieces * CORES * capacity, near_pieces * chips * capacity
     far = jax.ShapeDtypeStruct((far_rows, width // far_pieces), bf16)
     near = jax.ShapeDtypeStruct((near_rows, width // near_pieces), bf16)
-    w_gate, w_up, w_down = w_gate[0], w_up[0], w_down[0]
+    w_gate, w_up, w_down = (
+        pltpu.with_memory_space_constraint(w[0], pltpu.HBM) for w in (w_gate, w_up, w_down)
+    )
     units = w_gate.shape[1]
     ids, gains = expert_ids.T, gate_weights.T
 
@@ -342,7 +344,7 @@
     same, other = call(
         functools.partial(near_kernel, far_pieces, near_pieces, capacity, chips),
         "near", (near,) * 2, [VMEM] * chips, (VMEM,) * 2,
-        [pltpu.VMEM((chips * far_rows, width // far_pieces), bf16)], 4 * MIB, landed,
+        [pltpu.VMEM((chips * far_rows, width // far_pieces), bf16)], 2 * MIB, landed,
     )
     arrived = [same, along_dp(same), to_core(other), across(other)]
     latent = cache.shape[2] - ROPE
@@ -353,7 +355,7 @@
             pltpu.VMEM(w_down.shape, bf16),
             jax.ShapeDtypeStruct(queries.shape[:2] + (latent,), bf16),
         ),
-        [HBM, SMEM, HBM, VMEM, VMEM], (VMEM, VMEM), [pltpu.SemaphoreType.DMA((cuts,))], 8 * MIB,
+        [HBM, SMEM, HBM, VMEM, VMEM], (VMEM, VMEM), [pltpu.SemaphoreType.DMA((cuts,))], 2 * MIB,
         (same, lengths, w_down, queries.swapaxes(1, 2), cache.swapaxes(1, 2)),
         moved=2 * w_down.size,
     )
@@ -362,7 +364,7 @@
         functools.partial(expert_kernel, near_pieces),
         "experts", (near,) * 4, [VMEM] * 7, (VMEM,) * 4,
         [pltpu.VMEM((4 * near_rows, width // near_pieces), bf16), pltpu.VMEM((rows, units), bf16)],
-        8 * MIB, (*arrived, got_gate, got_up, got_down), flops=6 * rows * width * units,
+        4 * MIB, (*arrived, got_gate, got_up, got_down), flops=6 * rows * width * units,
     )
     sums = call(
         functools.partial(sum_kernel, far_pieces, near_pieces, capacity, chips),

time: 97.8 us -> 65.5 us (0.67)
  local copies, waits for them, and re-layouts: 40 us -> 1.66 us
  Pallas kernels: 21.8 us -> 27.9 us
    unnamed x30 -> x14, local copies, waits for them, and re-layouts: 40 us -> 1.66 us
    pallas_call x7, Pallas kernels: 21.8 us -> 27.9 us  [call(): pl.pallas_call(kernel, name=name, out_shape=out_shape, in_specs=in_specs,...]
  transfers between devices with their start and end apart: 12 -> 12, of which waited for: 5 -> 5; matrix products, arithmetic and copies ran while one was open for 0% -> 0% of each run, Pallas kernels for 11% -> 25%
where the time goes in v2:
time: 65.5 us; the launch traced here: 65.3 us
  Pallas kernels  27.9 us (43%)
  waiting for transfers between devices  20.5 us (31%)
  starting transfers between devices  14.5 us (22%)
  local copies, waits for them, and re-layouts  1.66 us (3%)
  between operations  0.75 us (1%)
    pallas_call x7, Pallas kernels, call(): pl.pallas_call(kernel, name=name, out_shape=out_shape, in_specs=in_specs,...  27.9 us
    ppermute x6, waiting for transfers between devices, to_chip(): return lax.ppermute(x, 'ep', [(i, i ^ CORES * d) for i in range(n_ep)])  13.9 us
    ppermute x6, starting transfers between devices, to_chip(): return lax.ppermute(x, 'ep', [(i, i ^ CORES * d) for i in range(n_ep)])  10.1 us
    ppermute x2, waiting for transfers between devices, along_dp(): return lax.ppermute(x, 'dp', [(0, 1), (1, 0)])  5.14 us
    ppermute x2, starting transfers between devices, along_dp(): return lax.ppermute(x, 'dp', [(0, 1), (1, 0)])  2.09 us
    unnamed x14, local copies, waits for them, and re-layouts  1.66 us
    ppermute x2, starting transfers between devices, to_core(): return lax.ppermute(x, 'ep', [(i, i ^ 1) for i in range(n_ep)])  1.6 us
    ppermute x2, waiting for transfers between devices, across(): return lax.ppermute(x, ('ep', 'dp'), [(i, i ^ 3) for i in range(2 * n_ep)])  1.42 us
  transfers between devices with their start and end apart: 12, of which 5 were waited for; matrix products, arithmetic and copies ran while one was open for 0% of the time, Pallas kernels for 25%

profile of v2, /device:TPU:0, one launch (start us, length us, event | category | flops | bytes accessed | tf_op | source)
XLA Modules:
  0.0 65.3 jit_solution(13120661040007632959)
XLA Ops:
  0.6 0.0 copy-start.2
  0.6 0.9 %copy-done.2 = bf16[8,7168]{1,0:T(8,128)(2,1)S(1)} copy-done((bf16[8,7168]{1,0:T(8,128)(2,1)S(1)}, bf16[8,7168]{1,0:T(8,128)(2,1)}, u32[]{:S(2)}) %copy-start.2) | copy-done | bytes 114712
  1.5 0.0 copy-start.3
  1.5 0.7 %copy-done.3 = s32[8,2]{0,1:T(2,128)S(1)} copy-done((s32[8,2]{0,1:T(2,128)S(1)}, s32[8,2]{0,1:T(2,128)}, u32[]{:S(2)}) %copy-start.3) | copy-done | bytes 88
  2.2 0.5 pack.1
  2.7 3.1 %collective-permute-start = (bf16[48,896]{1,0:T(8,128)(2,1)S(1)}, bf16[48,896]{1,0:T(8,128)(2,1)S(1)}, u32[]{:S(2)}, u32[]{:S(2)}) collective-permute-start(bf16[48,896]{1,0:T(8,128)(2,1)S(1)} %get-tuple-element.21), channel_id=1, source_target_pairs={{0,4},{2,6},{4,0},{6,2},{8,12},{10,14},{12,8},{14,10},{1,5},{3,7},... | collective-permute-start | bytes 258056 | tf_op jit(solution)/shard_map/ppermute | solution.py:320
  5.8 2.6 %collective-permute-start.1 = (bf16[48,896]{1,0:T(8,128)(2,1)S(1)}, bf16[48,896]{1,0:T(8,128)(2,1)S(1)}, u32[]{:S(2)}, u32[]{:S(2)}) collective-permute-start(bf16[48,896]{1,0:T(8,128)(2,1)S(1)} %get-tuple-element.22), channel_id=1, source_target_pairs={{0,8},{2,10},{4,12},{6,14},{8,0},{10,2},{12,4},{14,6},{1,9},{3,11}... | collective-permute-start | bytes 258056 | tf_op jit(solution)/shard_map/ppermute | solution.py:320
  8.4 0.0 collective-permute-start.2
  8.4 0.0 collective-permute-done.refs_1_
  8.4 6.9 %collective-permute-done.1.refs_2_ = bf16[48,896]{1,0:T(8,128)(2,1)S(1)} collective-permute-done((bf16[48,896]{1,0:T(8,128)(2,1)S(1)}, bf16[48,896]{1,0:T(8,128)(2,1)S(1)}, u32[]{:S(2)}, u32[]{:S(2)}) %collective-permute-start.1) | collective-permute-done | bytes 86048 | tf_op jit(solution)/shard_map/ppermute | solution.py:320
  15.3 0.0 collective-permute-done.2.refs_3_
  15.3 0.4 near.1
  15.7 0.1 collective-permute-start.5
  15.8 1.6 %collective-permute-start.4 = (bf16[48,1792]{1,0:T(8,128)(2,1)S(1)}, bf16[48,1792]{1,0:T(8,128)(2,1)S(1)}, u32[]{:S(2)}, u32[]{:S(2)}) collective-permute-start(bf16[48,1792]{1,0:T(8,128)(2,1)S(1)} %get-tuple-element.25), channel_id=1, source_target_pairs={{0,2},{2,0},{4,6},{6,4},{8,10},{10,8},{12,14},{14,12},{1,3},{3,1},... | collective-permute-start | bytes 516104 | tf_op jit(solution)/shard_map/ppermute | solution.py:323
  17.4 0.5 collective-permute-start.3
  17.9 0.0 copy-start
  17.9 0.0 copy-start.1
  17.9 0.0 copy-start.6
  17.9 9.7 %fetch.1 = (bf16[7168,1024]{1,0:T(8,128)(2,1)S(1)}, bf16[7168,1024]{1,0:T(8,128)(2,1)S(1)}) custom-call(bf16[48,896]{1,0:T(8,128)(2,1)S(1)} %get-tuple-element.20.refs_0_.after, bf16[7168,1024]{1,0:T(8,128)(2,1)} %bitcast.12, bf16[7168,1024]{1,0:T(8,128)(2,1)} %bitcast.13), custom_call_target="tpu_custom_call" | custom-call | bytes 29360128 | tf_op jit(solution)/shard_map/fetch/pallas_call | solution.py:291
  27.6 0.0 copy-done
  27.6 0.0 copy-done.1
  27.7 0.0 copy-done.6
  27.7 6.8 %attend.1 = (bf16[1024,7168]{1,0:T(8,128)(2,1)S(1)}, bf16[2,128,512]{2,1,0:T(8,128)(2,1)}) custom-call(bf16[48,1792]{1,0:T(8,128)(2,1)S(1)} %get-tuple-element.24.after.refs_0_, s32[2]{0:T(128)S(1)} %copy-done.6, bf16[1024,7168]{1,0:T(8,128)(2,1)} %bitcast.14, bf16[2,576,128]{2,1,0:T(8,128)(2,1)S(1)} %bitcast.8, bf16[2,576,512]{2,1,0:T(8,128)(2,1)S(1)} %bitcast.7), custom_call_target="tpu_custom_call" | custom-call | bytes 14680064 | tf_op jit(solution)/shard_map/attend/pallas_call | solution.py:291
  34.5 0.0 collective-permute-done.5.refs_3_
  34.5 0.0 collective-permute-done.4.refs_2_
  34.5 0.0 collective-permute-done.3.refs_1_
  34.5 0.0 copy-start.4
  34.5 0.0 copy-start.5
  34.5 8.6 %experts.1 = (bf16[48,1792]{1,0:T(8,128)(2,1)S(1)}, bf16[48,1792]{1,0:T(8,128)(2,1)S(1)}, bf16[48,1792]{1,0:T(8,128)(2,1)S(1)}, bf16[48,1792]{1,0:T(8,128)(2,1)S(1)}) custom-call(bf16[48,1792]{1,0:T(8,128)(2,1)S(1)} %get-tuple-element.24.after.refs_0_, bf16[48,1792]{1,0:T(8,128)(2,1)S(1)} %collective-permute-done.3.refs_1_, ...), custom_call_target="tpu_custom_call" | custom-call | flops 2113929216 | tf_op jit(solution)/shard_map/experts/pallas_call | solution.py:291
  43.1 1.6 %collective-permute-start.6 = (bf16[48,1792]{1,0:T(8,128)(2,1)S(1)}, bf16[48,1792]{1,0:T(8,128)(2,1)S(1)}, u32[]{:S(2)}, u32[]{:S(2)}) collective-permute-start(bf16[48,1792]{1,0:T(8,128)(2,1)S(1)} %get-tuple-element.30), channel_id=1, source_target_pairs={{0,1},{1,0},{2,3},{3,2},{4,5},{5,4},{6,7},{7,6},{8,9},{9,8},{10,11... | collective-permute-start | bytes 516104 | tf_op jit(solution)/shard_map/ppermute | solution.py:326
  44.7 0.0 collective-permute-start.7
  44.7 0.6 collective-permute-start.8
  45.3 5.1 %collective-permute-done.6.along = bf16[48,1792]{1,0:T(8,128)(2,1)S(1)} collective-permute-done((bf16[48,1792]{1,0:T(8,128)(2,1)S(1)}, bf16[48,1792]{1,0:T(8,128)(2,1)S(1)}, u32[]{:S(2)}, u32[]{:S(2)}) %collective-permute-start.6) | collective-permute-done | bytes 172064 | tf_op jit(solution)/shard_map/ppermute | solution.py:326
  50.5 0.0 collective-permute-done.7.core_ref
  50.5 1.4 %collective-permute-done.8.across = bf16[48,1792]{1,0:T(8,128)(2,1)S(1)} collective-permute-done((bf16[48,1792]{1,0:T(8,128)(2,1)S(1)}, bf16[48,1792]{1,0:T(8,128)(2,1)S(1)}, u32[]{:S(2)}, u32[]{:S(2)}) %collective-permute-start.8) | collective-permute-done | bytes 172064 | tf_op jit(solution)/shard_map/ppermute | solution.py:329
  51.9 0.5 sums.1
  52.4 1.5 %collective-permute-start.9 = (bf16[48,896]{1,0:T(8,128)(2,1)S(1)}, bf16[48,896]{1,0:T(8,128)(2,1)S(1)}, u32[]{:S(2)}, u32[]{:S(2)}) collective-permute-start(bf16[48,896]{1,0:T(8,128)(2,1)S(1)} %get-tuple-element.34), channel_id=1, source_target_pairs={{0,4},{2,6},{4,0},{6,2},{8,12},{10,14},{12,8},{14,10},{1,5},{3,7},... | collective-permute-start | bytes 258056 | tf_op jit(solution)/shard_map/ppermute | solution.py:320
  54.0 1.6 %collective-permute-start.10 = (bf16[48,896]{1,0:T(8,128)(2,1)S(1)}, bf16[48,896]{1,0:T(8,128)(2,1)S(1)}, u32[]{:S(2)}, u32[]{:S(2)}) collective-permute-start(bf16[48,896]{1,0:T(8,128)(2,1)S(1)} %get-tuple-element.35), channel_id=1, source_target_pairs={{0,8},{2,10},{4,12},{6,14},{8,0},{10,2},{12,4},{14,6},{1,9},{3,11}... | collective-permute-start | bytes 258056 | tf_op jit(solution)/shard_map/ppermute | solution.py:320
  55.5 1.3 %collective-permute-start.11 = (bf16[48,896]{1,0:T(8,128)(2,1)S(1)}, bf16[48,896]{1,0:T(8,128)(2,1)S(1)}, u32[]{:S(2)}, u32[]{:S(2)}) collective-permute-start(bf16[48,896]{1,0:T(8,128)(2,1)S(1)} %get-tuple-element.36), channel_id=1, source_target_pairs={{0,12},{2,14},{4,8},{6,10},{8,4},{10,6},{12,0},{14,2},{1,13},{3,15... | collective-permute-start | bytes 258056 | tf_op jit(solution)/shard_map/ppermute | solution.py:320
  56.9 0.9 %collective-permute-done.9.refs_1_ = bf16[48,896]{1,0:T(8,128)(2,1)S(1)} collective-permute-done((bf16[48,896]{1,0:T(8,128)(2,1)S(1)}, bf16[48,896]{1,0:T(8,128)(2,1)S(1)}, u32[]{:S(2)}, u32[]{:S(2)}) %collective-permute-start.9) | collective-permute-done | bytes 86048 | tf_op jit(solution)/shard_map/ppermute | solution.py:320
  57.7 6.1 %collective-permute-done.10.refs_2_ = bf16[48,896]{1,0:T(8,128)(2,1)S(1)} collective-permute-done((bf16[48,896]{1,0:T(8,128)(2,1)S(1)}, bf16[48,896]{1,0:T(8,128)(2,1)S(1)}, u32[]{:S(2)}, u32[]{:S(2)}) %collective-permute-start.10) | collective-permute-done | bytes 86048 | tf_op jit(solution)/shard_map/ppermute | solution.py:320
  63.9 0.0 collective-permute-done.11.refs_3_
  63.9 0.0 copy-done.4
  63.9 0.0 copy-done.5
  63.9 1.5 %combine.1 = bf16[8,7168]{1,0:T(8,128)(2,1)} custom-call(s32[2,8]{1,0:T(2,128)S(1)} %bitcast.10, f32[2,8]{1,0:T(2,128)S(1)} %bitcast.11, bf16[48,896]{1,0:T(8,128)(2,1)S(1)} %get-tuple-element.33.refs_0_, bf16[48,896]{1,0:T(8,128)(2,1)S(1)} %collective-permute-done.9.refs_1_, bf16[48,896]{1,0:T(8,128)(2,1)S(1)} %collective-permute-done.10.refs_2_, ...), custom_call_target="tpu_custom_call" | custom-call | tf_op jit(solution)/shard_map/combine/pallas_call | solution.py:291
Async XLA Ops:
  0.6 0.9 %copy-start.2 = (bf16[8,7168]{1,0:T(8,128)(2,1)S(1)}, bf16[8,7168]{1,0:T(8,128)(2,1)}, u32[]{:S(2)}) copy-start(bf16[8,7168]{1,0:T(8,128)(2,1)} %tok_ref.1) | copy-start | bytes 344068
  1.5 0.7 %copy-start.3 = (s32[8,2]{0,1:T(2,128)S(1)}, s32[8,2]{0,1:T(2,128)}, u32[]{:S(2)}) copy-start(s32[8,2]{0,1:T(2,128)} %param.10) | copy-start | bytes 196
  2.7 5.7 %collective-permute-start = (bf16[48,896]{1,0:T(8,128)(2,1)S(1)}, bf16[48,896]{1,0:T(8,128)(2,1)S(1)}, u32[]{:S(2)}, u32[]{:S(2)}) collective-permute-start(bf16[48,896]{1,0:T(8,128)(2,1)S(1)} %get-tuple-element.21), channel_id=1, source_target_pairs={{0,4},{2,6},{4,0},{6,2},{8,12},{10,14},{12,8},{14,10},{1,5},{3,7},... | collective-permute-start | bytes 258056 | tf_op jit(solution)/shard_map/ppermute | solution.py:320
  5.8 9.5 %collective-permute-start.1 = (bf16[48,896]{1,0:T(8,128)(2,1)S(1)}, bf16[48,896]{1,0:T(8,128)(2,1)S(1)}, u32[]{:S(2)}, u32[]{:S(2)}) collective-permute-start(bf16[48,896]{1,0:T(8,128)(2,1)S(1)} %get-tuple-element.22), channel_id=1, source_target_pairs={{0,8},{2,10},{4,12},{6,14},{8,0},{10,2},{12,4},{14,6},{1,9},{3,11}... | collective-permute-start | bytes 258056 | tf_op jit(solution)/shard_map/ppermute | solution.py:320
  8.4 6.9 %collective-permute-start.2 = (bf16[48,896]{1,0:T(8,128)(2,1)S(1)}, bf16[48,896]{1,0:T(8,128)(2,1)S(1)}, u32[]{:S(2)}, u32[]{:S(2)}) collective-permute-start(bf16[48,896]{1,0:T(8,128)(2,1)S(1)} %get-tuple-element.23), channel_id=1, source_target_pairs={{0,12},{2,14},{4,8},{6,10},{8,4},{10,6},{12,0},{14,2},{1,13},{3,15... | collective-permute-start | bytes 258056 | tf_op jit(solution)/shard_map/ppermute | solution.py:320
  15.7 18.7 %collective-permute-start.5 = (bf16[48,1792]{1,0:T(8,128)(2,1)S(1)}, bf16[48,1792]{1,0:T(8,128)(2,1)S(1)}, u32[]{:S(2)}, u32[]{:S(2)}) collective-permute-start(bf16[48,1792]{1,0:T(8,128)(2,1)S(1)} %get-tuple-element.25), channel_id=1, source_target_pairs={{0,3},{1,2},{2,1},{3,0},{4,7},{5,6},{6,5},{7,4},{8,11},{9,10},{10,... | collective-permute-start | bytes 516104 | tf_op jit(solution)/shard_map/ppermute | solution.py:329
  15.8 18.7 %collective-permute-start.4 = (bf16[48,1792]{1,0:T(8,128)(2,1)S(1)}, bf16[48,1792]{1,0:T(8,128)(2,1)S(1)}, u32[]{:S(2)}, u32[]{:S(2)}) collective-permute-start(bf16[48,1792]{1,0:T(8,128)(2,1)S(1)} %get-tuple-element.25), channel_id=1, source_target_pairs={{0,2},{2,0},{4,6},{6,4},{8,10},{10,8},{12,14},{14,12},{1,3},{3,1},... | collective-permute-start | bytes 516104 | tf_op jit(solution)/shard_map/ppermute | solution.py:323
  17.4 17.1 %collective-permute-start.3 = (bf16[48,1792]{1,0:T(8,128)(2,1)S(1)}, bf16[48,1792]{1,0:T(8,128)(2,1)S(1)}, u32[]{:S(2)}, u32[]{:S(2)}) collective-permute-start(bf16[48,1792]{1,0:T(8,128)(2,1)S(1)} %get-tuple-element.24.after.refs_0_), channel_id=1, source_target_pairs={{0,1},{1,0},{2,3},{3,2},{4,5},{5,4},{6,7},{7,6},{8,9},{9,8},{10,11... | collective-permute-start | bytes 516104 | tf_op jit(solution)/shard_map/ppermute | solution.py:326
  17.9 9.7 %copy-start = (bf16[2,512,576]{1,2,0:T(8,128)(2,1)S(1)}, bf16[2,512,576]{1,2,0:T(8,128)(2,1)}, u32[]{:S(2)}) copy-start(bf16[2,512,576]{1,2,0:T(8,128)(2,1)} %param.16) | copy-start | bytes 3538948
  17.9 9.7 %copy-start.1 = (bf16[2,128,576]{1,2,0:T(8,128)(2,1)S(1)}, bf16[2,128,576]{1,2,0:T(8,128)(2,1)}, u32[]{:S(2)}) copy-start(bf16[2,128,576]{1,2,0:T(8,128)(2,1)} %param.15) | copy-start | bytes 884740
  17.9 9.7 %copy-start.6 = (s32[2]{0:T(128)S(1)}, s32[2]{0:T(128)}, u32[]{:S(2)}) copy-start(s32[2]{0:T(128)} %lengths.1) | copy-start | bytes 28
  34.5 29.4 %copy-start.4 = (s32[8,2]{0,1:T(2,128)S(1)}, s32[8,2]{0,1:T(2,128)}, u32[]{:S(2)}) copy-start(s32[8,2]{0,1:T(2,128)} %param.10) | copy-start | bytes 196
  34.5 29.4 %copy-start.5 = (f32[8,2]{0,1:T(2,128)S(1)}, f32[8,2]{0,1:T(2,128)}, u32[]{:S(2)}) copy-start(f32[8,2]{0,1:T(2,128)} %param.11) | copy-start | bytes 196
  43.1 7.3 %collective-permute-start.6 = (bf16[48,1792]{1,0:T(8,128)(2,1)S(1)}, bf16[48,1792]{1,0:T(8,128)(2,1)S(1)}, u32[]{:S(2)}, u32[]{:S(2)}) collective-permute-start(bf16[48,1792]{1,0:T(8,128)(2,1)S(1)} %get-tuple-element.30), channel_id=1, source_target_pairs={{0,1},{1,0},{2,3},{3,2},{4,5},{5,4},{6,7},{7,6},{8,9},{9,8},{10,11... | collective-permute-start | bytes 516104 | tf_op jit(solution)/shard_map/ppermute | solution.py:326
  44.7 5.8 %collective-permute-start.7 = (bf16[48,1792]{1,0:T(8,128)(2,1)S(1)}, bf16[48,1792]{1,0:T(8,128)(2,1)S(1)}, u32[]{:S(2)}, u32[]{:S(2)}) collective-permute-start(bf16[48,1792]{1,0:T(8,128)(2,1)S(1)} %get-tuple-element.31), channel_id=1, source_target_pairs={{0,2},{2,0},{4,6},{6,4},{8,10},{10,8},{12,14},{14,12},{1,3},{3,1},... | collective-permute-start | bytes 516104 | tf_op jit(solution)/shard_map/ppermute | solution.py:323
  44.7 7.2 %collective-permute-start.8 = (bf16[48,1792]{1,0:T(8,128)(2,1)S(1)}, bf16[48,1792]{1,0:T(8,128)(2,1)S(1)}, u32[]{:S(2)}, u32[]{:S(2)}) collective-permute-start(bf16[48,1792]{1,0:T(8,128)(2,1)S(1)} %get-tuple-element.32), channel_id=1, source_target_pairs={{0,3},{1,2},{2,1},{3,0},{4,7},{5,6},{6,5},{7,4},{8,11},{9,10},{10,... | collective-permute-start | bytes 516104 | tf_op jit(solution)/shard_map/ppermute | solution.py:329
  52.4 5.3 %collective-permute-start.9 = (bf16[48,896]{1,0:T(8,128)(2,1)S(1)}, bf16[48,896]{1,0:T(8,128)(2,1)S(1)}, u32[]{:S(2)}, u32[]{:S(2)}) collective-permute-start(bf16[48,896]{1,0:T(8,128)(2,1)S(1)} %get-tuple-element.34), channel_id=1, source_target_pairs={{0,4},{2,6},{4,0},{6,2},{8,12},{10,14},{12,8},{14,10},{1,5},{3,7},... | collective-permute-start | bytes 258056 | tf_op jit(solution)/shard_map/ppermute | solution.py:320
  54.0 9.9 %collective-permute-start.10 = (bf16[48,896]{1,0:T(8,128)(2,1)S(1)}, bf16[48,896]{1,0:T(8,128)(2,1)S(1)}, u32[]{:S(2)}, u32[]{:S(2)}) collective-permute-start(bf16[48,896]{1,0:T(8,128)(2,1)S(1)} %get-tuple-element.35), channel_id=1, source_target_pairs={{0,8},{2,10},{4,12},{6,14},{8,0},{10,2},{12,4},{14,6},{1,9},{3,11}... | collective-permute-start | bytes 258056 | tf_op jit(solution)/shard_map/ppermute | solution.py:320
  55.5 8.3 %collective-permute-start.11 = (bf16[48,896]{1,0:T(8,128)(2,1)S(1)}, bf16[48,896]{1,0:T(8,128)(2,1)S(1)}, u32[]{:S(2)}, u32[]{:S(2)}) collective-permute-start(bf16[48,896]{1,0:T(8,128)(2,1)S(1)} %get-tuple-element.36), channel_id=1, source_target_pairs={{0,12},{2,14},{4,8},{6,10},{8,4},{10,6},{12,0},{14,2},{1,13},{3,15... | collective-permute-start | bytes 258056 | tf_op jit(solution)/shard_map/ppermute | solution.py:320

commit v3 on v0

--- a/solution.py
+++ b/solution.py
@@ -1,10 +1,15 @@
+import functools
+
 import jax
 import jax.numpy as jnp
 from jax import lax
+from jax.experimental import pallas as pl
+from jax.experimental.pallas import tpu as pltpu
 from jax.sharding import PartitionSpec as P
 
 ROPE = 64
-
+CORES = 2
+MIB = 1 << 20
 
 softmax_scale = 1.0 / 192.0**0.5
 
@@ -31,13 +36,13 @@
     ).astype(jnp.bfloat16)
 
 
-def per_device(tokens, expert_ids, gate_weights, w_gate, w_up, w_down, queries, cache, lengths):
+def plain(tokens, expert_ids, gate_weights, w_gate, w_up, w_down, queries, cache, lengths):
     n_ep = lax.axis_size("ep")
     n_dp = lax.axis_size("dp")
     tok_rows = tokens.shape[0]
     width = tokens.shape[1]
     top = expert_ids.shape[1]
-    capacity = (3 * tok_rows * top + 2 * n_ep - 1) // (2 * n_ep)
+    capacity = slots_per_expert(tok_rows, top, n_ep)
     flat_ids = expert_ids.reshape(-1)
     onehot = (flat_ids[:, None] == jnp.arange(n_ep, dtype=jnp.int32)[None, :]).astype(jnp.int32)
     slots = jnp.sum((jnp.cumsum(onehot, axis=0) - 1) * onehot, axis=1)
@@ -64,6 +69,364 @@
     moe_out = jnp.sum(gate_weights[:, :, None] * picked, axis=1).astype(jnp.bfloat16)
     attn_out = attend(queries, cache, lengths)
     return (moe_out, attn_out)
+
+
+def slots_per_expert(tok_rows, top, n_ep):
+    return (3 * tok_rows * top + 2 * n_ep - 1) // (2 * n_ep)
+
+
+PIECES = 8
+
+
+def iota(shape, dim):
+    return lax.broadcasted_iota(jnp.int32, shape, dim)
+
+
+def split(value, *sizes):
+    digits = []
+    for size in reversed(sizes):
+        digits.append(lax.rem(value, size))
+        value = lax.div(value, size)
+    return [value] + digits[::-1]
+
+
+def ones(mask):
+    return jnp.where(mask, 1.0, 0.0).astype(jnp.bfloat16)
+
+
+def dot(a, b):
+    return jnp.dot(a, b, preferred_element_type=jnp.float32)
+
+
+def move(mask, rows):
+    return dot(ones(mask), rows).astype(jnp.bfloat16)
+
+
+def below(refs):
+    return jnp.concatenate([ref[...] for ref in refs], axis=0)
+
+
+def chip_index():
+    return lax.div(lax.axis_index("ep"), CORES)
+
+
+def core_index():
+    return lax.rem(lax.axis_index("ep"), CORES)
+
+
+def slot_table(ids, chips, capacity, which=None):
+    top, toks = ids.shape
+    rows = chips * PIECES * CORES * capacity
+    away, piece, core, slot = split(iota((rows, toks), 0), PIECES, CORES, capacity)
+    expert = (chip_index() ^ away) * CORES + core
+    named = [ids[k : k + 1, :] == expert for k in range(top)]
+    any_named = functools.reduce(jnp.logical_or, named)
+    before = ones(iota((toks, toks), 0) < iota((toks, toks), 1))
+    rank = dot(ones(any_named), before)
+    return (any_named if which is None else named[which]) & (rank == slot.astype(jnp.float32))
+
+
+def spread_pieces(table, chips, capacity):
+    rows, toks = table.shape
+    repeat = ones(iota((toks, PIECES * toks), 0) == lax.rem(iota((toks, PIECES * toks), 1), toks))
+    wide = dot(ones(table), repeat)
+    piece = split(iota(wide.shape, 0), PIECES, CORES, capacity)[1]
+    return jnp.where(piece == lax.div(iota(wide.shape, 1), toks), wide, 0.0).astype(jnp.bfloat16)
+
+
+def pack_kernel(capacity, chips, ids_hbm, tok_hbm, *refs):
+    outs, (ids_ref, tok_ref, sems) = refs[:chips], refs[chips:]
+    copies = [
+        pltpu.make_async_copy(ids_hbm, ids_ref, sems.at[0]),
+        pltpu.make_async_copy(tok_hbm, tok_ref, sems.at[1]),
+    ]
+    for copy in copies:
+        copy.start()
+    copies[0].wait()
+    select = spread_pieces(slot_table(ids_ref[...], chips, capacity), chips, capacity)
+    copies[1].wait()
+    wide = tok_ref.shape[1] // PIECES
+    toks = tok_ref[...].astype(jnp.float32)
+    stacked = jnp.concatenate(
+        [toks[:, k * wide : (k + 1) * wide] for k in range(PIECES)], axis=0
+    ).astype(jnp.bfloat16)
+    packed = dot(select, stacked).astype(jnp.bfloat16)
+    rows = outs[0].shape[0]
+    for d, out in enumerate(outs):
+        out[...] = packed[d * rows : (d + 1) * rows]
+
+
+def near_kernel(capacity, batch, after, *refs):
+    del after
+    ins, (same, other) = refs[:batch], refs[batch:]
+    rows = below(ins)
+    shape = (same.shape[0], rows.shape[0])
+    piece, away, slot = split(iota(shape, 0), batch, capacity)
+    from_away, from_piece, from_core, from_slot = split(iota(shape, 1), PIECES, CORES, capacity)
+    match = (away == from_away) & (slot == from_slot) & (piece == from_piece)
+    same[...] = move(match & (from_core == core_index()), rows)
+    other[...] = move(match & (from_core != core_index()), rows)
+
+
+def expert_kernel(n_in, held, *refs):
+    ins, (gate_ref, up_ref, up_hbm, down_hbm), refs = refs[:n_in], refs[n_in : n_in + 4], refs[n_in + 4 :]
+    outs, (stack, hidden, up_rest, down_ref, sems) = refs[:n_in], refs[n_in:]
+    rows, wide = ins[0].shape
+    part = rows // PIECES
+    total = n_in * part
+    rest = [
+        pltpu.make_async_copy(
+            up_hbm.at[pl.ds(p * wide, wide)],
+            up_rest.at[pl.ds((p - held) * wide, wide)],
+            sems.at[p],
+        )
+        for p in range(held, PIECES)
+    ]
+    down = [
+        pltpu.make_async_copy(
+            down_hbm.at[:, pl.ds(p * wide, wide)],
+            down_ref.at[:, pl.ds(p * wide, wide)],
+            sems.at[PIECES + p],
+        )
+        for p in range(PIECES)
+    ]
+    for copy in rest + down:
+        copy.start()
+    shape = (PIECES * total, n_in * rows)
+    piece, who, which = split(iota(shape, 0), n_in, part)
+    from_who, from_piece, from_which = split(iota(shape, 1), PIECES, part)
+    match = (who == from_who) & (which == from_which) & (piece == from_piece)
+    stack[...] = move(match, below(ins))
+    gate = up = 0.0
+    for p in range(PIECES):
+        span = slice(p * wide, (p + 1) * wide)
+        gate += dot(stack[p * total : (p + 1) * total], gate_ref[span, :])
+    for p in range(PIECES):
+        if p < held:
+            block = up_ref[p * wide : (p + 1) * wide, :]
+        else:
+            rest[p - held].wait()
+            block = up_rest[(p - held) * wide : (p - held + 1) * wide, :]
+        up += dot(stack[p * total : (p + 1) * total], block)
+    hidden[...] = (gate / (1.0 + jnp.exp(-gate)) * up).astype(jnp.bfloat16)
+    for p in range(PIECES):
+        down[p].wait()
+        stack[p * total : (p + 1) * total] = dot(
+            hidden[...], down_ref[:, p * wide : (p + 1) * wide]
+        ).astype(jnp.bfloat16)
+    shape = (n_in * rows, PIECES * total)
+    who, piece, which = split(iota(shape, 0), PIECES, part)
+    from_piece, from_who, from_which = split(iota(shape, 1), n_in, part)
+    match = (who == from_who) & (which == from_which) & (piece == from_piece)
+    back = move(match, stack[...])
+    for s, out in enumerate(outs):
+        out[...] = back[s * rows : (s + 1) * rows]
+
+
+def sum_kernel(capacity, batch, after, own, along, beside, across, *outs):
+    del after
+    f32 = jnp.float32
+    same = own[...].astype(f32) + along[...].astype(f32)
+    other = beside[...].astype(f32) + across[...].astype(f32)
+    rows = jnp.concatenate([same.astype(jnp.bfloat16), other.astype(jnp.bfloat16)], axis=0)
+    far_rows = outs[0].shape[0]
+    shape = (batch * far_rows, rows.shape[0])
+    away, piece, core, slot = split(iota(shape, 0), PIECES, CORES, capacity)
+    from_other, from_piece, from_away, from_slot = split(iota(shape, 1), PIECES, batch, capacity)
+    match = (away == from_away) & (slot == from_slot) & (piece == from_piece)
+    sent = move(match & ((core != core_index()) == (from_other == 1)), rows)
+    for d, out in enumerate(outs):
+        out[...] = sent[d * far_rows : (d + 1) * far_rows]
+
+
+def combine_kernel(chips, picks_ref, gains_ref, *refs):
+    ins, out = refs[:chips], refs[chips]
+    wide = ins[0].shape[1]
+    top, toks = gains_ref.shape
+    picked = dot(picks_ref[...], below(ins))
+    eye = iota((toks, toks), 0) == iota((toks, toks), 1)
+    gains = [
+        jnp.sum(jnp.where(eye, gains_ref[k : k + 1, :], 0.0), axis=1, keepdims=True)
+        for k in range(top)
+    ]
+    for p in range(PIECES):
+        terms = [
+            picked[(k * PIECES + p) * toks : (k * PIECES + p + 1) * toks] * gains[k]
+            for k in range(top)
+        ]
+        out[:, p * wide : (p + 1) * wide] = sum(terms[1:], terms[0]).astype(jnp.bfloat16)
+
+
+def start_copies(src, dst, sems, cuts):
+    rows = dst.shape[0] // cuts
+    spans = [pl.ds(j * rows, rows) for j in range(cuts)]
+    copies = [
+        pltpu.make_async_copy(src.at[span], dst.at[span], sems.at[j]) for j, span in enumerate(spans)
+    ]
+    for copy in copies:
+        copy.start()
+    return copies
+
+
+def fetch_kernel(cuts, after, w_gate, got_gate, done, sems):
+    del after
+    for copy in start_copies(w_gate, got_gate, sems, cuts):
+        copy.wait()
+    done[...] = jnp.zeros_like(done)
+
+
+def attend_kernel(cuts, latent, chips, capacity, after, lengths, ids_ref, w_up, queries, cache, got_up, out, picks, sems):
+    del after
+    copies = start_copies(w_up, got_up, sems, cuts)
+    top, toks = ids_ref.shape
+    requests, _, heads = queries.shape
+    width = cache.shape[2]
+    rows = picks.shape[1]
+    eye = ones(iota((rows, rows), 0) == iota((rows, rows), 1))
+    for k in range(top):
+        select = spread_pieces(slot_table(ids_ref[...], chips, capacity, k), chips, capacity)
+        picks[k * PIECES * toks : (k + 1) * PIECES * toks] = lax.dot_general(
+            select, eye, (((0,), (0,)), ((), ())), preferred_element_type=jnp.float32
+        ).astype(jnp.bfloat16)
+    for r in range(requests):
+        scores = (
+            lax.dot_general(
+                queries[r], cache[r], (((0,), (0,)), ((), ())), preferred_element_type=jnp.float32
+            )
+            * softmax_scale
+        )
+        scores = jnp.where(iota((heads, width), 1) < lengths[r], scores, -jnp.inf)
+        weights = jnp.exp(scores - jnp.max(scores, axis=1, keepdims=True))
+        probs = (weights / jnp.sum(weights, axis=1, keepdims=True)).astype(jnp.bfloat16)
+        out[r] = lax.dot_general(
+            probs,
+            cache[r, :latent, :],
+            (((1,), (1,)), ((), ())),
+            preferred_element_type=jnp.float32,
+        ).astype(jnp.bfloat16)
+    for copy in copies:
+        copy.wait()
+
+
+VMEM = pl.BlockSpec(memory_space=pltpu.VMEM)
+HBM = pl.BlockSpec(memory_space=pltpu.HBM)
+SMEM = pl.BlockSpec(memory_space=pltpu.SMEM)
+DMA = pltpu.SemaphoreType.DMA
+
+
+def call(kernel, name, out_shape, in_specs, out_specs, scratch, limit, args, flops=0, moved=0):
+    return pl.pallas_call(
+        kernel,
+        name=name,
+        out_shape=out_shape,
+        in_specs=in_specs,
+        out_specs=out_specs,
+        scratch_shapes=scratch,
+        compiler_params=pltpu.CompilerParams(vmem_limit_bytes=limit),
+        cost_estimate=pl.CostEstimate(flops=flops, bytes_accessed=moved, transcendentals=0),
+    )(*args)
+
+
+def paired(n_ep, tokens, expert_ids, gate_weights, w_gate, w_up, w_down, queries, cache, lengths):
+    chips = n_ep // CORES
+    batches = [(0, 1), (2, 3)]
+    batch = 2
+    toks, width = tokens.shape
+    top = expert_ids.shape[1]
+    bf16 = jnp.bfloat16
+    capacity = slots_per_expert(toks, top, n_ep)
+    wide = width // PIECES
+    far = jax.ShapeDtypeStruct((PIECES * CORES * capacity, wide), bf16)
+    near = jax.ShapeDtypeStruct((PIECES * batch * capacity, wide), bf16)
+    in_hbm = functools.partial(pltpu.with_memory_space_constraint, memory_space=pltpu.HBM)
+    w_gate, w_up, w_down = in_hbm(w_gate[0]), in_hbm(w_up[0]), in_hbm(w_down[0])
+    units = w_gate.shape[1]
+    ids, gains = expert_ids.T, gate_weights.T
+
+    def to_chip(x, d):
+        return lax.ppermute(x, "ep", [(i, i ^ (CORES * d)) for i in range(n_ep)])
+
+    def along(x):
+        return lax.ppermute(x, "dp", [(0, 1), (1, 0)])
+
+    def beside(x):
+        return lax.ppermute(x, "ep", [(i, i ^ 1) for i in range(n_ep)])
+
+    def across(x):
+        return lax.ppermute(x, ("ep", "dp"), [(i, i ^ 3) for i in range(2 * n_ep)])
+
+    packed = call(
+        functools.partial(pack_kernel, capacity, chips),
+        "pack", (far,) * chips, [HBM] * 2, (VMEM,) * chips,
+        [pltpu.VMEM(ids.shape, ids.dtype), pltpu.VMEM(tokens.shape, bf16), DMA((2,))],
+        2 * MIB, (in_hbm(ids), in_hbm(tokens)),
+    )
+    landed = [None] * chips
+    landed[0] = packed[0]
+    for d in (2, 3, 1):
+        landed[d] = to_chip(packed[d], d)
+    cuts = 8
+    got_gate, token = call(
+        functools.partial(fetch_kernel, cuts),
+        "fetch", (pltpu.VMEM(w_gate.shape, bf16), jax.ShapeDtypeStruct((8, 128), jnp.float32)),
+        [HBM] * 2, (VMEM, VMEM), [DMA((cuts,))], 1 * MIB, (packed[0], w_gate), moved=2 * w_gate.size,
+    )
+    arrived = []
+    for chosen in batches:
+        same, other = call(
+            functools.partial(near_kernel, capacity, batch),
+            "near", (near,) * 2, [HBM] + [VMEM] * batch, (VMEM,) * 2, [], 1 * MIB,
+            (token, *[landed[d] for d in chosen]),
+        )
+        token = same
+        arrived += [same, along(same), beside(other), across(other)]
+    latent = cache.shape[2] - ROPE
+    held = PIECES // 2
+    picks_shape = (top * PIECES * toks, chips * far.shape[0])
+    got_up, attn_out, picks = call(
+        functools.partial(attend_kernel, held, latent, chips, capacity),
+        "attend",
+        (
+            pltpu.VMEM((held * wide, units), bf16),
+            jax.ShapeDtypeStruct(queries.shape[:2] + (latent,), bf16),
+            jax.ShapeDtypeStruct(picks_shape, bf16),
+        ),
+        [HBM, SMEM, VMEM, HBM, VMEM, VMEM], (VMEM,) * 3, [DMA((held,))], 2 * MIB,
+        (token, lengths, ids, w_up, queries.swapaxes(1, 2), cache.swapaxes(1, 2)),
+        moved=held * wide * units * 2,
+    )
+    n_in = len(arrived)
+    rows = n_in * batch * capacity
+    parts = call(
+        functools.partial(expert_kernel, n_in, held),
+        "experts", (near,) * n_in, [VMEM] * (n_in + 2) + [HBM] * 2, (VMEM,) * n_in,
+        [
+            pltpu.VMEM((PIECES * rows, wide), bf16),
+            pltpu.VMEM((rows, units), bf16),
+            pltpu.VMEM(((PIECES - held) * wide, units), bf16),
+            pltpu.VMEM(w_down.shape, bf16),
+            DMA((2 * PIECES,)),
+        ],
+        28 * MIB, (*arrived, got_gate, got_up, w_up, w_down), flops=6 * rows * width * units,
+    )
+    back = [None] * chips
+    token = picks
+    for b in reversed(range(len(batches))):
+        own, x, core, diagonal = parts[4 * b : 4 * b + 4]
+        sums = call(
+            functools.partial(sum_kernel, capacity, batch),
+            "sums", (far,) * batch, [HBM] + [VMEM] * 4, (VMEM,) * batch, [], 1 * MIB,
+            (token, own, along(x), beside(core), across(diagonal)),
+        )
+        token = sums[0]
+        for d, value in zip(batches[b], sums):
+            back[d] = to_chip(value, d) if d else value
+    moe_out = call(
+        functools.partial(combine_kernel, chips),
+        "combine", jax.ShapeDtypeStruct(tokens.shape, bf16), [VMEM] * (2 + chips), VMEM, [],
+        4 * MIB, (picks, gains, *back),
+    )
+    return moe_out, attn_out
 
 
 def solution(mesh):
@@ -78,8 +441,10 @@
         P(("group", "ep", "dp"), None, None),
         P(("group", "ep", "dp")),
     )
+    n_ep, n_dp = mesh.shape["ep"], mesh.shape["dp"]
+    fits = n_dp == 2 and n_ep == 8
     return jax.shard_map(
-        per_device,
+        functools.partial(paired, n_ep) if fits else plain,
         mesh=mesh,
         in_specs=placed,
         out_specs=(P(("group", "ep", "dp"), None), P(("group", "ep", "dp"), None, None)),

time: 88.1 us -> 53.8 us (0.61); the launches traced: 87.1 us -> 53.6 us
  blocking collectives: 30.7 us -> 0 us
  matrix products: 25.5 us -> 0 us
  Pallas kernels: 0 us -> 22.7 us
  starting transfers between devices: 3.66 us -> 18.2 us
  waiting for transfers between devices: 19.2 us -> 11.9 us
  local copies, waits for them, and re-layouts: 4.81 us -> 0.02 us
  other arithmetic: 2.51 us -> 0 us
    all_to_all x1 -> x0, blocking collectives: 30.7 us -> none  [per_device(): lax.all_to_all(spread.reshape(n_ep * n_dp, capacity, width), ('ep', 'dp')...]
    dot_general x5 -> x0, matrix products: 25.5 us -> none  [the longest x1 14.7 us: expert_rows(): return jnp.dot(hidden, w_down[0], preferred_element_type=jnp.float32)]
    pallas_call x0 -> x9, Pallas kernels: none -> 22.7 us  [call(): pl.pallas_call(kernel, name=name, out_shape=out_shape, in_specs=in_specs,...]
    all_to_all x1 -> x0, waiting for transfers between devices: 19.2 us -> none  [per_device(): lax.all_to_all(partial_out.reshape(arrived.shape), ('ep', 'dp'), split_ax...]
    ppermute x0 -> x18, starting transfers between devices: none -> 18.2 us  [the longest x6 10.3 us: to_chip(): return lax.ppermute(x, 'ep', [(i, i ^ CORES * d) for i in range(n_ep)])]
    ppermute x0 -> x18, waiting for transfers between devices: none -> 11.9 us  [the longest x6 7.95 us: to_chip(): return lax.ppermute(x, 'ep', [(i, i ^ CORES * d) for i in range(n_ep)])]
    all_to_all x1 -> x0, starting transfers between devices: 3.66 us -> none  [per_device(): lax.all_to_all(partial_out.reshape(arrived.shape), ('ep', 'dp'), split_ax...]
    reshape x3 -> x0, local copies, waits for them, and re-layouts: 2.17 us -> none  [the longest x1 1.22 us: per_device(): partial_out.reshape(arrived.shape)]
  transfers between devices with their start and end apart: 1 -> 18, of which waited for: 1 -> 8; matrix products, arithmetic and copies ran while one was open for 3% -> 0% of each run, Pallas kernels for 0% -> 20%
where the time goes in v3:
time: 53.8 us; the launch traced here: 53.6 us
  Pallas kernels  22.7 us (42%)
  starting transfers between devices  18.2 us (34%)
  waiting for transfers between devices  11.9 us (22%)
  between operations  0.79 us (1%)
    pallas_call x9, Pallas kernels, call(): pl.pallas_call(kernel, name=name, out_shape=out_shape, in_specs=in_specs,...  22.7 us
    ppermute x6, starting transfers between devices, to_chip(): return lax.ppermute(x, 'ep', [(i, i ^ CORES * d) for i in range(n_ep)])  10.3 us
    ppermute x6, waiting for transfers between devices, to_chip(): return lax.ppermute(x, 'ep', [(i, i ^ CORES * d) for i in range(n_ep)])  7.95 us
    ppermute x4, starting transfers between devices, along(): return lax.ppermute(x, 'dp', [(0, 1), (1, 0)])  3.86 us
    ppermute x4, waiting for transfers between devices, across(): return lax.ppermute(x, ('ep', 'dp'), [(i, i ^ 3) for i in range(2 * n_ep)])  2.6 us
    ppermute x4, starting transfers between devices, beside(): return lax.ppermute(x, 'ep', [(i, i ^ 1) for i in range(n_ep)])  2.38 us
    ppermute x4, starting transfers between devices, across(): return lax.ppermute(x, ('ep', 'dp'), [(i, i ^ 3) for i in range(2 * n_ep)])  1.72 us
    ppermute x4, waiting for transfers between devices, along(): return lax.ppermute(x, 'dp', [(0, 1), (1, 0)])  1.35 us
  transfers between devices with their start and end apart: 18, of which 8 were waited for; matrix products, arithmetic and copies ran while one was open for 0% of the time, Pallas kernels for 20%

profile of v3, /device:TPU:0, one launch (start us, length us, event | category | flops | bytes accessed | tf_op | source)
XLA Modules:
  0.0 53.6 jit_solution(387928484753709010)
XLA Ops:
  0.6 0.0 copy-start.2
  0.6 0.0 copy-start.4
  0.7 0.0 copy-start
  0.7 1.4 %pack.1 = (bf16[48,896]{1,0:T(8,128)(2,1)S(1)}, bf16[48,896]{1,0:T(8,128)(2,1)S(1)}, bf16[48,896]{1,0:T(8,128)(2,1)S(1)}, bf16[48,896]{1,0:T(8,128)(2,1)S(1)}) custom-call(s32[2,8]{1,0:T(2,128)} %bitcast.9, bf16[8,7168]{1,0:T(8,128)(2,1)} %tok_hbm.1), custom_call_target="tpu_custom_call" | custom-call | tf_op jit(solution)/shard_map/pack/pallas_call | solution.py:318
  2.1 3.1 %collective-permute-start = (bf16[48,896]{1,0:T(8,128)(2,1)S(1)}, bf16[48,896]{1,0:T(8,128)(2,1)S(1)}, u32[]{:S(2)}, u32[]{:S(2)}) collective-permute-start(bf16[48,896]{1,0:T(8,128)(2,1)S(1)} %get-tuple-element.29), channel_id=1, source_target_pairs={{0,4},{2,6},{4,0},{6,2},{8,12},{10,14},{12,8},{14,10},{1,5},{3,7},... | collective-permute-start | bytes 258056 | tf_op jit(solution)/shard_map/ppermute | solution.py:347
  5.2 2.6 %collective-permute-start.1 = (bf16[48,896]{1,0:T(8,128)(2,1)S(1)}, bf16[48,896]{1,0:T(8,128)(2,1)S(1)}, u32[]{:S(2)}, u32[]{:S(2)}) collective-permute-start(bf16[48,896]{1,0:T(8,128)(2,1)S(1)} %get-tuple-element.31), channel_id=1, source_target_pairs={{0,8},{2,10},{4,12},{6,14},{8,0},{10,2},{12,4},{14,6},{1,9},{3,11}... | collective-permute-start | bytes 258056 | tf_op jit(solution)/shard_map/ppermute | solution.py:347
  7.7 0.0 collective-permute-start.2
  7.8 5.3 %fetch.1 = (bf16[7168,1024]{1,0:T(8,128)(2,1)S(1)}, f32[8,128]{1,0:T(8,128)S(1)}) custom-call(bf16[48,896]{1,0:T(8,128)(2,1)S(1)} %get-tuple-element.27.after.refs_0_, bf16[7168,1024]{1,0:T(8,128)(2,1)} %bitcast.14), custom_call_target="tpu_custom_call" | custom-call | bytes 14680064 | tf_op jit(solution)/shard_map/fetch/pallas_call | solution.py:318
  13.1 0.0 collective-permute-done.refs_1_
  13.1 0.2 near.2
  13.3 1.4 %collective-permute-done.1.refs_0_ = bf16[48,896]{1,0:T(8,128)(2,1)S(1)} collective-permute-done((bf16[48,896]{1,0:T(8,128)(2,1)S(1)}, bf16[48,896]{1,0:T(8,128)(2,1)S(1)}, u32[]{:S(2)}, u32[]{:S(2)}) %collective-permute-start.1) | collective-permute-done | bytes 86048 | tf_op jit(solution)/shard_map/ppermute | solution.py:347
  14.7 0.0 collective-permute-done.2.refs_1_
  14.7 0.2 near.3
  14.9 0.1 collective-permute-start.8
  14.9 1.6 %collective-permute-start.7 = (bf16[48,896]{1,0:T(8,128)(2,1)S(1)}, bf16[48,896]{1,0:T(8,128)(2,1)S(1)}, u32[]{:S(2)}, u32[]{:S(2)}) collective-permute-start(bf16[48,896]{1,0:T(8,128)(2,1)S(1)} %get-tuple-element.36), channel_id=1, source_target_pairs={{0,2},{2,0},{4,6},{6,4},{8,10},{10,8},{12,14},{14,12},{1,3},{3,1},... | collective-permute-start | bytes 258056 | tf_op jit(solution)/shard_map/ppermute | solution.py:353
  16.5 0.5 collective-permute-start.6
  17.1 0.8 %collective-permute-start.5 = (bf16[48,896]{1,0:T(8,128)(2,1)S(1)}, bf16[48,896]{1,0:T(8,128)(2,1)S(1)}, u32[]{:S(2)}, u32[]{:S(2)}) collective-permute-start(bf16[48,896]{1,0:T(8,128)(2,1)S(1)} %get-tuple-element.35), channel_id=1, source_target_pairs={{0,3},{1,2},{2,1},{3,0},{4,7},{5,6},{6,5},{7,4},{8,11},{9,10},{10,... | collective-permute-start | bytes 258056 | tf_op jit(solution)/shard_map/ppermute | solution.py:356
  17.9 0.8 %collective-permute-start.4 = (bf16[48,896]{1,0:T(8,128)(2,1)S(1)}, bf16[48,896]{1,0:T(8,128)(2,1)S(1)}, u32[]{:S(2)}, u32[]{:S(2)}) collective-permute-start(bf16[48,896]{1,0:T(8,128)(2,1)S(1)} %get-tuple-element.35), channel_id=1, source_target_pairs={{0,2},{2,0},{4,6},{6,4},{8,10},{10,8},{12,14},{14,12},{1,3},{3,1},... | collective-permute-start | bytes 258056 | tf_op jit(solution)/shard_map/ppermute | solution.py:353
  18.7 1.0 %collective-permute-done.8.refs_7_ = bf16[48,896]{1,0:T(8,128)(2,1)S(1)} collective-permute-done((bf16[48,896]{1,0:T(8,128)(2,1)S(1)}, bf16[48,896]{1,0:T(8,128)(2,1)S(1)}, u32[]{:S(2)}, u32[]{:S(2)}) %collective-permute-start.8) | collective-permute-done | bytes 86048 | tf_op jit(solution)/shard_map/ppermute | solution.py:356
  19.7 0.6 %collective-permute-start.3 = (bf16[48,896]{1,0:T(8,128)(2,1)S(1)}, bf16[48,896]{1,0:T(8,128)(2,1)S(1)}, u32[]{:S(2)}, u32[]{:S(2)}) collective-permute-start(bf16[48,896]{1,0:T(8,128)(2,1)S(1)} %get-tuple-element.30.after.refs_0_), channel_id=1, source_target_pairs={{0,1},{1,0},{2,3},{3,2},{4,5},{5,4},{6,7},{7,6},{8,9},{9,8},{10,11... | collective-permute-start | bytes 258056 | tf_op jit(solution)/shard_map/ppermute | solution.py:350
  20.4 4.8 %attend.1 = (bf16[3584,1024]{1,0:T(8,128)(2,1)S(1)}, bf16[2,128,512]{2,1,0:T(8,128)(2,1)}, bf16[128,192]{1,0:T(8,128)(2,1)S(1)}) custom-call(bf16[48,896]{1,0:T(8,128)(2,1)S(1)} %get-tuple-element.33.after.refs_4_, s32[2]{0:T(128)S(1)} %copy-done.4, s32[2,8]{1,0:T(2,128)S(1)} %bitcast.10, bf16[7168,1024]{1,0:T(8,128)(2,1)} %bitcast.12, ...), custom_call_target="tpu_custom_call" | custom-call | bytes 7340032 | tf_op jit(solution)/shard_map/attend/pallas_call | solution.py:318
  25.1 0.0 collective-permute-done.7.refs_6_
  25.2 0.0 collective-permute-done.6.refs_5_
  25.2 0.0 collective-permute-done.5.refs_3_
  25.2 0.0 collective-permute-done.4.refs_2_
  25.2 0.1 collective-permute-done.3.refs_1_
  25.3 9.5 %experts.1 = (bf16[48,896]{1,0:T(8,128)(2,1)S(1)}, bf16[48,896]{1,0:T(8,128)(2,1)S(1)}, bf16[48,896]{1,0:T(8,128)(2,1)S(1)}, bf16[48,896]{1,0:T(8,128)(2,1)S(1)}...) custom-call(bf16[48,896]{1,0:T(8,128)(2,1)S(1)} %get-tuple-element.3, ...), custom_call_target="tpu_custom_call" | custom-call | flops 2113929216 | tf_op jit(solution)/shard_map/experts/pallas_call | solution.py:318
  34.8 1.4 %collective-permute-start.9 = (bf16[48,896]{1,0:T(8,128)(2,1)S(1)}, bf16[48,896]{1,0:T(8,128)(2,1)S(1)}, u32[]{:S(2)}, u32[]{:S(2)}) collective-permute-start(bf16[48,896]{1,0:T(8,128)(2,1)S(1)} %get-tuple-element.40), channel_id=1, source_target_pairs={{0,1},{1,0},{2,3},{3,2},{4,5},{5,4},{6,7},{7,6},{8,9},{9,8},{10,11... | collective-permute-start | bytes 258056 | tf_op jit(solution)/shard_map/ppermute | solution.py:350
  36.2 0.0 collective-permute-start.10
  36.2 0.8 %collective-permute-start.11 = (bf16[48,896]{1,0:T(8,128)(2,1)S(1)}, bf16[48,896]{1,0:T(8,128)(2,1)S(1)}, u32[]{:S(2)}, u32[]{:S(2)}) collective-permute-start(bf16[48,896]{1,0:T(8,128)(2,1)S(1)} %get-tuple-element.42), channel_id=1, source_target_pairs={{0,3},{1,2},{2,1},{3,0},{4,7},{5,6},{6,5},{7,4},{8,11},{9,10},{10,... | collective-permute-start | bytes 258056 | tf_op jit(solution)/shard_map/ppermute | solution.py:356
  37.0 1.3 %collective-permute-start.12 = (bf16[48,896]{1,0:T(8,128)(2,1)S(1)}, bf16[48,896]{1,0:T(8,128)(2,1)S(1)}, u32[]{:S(2)}, u32[]{:S(2)}) collective-permute-start(bf16[48,896]{1,0:T(8,128)(2,1)S(1)} %get-tuple-element.45), channel_id=1, source_target_pairs={{0,1},{1,0},{2,3},{3,2},{4,5},{5,4},{6,7},{7,6},{8,9},{9,8},{10,11... | collective-permute-start | bytes 258056 | tf_op jit(solution)/shard_map/ppermute | solution.py:350
  38.3 0.0 collective-permute-start.13
  38.3 1.2 %collective-permute-done.9.along = bf16[48,896]{1,0:T(8,128)(2,1)S(1)} collective-permute-done((bf16[48,896]{1,0:T(8,128)(2,1)S(1)}, bf16[48,896]{1,0:T(8,128)(2,1)S(1)}, u32[]{:S(2)}, u32[]{:S(2)}) %collective-permute-start.9) | collective-permute-done | bytes 86048 | tf_op jit(solution)/shard_map/ppermute | solution.py:350
  39.5 0.0 collective-permute-start.14
  39.5 0.0 collective-permute-done.10.beside
  39.6 1.2 %collective-permute-done.11.across = bf16[48,896]{1,0:T(8,128)(2,1)S(1)} collective-permute-done((bf16[48,896]{1,0:T(8,128)(2,1)S(1)}, bf16[48,896]{1,0:T(8,128)(2,1)S(1)}, u32[]{:S(2)}, u32[]{:S(2)}) %collective-permute-start.11) | collective-permute-done | bytes 86048 | tf_op jit(solution)/shard_map/ppermute | solution.py:356
  40.8 0.2 sums.2
  41.0 2.5 %collective-permute-start.17 = (bf16[48,896]{1,0:T(8,128)(2,1)S(1)}, bf16[48,896]{1,0:T(8,128)(2,1)S(1)}, u32[]{:S(2)}, u32[]{:S(2)}) collective-permute-start(bf16[48,896]{1,0:T(8,128)(2,1)S(1)} %get-tuple-element.50), channel_id=1, source_target_pairs={{0,12},{2,14},{4,8},{6,10},{8,4},{10,6},{12,0},{14,2},{1,13},{3,15... | collective-permute-start | bytes 258056 | tf_op jit(solution)/shard_map/ppermute | solution.py:347
  43.6 0.5 collective-permute-start.16
  44.1 0.0 collective-permute-done.12.along
  44.1 0.0 collective-permute-done.13.beside
  44.1 0.3 collective-permute-done.14.across
  44.4 0.2 sums.3
  44.6 1.5 %collective-permute-start.15 = (bf16[48,896]{1,0:T(8,128)(2,1)S(1)}, bf16[48,896]{1,0:T(8,128)(2,1)S(1)}, u32[]{:S(2)}, u32[]{:S(2)}) collective-permute-start(bf16[48,896]{1,0:T(8,128)(2,1)S(1)} %get-tuple-element.49), channel_id=1, source_target_pairs={{0,4},{2,6},{4,0},{6,2},{8,12},{10,14},{12,8},{14,10},{1,5},{3,7},... | collective-permute-start | bytes 258056 | tf_op jit(solution)/shard_map/ppermute | solution.py:347
  46.2 2.2 %collective-permute-done.17.refs_3_ = bf16[48,896]{1,0:T(8,128)(2,1)S(1)} collective-permute-done((bf16[48,896]{1,0:T(8,128)(2,1)S(1)}, bf16[48,896]{1,0:T(8,128)(2,1)S(1)}, u32[]{:S(2)}, u32[]{:S(2)}) %collective-permute-start.17) | collective-permute-done | bytes 86048 | tf_op jit(solution)/shard_map/ppermute | solution.py:347
  48.4 4.4 %collective-permute-done.16.refs_2_ = bf16[48,896]{1,0:T(8,128)(2,1)S(1)} collective-permute-done((bf16[48,896]{1,0:T(8,128)(2,1)S(1)}, bf16[48,896]{1,0:T(8,128)(2,1)S(1)}, u32[]{:S(2)}, u32[]{:S(2)}) %collective-permute-start.16) | collective-permute-done | bytes 86048 | tf_op jit(solution)/shard_map/ppermute | solution.py:347
  52.8 0.0 collective-permute-done.15.refs_1_
  52.8 0.9 %combine.1 = bf16[8,7168]{1,0:T(8,128)(2,1)} custom-call(bf16[128,192]{1,0:T(8,128)(2,1)S(1)} %get-tuple-element.34.after.picks_ref, f32[2,8]{1,0:T(2,128)S(1)} %bitcast.11, bf16[48,896]{1,0:T(8,128)(2,1)S(1)} %get-tuple-element.48.refs_0_, bf16[48,896]{1,0:T(8,128)(2,1)S(1)} %collective-permute-done.15.refs_1_, ...), custom_call_target="tpu_custom_call" | custom-call | tf_op jit(solution)/shard_map/combine/pallas_call | solution.py:318
  (7 shorter events, 0.0 us)
Async XLA Ops:
  0.6 19.7 %copy-start.2 = (s32[8,2]{0,1:T(2,128)S(1)}, s32[8,2]{0,1:T(2,128)}, u32[]{:S(2)}) copy-start(s32[8,2]{0,1:T(2,128)} %param.10) | copy-start | bytes 196
  0.6 19.7 %copy-start.4 = (s32[2]{0:T(128)S(1)}, s32[2]{0:T(128)}, u32[]{:S(2)}) copy-start(s32[2]{0:T(128)} %lengths.1) | copy-start | bytes 28
  0.7 19.7 %copy-start = (bf16[2,512,576]{1,2,0:T(8,128)(2,1)S(1)}, bf16[2,512,576]{1,2,0:T(8,128)(2,1)}, u32[]{:S(2)}) copy-start(bf16[2,512,576]{1,2,0:T(8,128)(2,1)} %param.16) | copy-start | bytes 3538948
  0.7 19.7 %copy-start.1 = (bf16[2,128,576]{1,2,0:T(8,128)(2,1)S(1)}, bf16[2,128,576]{1,2,0:T(8,128)(2,1)}, u32[]{:S(2)}) copy-start(bf16[2,128,576]{1,2,0:T(8,128)(2,1)} %param.15) | copy-start | bytes 884740
  2.1 11.0 %collective-permute-start = (bf16[48,896]{1,0:T(8,128)(2,1)S(1)}, bf16[48,896]{1,0:T(8,128)(2,1)S(1)}, u32[]{:S(2)}, u32[]{:S(2)}) collective-permute-start(bf16[48,896]{1,0:T(8,128)(2,1)S(1)} %get-tuple-element.29), channel_id=1, source_target_pairs={{0,4},{2,6},{4,0},{6,2},{8,12},{10,14},{12,8},{14,10},{1,5},{3,7},... | collective-permute-start | bytes 258056 | tf_op jit(solution)/shard_map/ppermute | solution.py:347
  5.2 9.5 %collective-permute-start.1 = (bf16[48,896]{1,0:T(8,128)(2,1)S(1)}, bf16[48,896]{1,0:T(8,128)(2,1)S(1)}, u32[]{:S(2)}, u32[]{:S(2)}) collective-permute-start(bf16[48,896]{1,0:T(8,128)(2,1)S(1)} %get-tuple-element.31), channel_id=1, source_target_pairs={{0,8},{2,10},{4,12},{6,14},{8,0},{10,2},{12,4},{14,6},{1,9},{3,11}... | collective-permute-start | bytes 258056 | tf_op jit(solution)/shard_map/ppermute | solution.py:347
  7.7 6.9 %collective-permute-start.2 = (bf16[48,896]{1,0:T(8,128)(2,1)S(1)}, bf16[48,896]{1,0:T(8,128)(2,1)S(1)}, u32[]{:S(2)}, u32[]{:S(2)}) collective-permute-start(bf16[48,896]{1,0:T(8,128)(2,1)S(1)} %get-tuple-element.32), channel_id=1, source_target_pairs={{0,12},{2,14},{4,8},{6,10},{8,4},{10,6},{12,0},{14,2},{1,13},{3,15... | collective-permute-start | bytes 258056 | tf_op jit(solution)/shard_map/ppermute | solution.py:347
  14.9 4.8 %collective-permute-start.8 = (bf16[48,896]{1,0:T(8,128)(2,1)S(1)}, bf16[48,896]{1,0:T(8,128)(2,1)S(1)}, u32[]{:S(2)}, u32[]{:S(2)}) collective-permute-start(bf16[48,896]{1,0:T(8,128)(2,1)S(1)} %get-tuple-element.36), channel_id=1, source_target_pairs={{0,3},{1,2},{2,1},{3,0},{4,7},{5,6},{6,5},{7,4},{8,11},{9,10},{10,... | collective-permute-start | bytes 258056 | tf_op jit(solution)/shard_map/ppermute | solution.py:356
  14.9 10.2 %collective-permute-start.7 = (bf16[48,896]{1,0:T(8,128)(2,1)S(1)}, bf16[48,896]{1,0:T(8,128)(2,1)S(1)}, u32[]{:S(2)}, u32[]{:S(2)}) collective-permute-start(bf16[48,896]{1,0:T(8,128)(2,1)S(1)} %get-tuple-element.36), channel_id=1, source_target_pairs={{0,2},{2,0},{4,6},{6,4},{8,10},{10,8},{12,14},{14,12},{1,3},{3,1},... | collective-permute-start | bytes 258056 | tf_op jit(solution)/shard_map/ppermute | solution.py:353
  16.5 8.6 %collective-permute-start.6 = (bf16[48,896]{1,0:T(8,128)(2,1)S(1)}, bf16[48,896]{1,0:T(8,128)(2,1)S(1)}, u32[]{:S(2)}, u32[]{:S(2)}) collective-permute-start(bf16[48,896]{1,0:T(8,128)(2,1)S(1)} %get-tuple-element.33.after.refs_4_), channel_id=1, source_target_pairs={{0,1},{1,0},{2,3},{3,2},{4,5},{5,4},{6,7},{7,6},{8,9},{9,8},{10,11... | collective-permute-start | bytes 258056 | tf_op jit(solution)/shard_map/ppermute | solution.py:350
  17.1 8.1 %collective-permute-start.5 = (bf16[48,896]{1,0:T(8,128)(2,1)S(1)}, bf16[48,896]{1,0:T(8,128)(2,1)S(1)}, u32[]{:S(2)}, u32[]{:S(2)}) collective-permute-start(bf16[48,896]{1,0:T(8,128)(2,1)S(1)} %get-tuple-element.35), channel_id=1, source_target_pairs={{0,3},{1,2},{2,1},{3,0},{4,7},{5,6},{6,5},{7,4},{8,11},{9,10},{10,... | collective-permute-start | bytes 258056 | tf_op jit(solution)/shard_map/ppermute | solution.py:356
  17.9 7.3 %collective-permute-start.4 = (bf16[48,896]{1,0:T(8,128)(2,1)S(1)}, bf16[48,896]{1,0:T(8,128)(2,1)S(1)}, u32[]{:S(2)}, u32[]{:S(2)}) collective-permute-start(bf16[48,896]{1,0:T(8,128)(2,1)S(1)} %get-tuple-element.35), channel_id=1, source_target_pairs={{0,2},{2,0},{4,6},{6,4},{8,10},{10,8},{12,14},{14,12},{1,3},{3,1},... | collective-permute-start | bytes 258056 | tf_op jit(solution)/shard_map/ppermute | solution.py:353
  19.7 5.6 %collective-permute-start.3 = (bf16[48,896]{1,0:T(8,128)(2,1)S(1)}, bf16[48,896]{1,0:T(8,128)(2,1)S(1)}, u32[]{:S(2)}, u32[]{:S(2)}) collective-permute-start(bf16[48,896]{1,0:T(8,128)(2,1)S(1)} %get-tuple-element.30.after.refs_0_), channel_id=1, source_target_pairs={{0,1},{1,0},{2,3},{3,2},{4,5},{5,4},{6,7},{7,6},{8,9},{9,8},{10,11... | collective-permute-start | bytes 258056 | tf_op jit(solution)/shard_map/ppermute | solution.py:350
  25.3 27.5 %copy-start.3 = (f32[8,2]{0,1:T(2,128)S(1)}, f32[8,2]{0,1:T(2,128)}, u32[]{:S(2)}) copy-start(f32[8,2]{0,1:T(2,128)} %param.11) | copy-start | bytes 196
  34.8 4.8 %collective-permute-start.9 = (bf16[48,896]{1,0:T(8,128)(2,1)S(1)}, bf16[48,896]{1,0:T(8,128)(2,1)S(1)}, u32[]{:S(2)}, u32[]{:S(2)}) collective-permute-start(bf16[48,896]{1,0:T(8,128)(2,1)S(1)} %get-tuple-element.40), channel_id=1, source_target_pairs={{0,1},{1,0},{2,3},{3,2},{4,5},{5,4},{6,7},{7,6},{8,9},{9,8},{10,11... | collective-permute-start | bytes 258056 | tf_op jit(solution)/shard_map/ppermute | solution.py:350
  36.2 3.4 %collective-permute-start.10 = (bf16[48,896]{1,0:T(8,128)(2,1)S(1)}, bf16[48,896]{1,0:T(8,128)(2,1)S(1)}, u32[]{:S(2)}, u32[]{:S(2)}) collective-permute-start(bf16[48,896]{1,0:T(8,128)(2,1)S(1)} %get-tuple-element.41), channel_id=1, source_target_pairs={{0,2},{2,0},{4,6},{6,4},{8,10},{10,8},{12,14},{14,12},{1,3},{3,1},... | collective-permute-start | bytes 258056 | tf_op jit(solution)/shard_map/ppermute | solution.py:353
  36.2 4.6 %collective-permute-start.11 = (bf16[48,896]{1,0:T(8,128)(2,1)S(1)}, bf16[48,896]{1,0:T(8,128)(2,1)S(1)}, u32[]{:S(2)}, u32[]{:S(2)}) collective-permute-start(bf16[48,896]{1,0:T(8,128)(2,1)S(1)} %get-tuple-element.42), channel_id=1, source_target_pairs={{0,3},{1,2},{2,1},{3,0},{4,7},{5,6},{6,5},{7,4},{8,11},{9,10},{10,... | collective-permute-start | bytes 258056 | tf_op jit(solution)/shard_map/ppermute | solution.py:356
  37.0 7.1 %collective-permute-start.12 = (bf16[48,896]{1,0:T(8,128)(2,1)S(1)}, bf16[48,896]{1,0:T(8,128)(2,1)S(1)}, u32[]{:S(2)}, u32[]{:S(2)}) collective-permute-start(bf16[48,896]{1,0:T(8,128)(2,1)S(1)} %get-tuple-element.45), channel_id=1, source_target_pairs={{0,1},{1,0},{2,3},{3,2},{4,5},{5,4},{6,7},{7,6},{8,9},{9,8},{10,11... | collective-permute-start | bytes 258056 | tf_op jit(solution)/shard_map/ppermute | solution.py:350
  38.3 5.8 %collective-permute-start.13 = (bf16[48,896]{1,0:T(8,128)(2,1)S(1)}, bf16[48,896]{1,0:T(8,128)(2,1)S(1)}, u32[]{:S(2)}, u32[]{:S(2)}) collective-permute-start(bf16[48,896]{1,0:T(8,128)(2,1)S(1)} %get-tuple-element.46), channel_id=1, source_target_pairs={{0,2},{2,0},{4,6},{6,4},{8,10},{10,8},{12,14},{14,12},{1,3},{3,1},... | collective-permute-start | bytes 258056 | tf_op jit(solution)/shard_map/ppermute | solution.py:353
  39.5 4.8 %collective-permute-start.14 = (bf16[48,896]{1,0:T(8,128)(2,1)S(1)}, bf16[48,896]{1,0:T(8,128)(2,1)S(1)}, u32[]{:S(2)}, u32[]{:S(2)}) collective-permute-start(bf16[48,896]{1,0:T(8,128)(2,1)S(1)} %get-tuple-element.47), channel_id=1, source_target_pairs={{0,3},{1,2},{2,1},{3,0},{4,7},{5,6},{6,5},{7,4},{8,11},{9,10},{10,... | collective-permute-start | bytes 258056 | tf_op jit(solution)/shard_map/ppermute | solution.py:356
  41.0 7.4 %collective-permute-start.17 = (bf16[48,896]{1,0:T(8,128)(2,1)S(1)}, bf16[48,896]{1,0:T(8,128)(2,1)S(1)}, u32[]{:S(2)}, u32[]{:S(2)}) collective-permute-start(bf16[48,896]{1,0:T(8,128)(2,1)S(1)} %get-tuple-element.50), channel_id=1, source_target_pairs={{0,12},{2,14},{4,8},{6,10},{8,4},{10,6},{12,0},{14,2},{1,13},{3,15... | collective-permute-start | bytes 258056 | tf_op jit(solution)/shard_map/ppermute | solution.py:347
  43.6 9.2 %collective-permute-start.16 = (bf16[48,896]{1,0:T(8,128)(2,1)S(1)}, bf16[48,896]{1,0:T(8,128)(2,1)S(1)}, u32[]{:S(2)}, u32[]{:S(2)}) collective-permute-start(bf16[48,896]{1,0:T(8,128)(2,1)S(1)} %get-tuple-element.43.after), channel_id=1, source_target_pairs={{0,8},{2,10},{4,12},{6,14},{8,0},{10,2},{12,4},{14,6},{1,9},{3,11}... | collective-permute-start | bytes 258056 | tf_op jit(solution)/shard_map/ppermute | solution.py:347
  44.6 8.1 %collective-permute-start.15 = (bf16[48,896]{1,0:T(8,128)(2,1)S(1)}, bf16[48,896]{1,0:T(8,128)(2,1)S(1)}, u32[]{:S(2)}, u32[]{:S(2)}) collective-permute-start(bf16[48,896]{1,0:T(8,128)(2,1)S(1)} %get-tuple-element.49), channel_id=1, source_target_pairs={{0,4},{2,6},{4,0},{6,2},{8,12},{10,14},{12,8},{14,10},{1,5},{3,7},... | collective-permute-start | bytes 258056 | tf_op jit(solution)/shard_map/ppermute | solution.py:347

commit v4 on v3

--- a/solution.py
+++ b/solution.py
@@ -76,6 +76,7 @@
 
 
 PIECES = 8
+FETCHED = (4, 4)
 
 
 def iota(shape, dim):
@@ -168,51 +169,30 @@
     other[...] = move(match & (from_core != core_index()), rows)
 
 
-def expert_kernel(n_in, held, *refs):
-    ins, (gate_ref, up_ref, up_hbm, down_hbm), refs = refs[:n_in], refs[n_in : n_in + 4], refs[n_in + 4 :]
-    outs, (stack, hidden, up_rest, down_ref, sems) = refs[:n_in], refs[n_in:]
+def expert_kernel(n_in, n_up, *refs):
+    ins, gate_ref, ups, refs = refs[:n_in], refs[n_in], refs[n_in + 1 : n_in + 1 + n_up], refs[n_in + 1 + n_up :]
+    w_down, outs, (stack, hidden) = refs[0], refs[1 : n_in + 1], refs[n_in + 1 :]
     rows, wide = ins[0].shape
     part = rows // PIECES
     total = n_in * part
-    rest = [
-        pltpu.make_async_copy(
-            up_hbm.at[pl.ds(p * wide, wide)],
-            up_rest.at[pl.ds((p - held) * wide, wide)],
-            sems.at[p],
-        )
-        for p in range(held, PIECES)
-    ]
-    down = [
-        pltpu.make_async_copy(
-            down_hbm.at[:, pl.ds(p * wide, wide)],
-            down_ref.at[:, pl.ds(p * wide, wide)],
-            sems.at[PIECES + p],
-        )
-        for p in range(PIECES)
-    ]
-    for copy in rest + down:
-        copy.start()
     shape = (PIECES * total, n_in * rows)
     piece, who, which = split(iota(shape, 0), n_in, part)
     from_who, from_piece, from_which = split(iota(shape, 1), PIECES, part)
     match = (who == from_who) & (which == from_which) & (piece == from_piece)
     stack[...] = move(match, below(ins))
+    blocks = [
+        (ref, slice(p * wide, (p + 1) * wide)) for ref in ups for p in range(ref.shape[0] // wide)
+    ]
     gate = up = 0.0
     for p in range(PIECES):
-        span = slice(p * wide, (p + 1) * wide)
-        gate += dot(stack[p * total : (p + 1) * total], gate_ref[span, :])
-    for p in range(PIECES):
-        if p < held:
-            block = up_ref[p * wide : (p + 1) * wide, :]
-        else:
-            rest[p - held].wait()
-            block = up_rest[(p - held) * wide : (p - held + 1) * wide, :]
-        up += dot(stack[p * total : (p + 1) * total], block)
+        x = stack[p * total : (p + 1) * total]
+        gate += dot(x, gate_ref[p * wide : (p + 1) * wide, :])
+        ref, span = blocks[p]
+        up += dot(x, ref[span, :])
     hidden[...] = (gate / (1.0 + jnp.exp(-gate)) * up).astype(jnp.bfloat16)
     for p in range(PIECES):
-        down[p].wait()
         stack[p * total : (p + 1) * total] = dot(
-            hidden[...], down_ref[:, p * wide : (p + 1) * wide]
+            hidden[...], w_down[:, p * wide : (p + 1) * wide]
         ).astype(jnp.bfloat16)
     shape = (n_in * rows, PIECES * total)
     who, piece, which = split(iota(shape, 0), PIECES, part)
@@ -257,30 +237,35 @@
         out[:, p * wide : (p + 1) * wide] = sum(terms[1:], terms[0]).astype(jnp.bfloat16)
 
 
-def start_copies(src, dst, sems, cuts):
-    rows = dst.shape[0] // cuts
-    spans = [pl.ds(j * rows, rows) for j in range(cuts)]
+def fetch_kernel(start, count, wide, after, weights, got, done, sems):
+    del after
     copies = [
-        pltpu.make_async_copy(src.at[span], dst.at[span], sems.at[j]) for j, span in enumerate(spans)
+        pltpu.make_async_copy(
+            weights.at[pl.ds((start + p) * wide, wide)], got.at[pl.ds(p * wide, wide)], sems.at[p]
+        )
+        for p in range(count)
     ]
     for copy in copies:
         copy.start()
-    return copies
-
-
-def fetch_kernel(cuts, after, w_gate, got_gate, done, sems):
+    done[...] = jnp.zeros_like(done)
+    for copy in copies:
+        copy.wait()
+
+
+def attend_kernel(chips, capacity, after, lengths, ids_hbm, queries_hbm, cache_hbm, *refs):
     del after
-    for copy in start_copies(w_gate, got_gate, sems, cuts):
-        copy.wait()
-    done[...] = jnp.zeros_like(done)
-
-
-def attend_kernel(cuts, latent, chips, capacity, after, lengths, ids_ref, w_up, queries, cache, got_up, out, picks, sems):
-    del after
-    copies = start_copies(w_up, got_up, sems, cuts)
-    top, toks = ids_ref.shape
+    out_hbm, picks, ids_ref, queries, cache, out, sems = refs
     requests, _, heads = queries.shape
     width = cache.shape[2]
+    latent = out.shape[2]
+    inward = [pltpu.make_async_copy(ids_hbm, ids_ref, sems.at[0])]
+    for r in range(requests):
+        inward.append(pltpu.make_async_copy(queries_hbm.at[r], queries.at[r], sems.at[1 + 3 * r]))
+        inward.append(pltpu.make_async_copy(cache_hbm.at[r], cache.at[r], sems.at[2 + 3 * r]))
+    for copy in inward:
+        copy.start()
+    inward[0].wait()
+    top, toks = ids_ref.shape
     rows = picks.shape[1]
     eye = ones(iota((rows, rows), 0) == iota((rows, rows), 1))
     for k in range(top):
@@ -288,7 +273,10 @@
         picks[k * PIECES * toks : (k + 1) * PIECES * toks] = lax.dot_general(
             select, eye, (((0,), (0,)), ((), ())), preferred_element_type=jnp.float32
         ).astype(jnp.bfloat16)
+    outward = []
     for r in range(requests):
+        inward[1 + 2 * r].wait()
+        inward[2 + 2 * r].wait()
         scores = (
             lax.dot_general(
                 queries[r], cache[r], (((0,), (0,)), ((), ())), preferred_element_type=jnp.float32
@@ -304,7 +292,9 @@
             (((1,), (1,)), ((), ())),
             preferred_element_type=jnp.float32,
         ).astype(jnp.bfloat16)
-    for copy in copies:
+        outward.append(pltpu.make_async_copy(out.at[r], out_hbm.at[r], sems.at[3 + 3 * r]))
+        outward[r].start()
+    for copy in outward:
         copy.wait()
 
 
@@ -339,9 +329,10 @@
     far = jax.ShapeDtypeStruct((PIECES * CORES * capacity, wide), bf16)
     near = jax.ShapeDtypeStruct((PIECES * batch * capacity, wide), bf16)
     in_hbm = functools.partial(pltpu.with_memory_space_constraint, memory_space=pltpu.HBM)
-    w_gate, w_up, w_down = in_hbm(w_gate[0]), in_hbm(w_up[0]), in_hbm(w_down[0])
-    units = w_gate.shape[1]
-    ids, gains = expert_ids.T, gate_weights.T
+    got_gate = pltpu.with_memory_space_constraint(w_gate[0], pltpu.VMEM)
+    w_up, got_down = in_hbm(w_up[0]), pltpu.with_memory_space_constraint(w_down[0], pltpu.VMEM)
+    units = w_up.shape[1]
+    ids, gains = in_hbm(expert_ids.T), gate_weights.T
 
     def to_chip(x, d):
         return lax.ppermute(x, "ep", [(i, i ^ (CORES * d)) for i in range(n_ep)])
@@ -359,58 +350,43 @@
         functools.partial(pack_kernel, capacity, chips),
         "pack", (far,) * chips, [HBM] * 2, (VMEM,) * chips,
         [pltpu.VMEM(ids.shape, ids.dtype), pltpu.VMEM(tokens.shape, bf16), DMA((2,))],
-        2 * MIB, (in_hbm(ids), in_hbm(tokens)),
+        2 * MIB, (ids, in_hbm(tokens)),
     )
     landed = [None] * chips
     landed[0] = packed[0]
     for d in (2, 3, 1):
         landed[d] = to_chip(packed[d], d)
-    cuts = 8
-    got_gate, token = call(
-        functools.partial(fetch_kernel, cuts),
-        "fetch", (pltpu.VMEM(w_gate.shape, bf16), jax.ShapeDtypeStruct((8, 128), jnp.float32)),
-        [HBM] * 2, (VMEM, VMEM), [DMA((cuts,))], 1 * MIB, (packed[0], w_gate), moved=2 * w_gate.size,
-    )
-    arrived = []
-    for chosen in batches:
+    arrived, got_up = [], []
+    token, begin = packed[0], 0
+    for chosen, count in zip(batches, FETCHED):
         same, other = call(
             functools.partial(near_kernel, capacity, batch),
             "near", (near,) * 2, [HBM] + [VMEM] * batch, (VMEM,) * 2, [], 1 * MIB,
             (token, *[landed[d] for d in chosen]),
         )
-        token = same
         arrived += [same, along(same), beside(other), across(other)]
-    latent = cache.shape[2] - ROPE
-    held = PIECES // 2
-    picks_shape = (top * PIECES * toks, chips * far.shape[0])
-    got_up, attn_out, picks = call(
-        functools.partial(attend_kernel, held, latent, chips, capacity),
-        "attend",
-        (
-            pltpu.VMEM((held * wide, units), bf16),
-            jax.ShapeDtypeStruct(queries.shape[:2] + (latent,), bf16),
-            jax.ShapeDtypeStruct(picks_shape, bf16),
-        ),
-        [HBM, SMEM, VMEM, HBM, VMEM, VMEM], (VMEM,) * 3, [DMA((held,))], 2 * MIB,
-        (token, lengths, ids, w_up, queries.swapaxes(1, 2), cache.swapaxes(1, 2)),
-        moved=held * wide * units * 2,
-    )
+        fetched, token = call(
+            functools.partial(fetch_kernel, begin, count, wide),
+            "fetch",
+            (pltpu.VMEM((count * wide, units), bf16), jax.ShapeDtypeStruct((8, 128), jnp.float32)),
+            [HBM] * 2, (VMEM, VMEM), [DMA((count,))], 1 * MIB, (same, w_up),
+            moved=2 * count * wide * units,
+        )
+        got_up.append(fetched)
+        begin += count
     n_in = len(arrived)
     rows = n_in * batch * capacity
     parts = call(
-        functools.partial(expert_kernel, n_in, held),
-        "experts", (near,) * n_in, [VMEM] * (n_in + 2) + [HBM] * 2, (VMEM,) * n_in,
+        functools.partial(expert_kernel, n_in, len(got_up)),
+        "experts", (near,) * n_in, [VMEM] * (n_in + 2 + len(got_up)), (VMEM,) * n_in,
         [
             pltpu.VMEM((PIECES * rows, wide), bf16),
             pltpu.VMEM((rows, units), bf16),
-            pltpu.VMEM(((PIECES - held) * wide, units), bf16),
-            pltpu.VMEM(w_down.shape, bf16),
-            DMA((2 * PIECES,)),
         ],
-        28 * MIB, (*arrived, got_gate, got_up, w_up, w_down), flops=6 * rows * width * units,
+        4 * MIB, (*arrived, got_gate, *got_up, got_down), flops=6 * rows * width * units,
     )
     back = [None] * chips
-    token = picks
+    token = parts[0]
     for b in reversed(range(len(batches))):
         own, x, core, diagonal = parts[4 * b : 4 * b + 4]
         sums = call(
@@ -421,6 +397,26 @@
         token = sums[0]
         for d, value in zip(batches[b], sums):
             back[d] = to_chip(value, d) if d else value
+    latent = cache.shape[2] - ROPE
+    queries, cache = in_hbm(queries.swapaxes(1, 2)), in_hbm(cache.swapaxes(1, 2))
+    requests, _, heads = queries.shape
+    attn_out, picks = call(
+        functools.partial(attend_kernel, chips, capacity),
+        "attend",
+        (
+            jax.ShapeDtypeStruct((requests, heads, latent), bf16),
+            jax.ShapeDtypeStruct((top * PIECES * toks, chips * far.shape[0]), bf16),
+        ),
+        [HBM, SMEM] + [HBM] * 3, (HBM, VMEM),
+        [
+            pltpu.VMEM(ids.shape, ids.dtype),
+            pltpu.VMEM(queries.shape, bf16),
+            pltpu.VMEM(cache.shape, bf16),
+            pltpu.VMEM((requests, heads, latent), bf16),
+            DMA((1 + 3 * requests,)),
+        ],
+        6 * MIB, (token, in_hbm(lengths), ids, queries, cache), moved=2 * cache.size,
+    )
     moe_out = call(
         functools.partial(combine_kernel, chips),
         "combine", jax.ShapeDtypeStruct(tokens.shape, bf16), [VMEM] * (2 + chips), VMEM, [],

time: 53.8 us -> 50.6 us (0.941)
  waiting for transfers between devices: 11.9 us -> 6.12 us
  starting transfers between devices: 18.2 us -> 19.5 us
  local copies, waits for them, and re-layouts: 0.02 us -> 1.23 us
    ppermute x6, waiting for transfers between devices: 7.95 us -> 3.65 us  [to_chip(): return lax.ppermute(x, 'ep', [(i, i ^ CORES * d) for i in range(n_ep)])]
    unnamed x10 -> x12, local copies, waits for them, and re-layouts: 0.02 us -> 1.23 us
    ppermute x4, waiting for transfers between devices: 2.6 us -> 1.67 us  [across(): return lax.ppermute(x, ('ep', 'dp'), [(i, i ^ 3) for i in range(2 * n_ep)])]
    ppermute x4, starting transfers between devices: 1.72 us -> 0.85 us  [across(): return lax.ppermute(x, ('ep', 'dp'), [(i, i ^ 3) for i in range(2 * n_ep)])]
    ppermute x6, starting transfers between devices: 10.3 us -> 11.1 us  [to_chip(): return lax.ppermute(x, 'ep', [(i, i ^ CORES * d) for i in range(n_ep)])]
    ppermute x4, starting transfers between devices: 2.38 us -> 3.14 us  [beside(): return lax.ppermute(x, 'ep', [(i, i ^ 1) for i in range(n_ep)])]
    ppermute x4, starting transfers between devices: 3.86 us -> 4.43 us  [along(): return lax.ppermute(x, 'dp', [(0, 1), (1, 0)])]
    ppermute x4, waiting for transfers between devices: 1.35 us -> 0.79 us  [along(): return lax.ppermute(x, 'dp', [(0, 1), (1, 0)])]
  transfers between devices with their start and end apart: 18 -> 18, of which waited for: 8 -> 4; matrix products, arithmetic and copies ran while one was open for 0% -> 0% of each run, Pallas kernels for 20% -> 26%
where the time goes in v4:
time: 50.6 us; the launch traced here: 50.4 us
  Pallas kernels  22.8 us (45%)
  starting transfers between devices  19.5 us (39%)
  waiting for transfers between devices  6.12 us (12%)
  local copies, waits for them, and re-layouts  1.23 us (2%)
  between operations  0.8 us (2%)
    pallas_call x10, Pallas kernels, call(): pl.pallas_call(kernel, name=name, out_shape=out_shape, in_specs=in_specs,...  22.8 us
    ppermute x6, starting transfers between devices, to_chip(): return lax.ppermute(x, 'ep', [(i, i ^ CORES * d) for i in range(n_ep)])  11.1 us
    ppermute x4, starting transfers between devices, along(): return lax.ppermute(x, 'dp', [(0, 1), (1, 0)])  4.43 us
    ppermute x6, waiting for transfers between devices, to_chip(): return lax.ppermute(x, 'ep', [(i, i ^ CORES * d) for i in range(n_ep)])  3.65 us
    ppermute x4, starting transfers between devices, beside(): return lax.ppermute(x, 'ep', [(i, i ^ 1) for i in range(n_ep)])  3.14 us
    ppermute x4, waiting for transfers between devices, across(): return lax.ppermute(x, ('ep', 'dp'), [(i, i ^ 3) for i in range(2 * n_ep)])  1.67 us
    unnamed x12, local copies, waits for them, and re-layouts  1.23 us
  transfers between devices with their start and end apart: 18, of which 4 were waited for; matrix products, arithmetic and copies ran while one was open for 0% of the time, Pallas kernels for 26%

profile of v4, /device:TPU:0, one launch (start us, length us, event | category | flops | bytes accessed | tf_op | source)
XLA Modules:
  0.0 50.4 jit_solution(1322035992666490065)
XLA Ops:
  0.6 1.3 %pack.1 = (bf16[48,896]{1,0:T(8,128)(2,1)S(1)}, bf16[48,896]{1,0:T(8,128)(2,1)S(1)}, bf16[48,896]{1,0:T(8,128)(2,1)S(1)}, bf16[48,896]{1,0:T(8,128)(2,1)S(1)}) custom-call(s32[2,8]{1,0:T(2,128)} %bitcast.16, bf16[8,7168]{1,0:T(8,128)(2,1)} %tok_hbm.1), custom_call_target="tpu_custom_call" | custom-call | tf_op jit(solution)/shard_map/pack/pallas_call | solution.py:308
  1.9 3.1 %collective-permute-start = (bf16[48,896]{1,0:T(8,128)(2,1)S(1)}, bf16[48,896]{1,0:T(8,128)(2,1)S(1)}, u32[]{:S(2)}, u32[]{:S(2)}) collective-permute-start(bf16[48,896]{1,0:T(8,128)(2,1)S(1)} %get-tuple-element.28), channel_id=1, source_target_pairs={{0,4},{2,6},{4,0},{6,2},{8,12},{10,14},{12,8},{14,10},{1,5},{3,7},... | collective-permute-start | bytes 258056 | tf_op jit(solution)/shard_map/ppermute | solution.py:338
  5.0 2.6 %collective-permute-start.4 = (bf16[48,896]{1,0:T(8,128)(2,1)S(1)}, bf16[48,896]{1,0:T(8,128)(2,1)S(1)}, u32[]{:S(2)}, u32[]{:S(2)}) collective-permute-start(bf16[48,896]{1,0:T(8,128)(2,1)S(1)} %get-tuple-element.32), channel_id=1, source_target_pairs={{0,8},{2,10},{4,12},{6,14},{8,0},{10,2},{12,4},{14,6},{1,9},{3,11}... | collective-permute-start | bytes 258056 | tf_op jit(solution)/shard_map/ppermute | solution.py:338
  7.6 0.0 collective-permute-start.5
  7.6 0.0 collective-permute-done.refs_1_
  7.6 0.2 near.2
  7.8 0.4 collective-permute-start.3
  8.2 1.5 %collective-permute-start.2 = (bf16[48,896]{1,0:T(8,128)(2,1)S(1)}, bf16[48,896]{1,0:T(8,128)(2,1)S(1)}, u32[]{:S(2)}, u32[]{:S(2)}) collective-permute-start(bf16[48,896]{1,0:T(8,128)(2,1)S(1)} %get-tuple-element.30), channel_id=1, source_target_pairs={{0,2},{2,0},{4,6},{6,4},{8,10},{10,8},{12,14},{14,12},{1,3},{3,1},... | collective-permute-start | bytes 258056 | tf_op jit(solution)/shard_map/ppermute | solution.py:344
  9.8 0.2 collective-permute-start.1
  10.0 3.3 %fetch.2 = (bf16[3584,1024]{1,0:T(8,128)(2,1)S(1)}, f32[8,128]{1,0:T(8,128)S(1)}) custom-call(bf16[48,896]{1,0:T(8,128)(2,1)S(1)} %get-tuple-element.29.after.refs_0_, bf16[7168,1024]{1,0:T(8,128)(2,1)} %bitcast.12), custom_call_target="tpu_custom_call" | custom-call | bytes 7340032 | tf_op jit(solution)/shard_map/fetch/pallas_call | solution.py:308
  13.4 1.1 %collective-permute-done.4.refs_0_ = bf16[48,896]{1,0:T(8,128)(2,1)S(1)} collective-permute-done((bf16[48,896]{1,0:T(8,128)(2,1)S(1)}, bf16[48,896]{1,0:T(8,128)(2,1)S(1)}, u32[]{:S(2)}, u32[]{:S(2)}) %collective-permute-start.4) | collective-permute-done | bytes 86048 | tf_op jit(solution)/shard_map/ppermute | solution.py:338
  14.5 0.0 collective-permute-done.5.refs_1_
  14.5 0.2 near.3
  14.7 0.1 collective-permute-start.8
  14.8 1.6 %collective-permute-start.7 = (bf16[48,896]{1,0:T(8,128)(2,1)S(1)}, bf16[48,896]{1,0:T(8,128)(2,1)S(1)}, u32[]{:S(2)}, u32[]{:S(2)}) collective-permute-start(bf16[48,896]{1,0:T(8,128)(2,1)S(1)} %get-tuple-element.35), channel_id=1, source_target_pairs={{0,2},{2,0},{4,6},{6,4},{8,10},{10,8},{12,14},{14,12},{1,3},{3,1},... | collective-permute-start | bytes 258056 | tf_op jit(solution)/shard_map/ppermute | solution.py:344
  16.4 0.0 collective-permute-done.3.refs_3_
  16.4 0.5 %collective-permute-start.6 = (bf16[48,896]{1,0:T(8,128)(2,1)S(1)}, bf16[48,896]{1,0:T(8,128)(2,1)S(1)}, u32[]{:S(2)}, u32[]{:S(2)}) collective-permute-start(bf16[48,896]{1,0:T(8,128)(2,1)S(1)} %get-tuple-element.34.after.refs_4_), channel_id=1, source_target_pairs={{0,1},{1,0},{2,3},{3,2},{4,5},{5,4},{6,7},{7,6},{8,9},{9,8},{10,11... | collective-permute-start | bytes 258056 | tf_op jit(solution)/shard_map/ppermute | solution.py:341
  16.9 4.6 %fetch.3 = (bf16[3584,1024]{1,0:T(8,128)(2,1)S(1)}, f32[8,128]{1,0:T(8,128)}) custom-call(bf16[48,896]{1,0:T(8,128)(2,1)S(1)} %get-tuple-element.34.after.refs_4_, bf16[7168,1024]{1,0:T(8,128)(2,1)} %bitcast.13), custom_call_target="tpu_custom_call" | custom-call | bytes 7340032 | tf_op jit(solution)/shard_map/fetch/pallas_call | solution.py:308
  21.5 0.0 collective-permute-done.2.refs_2_
  21.5 0.0 collective-permute-done.1.refs_1_
  21.6 0.0 collective-permute-done.8.refs_7_
  21.6 0.0 collective-permute-done.7.refs_6_
  21.6 0.0 collective-permute-done.6.refs_5_
  21.6 0.4 copy-done
  22.0 0.8 %slice-done.3 = s8[2097152]{0:T(1024)(128)(4,1)S(1)} async-done(((s8[14680064]{0:T(1024)(128)(4,1)}), s8[2097152]{0:T(1024)(128)(4,1)S(1)}, s32[]{:S(2)}) %slice-start.3) | async-done | bytes 2097176
  22.8 7.6 %experts.1 = (bf16[48,896]{1,0:T(8,128)(2,1)S(1)}, bf16[48,896]{1,0:T(8,128)(2,1)S(1)}, bf16[48,896]{1,0:T(8,128)(2,1)S(1)}, bf16[48,896]{1,0:T(8,128)(2,1)S(1)}...) custom-call(bf16[48,896]{1,0:T(8,128)(2,1)S(1)} %get-tuple-element.2, ...), custom_call_target="tpu_custom_call" | custom-call | flops 2113929216 | tf_op jit(solution)/shard_map/experts/pallas_call | solution.py:308
  30.5 1.9 %collective-permute-start.9 = (bf16[48,896]{1,0:T(8,128)(2,1)S(1)}, bf16[48,896]{1,0:T(8,128)(2,1)S(1)}, u32[]{:S(2)}, u32[]{:S(2)}) collective-permute-start(bf16[48,896]{1,0:T(8,128)(2,1)S(1)} %get-tuple-element.40), channel_id=1, source_target_pairs={{0,1},{1,0},{2,3},{3,2},{4,5},{5,4},{6,7},{7,6},{8,9},{9,8},{10,11... | collective-permute-start | bytes 258056 | tf_op jit(solution)/shard_map/ppermute | solution.py:341
  32.3 0.0 collective-permute-start.10
  32.3 0.3 collective-permute-start.11
  32.7 1.8 %collective-permute-start.12 = (bf16[48,896]{1,0:T(8,128)(2,1)S(1)}, bf16[48,896]{1,0:T(8,128)(2,1)S(1)}, u32[]{:S(2)}, u32[]{:S(2)}) collective-permute-start(bf16[48,896]{1,0:T(8,128)(2,1)S(1)} %get-tuple-element.44), channel_id=1, source_target_pairs={{0,1},{1,0},{2,3},{3,2},{4,5},{5,4},{6,7},{7,6},{8,9},{9,8},{10,11... | collective-permute-start | bytes 258056 | tf_op jit(solution)/shard_map/ppermute | solution.py:341
  34.5 0.0 collective-permute-start.13
  34.5 0.8 %collective-permute-done.9.along = bf16[48,896]{1,0:T(8,128)(2,1)S(1)} collective-permute-done((bf16[48,896]{1,0:T(8,128)(2,1)S(1)}, bf16[48,896]{1,0:T(8,128)(2,1)S(1)}, u32[]{:S(2)}, u32[]{:S(2)}) %collective-permute-start.9) | collective-permute-done | bytes 86048 | tf_op jit(solution)/shard_map/ppermute | solution.py:341
  35.3 0.0 collective-permute-start.14
  35.3 0.0 collective-permute-done.10.beside
  35.3 1.7 %collective-permute-done.11.across = bf16[48,896]{1,0:T(8,128)(2,1)S(1)} collective-permute-done((bf16[48,896]{1,0:T(8,128)(2,1)S(1)}, bf16[48,896]{1,0:T(8,128)(2,1)S(1)}, u32[]{:S(2)}, u32[]{:S(2)}) %collective-permute-start.11) | collective-permute-done | bytes 86048 | tf_op jit(solution)/shard_map/ppermute | solution.py:347
  36.9 0.2 sums.2
  37.2 4.7 %collective-permute-start.17 = (bf16[48,896]{1,0:T(8,128)(2,1)S(1)}, bf16[48,896]{1,0:T(8,128)(2,1)S(1)}, u32[]{:S(2)}, u32[]{:S(2)}) collective-permute-start(bf16[48,896]{1,0:T(8,128)(2,1)S(1)} %get-tuple-element.50), channel_id=1, source_target_pairs={{0,12},{2,14},{4,8},{6,10},{8,4},{10,6},{12,0},{14,2},{1,13},{3,15... | collective-permute-start | bytes 258056 | tf_op jit(solution)/shard_map/ppermute | solution.py:338
  41.8 0.0 collective-permute-start.16
  41.8 0.0 collective-permute-done.12.along
  41.8 0.0 collective-permute-done.13.beside
  41.9 0.0 collective-permute-done.14.across
  41.9 0.2 sums.3
  42.1 0.7 %collective-permute-start.15 = (bf16[48,896]{1,0:T(8,128)(2,1)S(1)}, bf16[48,896]{1,0:T(8,128)(2,1)S(1)}, u32[]{:S(2)}, u32[]{:S(2)}) collective-permute-start(bf16[48,896]{1,0:T(8,128)(2,1)S(1)} %get-tuple-element.49), channel_id=1, source_target_pairs={{0,4},{2,6},{4,0},{6,2},{8,12},{10,14},{12,8},{14,10},{1,5},{3,7},... | collective-permute-start | bytes 258056 | tf_op jit(solution)/shard_map/ppermute | solution.py:338
  42.8 4.2 %attend.1 = (bf16[2,128,512]{2,1,0:T(8,128)(2,1)}, bf16[128,192]{1,0:T(8,128)(2,1)S(1)}) custom-call(bf16[48,896]{1,0:T(8,128)(2,1)S(1)} %get-tuple-element.47.after.refs_0_, s32[2]{0:T(128)} %lengths.1, s32[2,8]{1,0:T(2,128)} %bitcast.17, bf16[2,576,128]{2,1,0:T(8,128)(2,1)} %bitcast.15, bf16[2,576,512]{2,1,0:T(8,128)(2,1)} %bitcast.14), custom_call_target="tpu_custom_call" | custom-call | bytes 1179648 | tf_op jit(solution)/shard_map/attend/pallas_call | solution.py:308
  47.0 0.0 collective-permute-done.17.refs_3_
  47.0 2.5 %collective-permute-done.16.refs_2_ = bf16[48,896]{1,0:T(8,128)(2,1)S(1)} collective-permute-done((bf16[48,896]{1,0:T(8,128)(2,1)S(1)}, bf16[48,896]{1,0:T(8,128)(2,1)S(1)}, u32[]{:S(2)}, u32[]{:S(2)}) %collective-permute-start.16) | collective-permute-done | bytes 86048 | tf_op jit(solution)/shard_map/ppermute | solution.py:338
  49.5 0.0 collective-permute-done.15.refs_1_
  49.5 0.9 %combine.1 = bf16[8,7168]{1,0:T(8,128)(2,1)} custom-call(bf16[128,192]{1,0:T(8,128)(2,1)S(1)} %get-tuple-element.48.picks_ref, f32[2,8]{1,0:T(2,128)S(1)} %bitcast.11, bf16[48,896]{1,0:T(8,128)(2,1)S(1)} %get-tuple-element.47.after.refs_0_, bf16[48,896]{1,0:T(8,128)(2,1)S(1)} %collective-permute-done.15.refs_1_, ...), custom_call_target="tpu_custom_call" | custom-call | tf_op jit(solution)/shard_map/combine/pallas_call | solution.py:308
  (11 shorter events, 0.0 us)
Async XLA Ops:
  1.9 5.7 %collective-permute-start = (bf16[48,896]{1,0:T(8,128)(2,1)S(1)}, bf16[48,896]{1,0:T(8,128)(2,1)S(1)}, u32[]{:S(2)}, u32[]{:S(2)}) collective-permute-start(bf16[48,896]{1,0:T(8,128)(2,1)S(1)} %get-tuple-element.28), channel_id=1, source_target_pairs={{0,4},{2,6},{4,0},{6,2},{8,12},{10,14},{12,8},{14,10},{1,5},{3,7},... | collective-permute-start | bytes 258056 | tf_op jit(solution)/shard_map/ppermute | solution.py:338
  5.0 9.5 %collective-permute-start.4 = (bf16[48,896]{1,0:T(8,128)(2,1)S(1)}, bf16[48,896]{1,0:T(8,128)(2,1)S(1)}, u32[]{:S(2)}, u32[]{:S(2)}) collective-permute-start(bf16[48,896]{1,0:T(8,128)(2,1)S(1)} %get-tuple-element.32), channel_id=1, source_target_pairs={{0,8},{2,10},{4,12},{6,14},{8,0},{10,2},{12,4},{14,6},{1,9},{3,11}... | collective-permute-start | bytes 258056 | tf_op jit(solution)/shard_map/ppermute | solution.py:338
  7.6 6.9 %collective-permute-start.5 = (bf16[48,896]{1,0:T(8,128)(2,1)S(1)}, bf16[48,896]{1,0:T(8,128)(2,1)S(1)}, u32[]{:S(2)}, u32[]{:S(2)}) collective-permute-start(bf16[48,896]{1,0:T(8,128)(2,1)S(1)} %get-tuple-element.33), channel_id=1, source_target_pairs={{0,12},{2,14},{4,8},{6,10},{8,4},{10,6},{12,0},{14,2},{1,13},{3,15... | collective-permute-start | bytes 258056 | tf_op jit(solution)/shard_map/ppermute | solution.py:338
  7.6 14.0 %slice-start = ((s8[14680064]{0:T(1024)(128)(4,1)}), s8[4194304]{0:T(1024)(128)(4,1)S(1)}, s32[]{:S(2)}) async-start(s8[14680064]{0:T(1024)(128)(4,1)} %bitcast.7), calls=%async_computation | async-start | bytes 8388608
  7.8 8.6 %collective-permute-start.3 = (bf16[48,896]{1,0:T(8,128)(2,1)S(1)}, bf16[48,896]{1,0:T(8,128)(2,1)S(1)}, u32[]{:S(2)}, u32[]{:S(2)}) collective-permute-start(bf16[48,896]{1,0:T(8,128)(2,1)S(1)} %get-tuple-element.30), channel_id=1, source_target_pairs={{0,3},{1,2},{2,1},{3,0},{4,7},{5,6},{6,5},{7,4},{8,11},{9,10},{10,... | collective-permute-start | bytes 258056 | tf_op jit(solution)/shard_map/ppermute | solution.py:347
  8.2 13.3 %collective-permute-start.2 = (bf16[48,896]{1,0:T(8,128)(2,1)S(1)}, bf16[48,896]{1,0:T(8,128)(2,1)S(1)}, u32[]{:S(2)}, u32[]{:S(2)}) collective-permute-start(bf16[48,896]{1,0:T(8,128)(2,1)S(1)} %get-tuple-element.30), channel_id=1, source_target_pairs={{0,2},{2,0},{4,6},{6,4},{8,10},{10,8},{12,14},{14,12},{1,3},{3,1},... | collective-permute-start | bytes 258056 | tf_op jit(solution)/shard_map/ppermute | solution.py:344
  9.8 11.8 %collective-permute-start.1 = (bf16[48,896]{1,0:T(8,128)(2,1)S(1)}, bf16[48,896]{1,0:T(8,128)(2,1)S(1)}, u32[]{:S(2)}, u32[]{:S(2)}) collective-permute-start(bf16[48,896]{1,0:T(8,128)(2,1)S(1)} %get-tuple-element.29.after.refs_0_), channel_id=1, source_target_pairs={{0,1},{1,0},{2,3},{3,2},{4,5},{5,4},{6,7},{7,6},{8,9},{9,8},{10,11... | collective-permute-start | bytes 258056 | tf_op jit(solution)/shard_map/ppermute | solution.py:341
  10.0 11.6 %slice-start.1 = ((s8[14680064]{0:T(1024)(128)(4,1)}), s8[4194304]{0:T(1024)(128)(4,1)S(1)}, s32[]{:S(2)}) async-start(s8[14680064]{0:T(1024)(128)(4,1)} %bitcast.7), calls=%async_computation.1 | async-start | bytes 8388608
  10.0 11.6 %slice-start.2 = ((s8[14680064]{0:T(1024)(128)(4,1)}), s8[4194304]{0:T(1024)(128)(4,1)S(1)}, s32[]{:S(2)}) async-start(s8[14680064]{0:T(1024)(128)(4,1)} %bitcast.7), calls=%async_computation.2 | async-start | bytes 8388608
  10.0 12.0 %copy-start = (bf16[1,1024,7168]{2,1,0:T(8,128)(2,1)S(1)}, bf16[1,1024,7168]{2,1,0:T(8,128)(2,1)}, u32[]{:S(2)}) copy-start(bf16[1,1024,7168]{2,1,0:T(8,128)(2,1)} %param.14) | copy-start | bytes 44040196
  14.7 6.8 %collective-permute-start.8 = (bf16[48,896]{1,0:T(8,128)(2,1)S(1)}, bf16[48,896]{1,0:T(8,128)(2,1)S(1)}, u32[]{:S(2)}, u32[]{:S(2)}) collective-permute-start(bf16[48,896]{1,0:T(8,128)(2,1)S(1)} %get-tuple-element.35), channel_id=1, source_target_pairs={{0,3},{1,2},{2,1},{3,0},{4,7},{5,6},{6,5},{7,4},{8,11},{9,10},{10,... | collective-permute-start | bytes 258056 | tf_op jit(solution)/shard_map/ppermute | solution.py:347
  14.8 6.8 %collective-permute-start.7 = (bf16[48,896]{1,0:T(8,128)(2,1)S(1)}, bf16[48,896]{1,0:T(8,128)(2,1)S(1)}, u32[]{:S(2)}, u32[]{:S(2)}) collective-permute-start(bf16[48,896]{1,0:T(8,128)(2,1)S(1)} %get-tuple-element.35), channel_id=1, source_target_pairs={{0,2},{2,0},{4,6},{6,4},{8,10},{10,8},{12,14},{14,12},{1,3},{3,1},... | collective-permute-start | bytes 258056 | tf_op jit(solution)/shard_map/ppermute | solution.py:344
  16.4 6.4 %slice-start.3 = ((s8[14680064]{0:T(1024)(128)(4,1)}), s8[2097152]{0:T(1024)(128)(4,1)S(1)}, s32[]{:S(2)}) async-start(s8[14680064]{0:T(1024)(128)(4,1)} %bitcast.7), calls=%async_computation.3 | async-start | bytes 4194304
  16.4 5.2 %collective-permute-start.6 = (bf16[48,896]{1,0:T(8,128)(2,1)S(1)}, bf16[48,896]{1,0:T(8,128)(2,1)S(1)}, u32[]{:S(2)}, u32[]{:S(2)}) collective-permute-start(bf16[48,896]{1,0:T(8,128)(2,1)S(1)} %get-tuple-element.34.after.refs_4_), channel_id=1, source_target_pairs={{0,1},{1,0},{2,3},{3,2},{4,5},{5,4},{6,7},{7,6},{8,9},{9,8},{10,11... | collective-permute-start | bytes 258056 | tf_op jit(solution)/shard_map/ppermute | solution.py:341
  22.8 26.7 %copy-start.1 = (f32[8,2]{0,1:T(2,128)S(1)}, f32[8,2]{0,1:T(2,128)}, u32[]{:S(2)}) copy-start(f32[8,2]{0,1:T(2,128)} %param.11) | copy-start | bytes 196
  30.5 4.8 %collective-permute-start.9 = (bf16[48,896]{1,0:T(8,128)(2,1)S(1)}, bf16[48,896]{1,0:T(8,128)(2,1)S(1)}, u32[]{:S(2)}, u32[]{:S(2)}) collective-permute-start(bf16[48,896]{1,0:T(8,128)(2,1)S(1)} %get-tuple-element.40), channel_id=1, source_target_pairs={{0,1},{1,0},{2,3},{3,2},{4,5},{5,4},{6,7},{7,6},{8,9},{9,8},{10,11... | collective-permute-start | bytes 258056 | tf_op jit(solution)/shard_map/ppermute | solution.py:341
  32.3 2.9 %collective-permute-start.10 = (bf16[48,896]{1,0:T(8,128)(2,1)S(1)}, bf16[48,896]{1,0:T(8,128)(2,1)S(1)}, u32[]{:S(2)}, u32[]{:S(2)}) collective-permute-start(bf16[48,896]{1,0:T(8,128)(2,1)S(1)} %get-tuple-element.41), channel_id=1, source_target_pairs={{0,2},{2,0},{4,6},{6,4},{8,10},{10,8},{12,14},{14,12},{1,3},{3,1},... | collective-permute-start | bytes 258056 | tf_op jit(solution)/shard_map/ppermute | solution.py:344
  32.3 4.6 %collective-permute-start.11 = (bf16[48,896]{1,0:T(8,128)(2,1)S(1)}, bf16[48,896]{1,0:T(8,128)(2,1)S(1)}, u32[]{:S(2)}, u32[]{:S(2)}) collective-permute-start(bf16[48,896]{1,0:T(8,128)(2,1)S(1)} %get-tuple-element.42), channel_id=1, source_target_pairs={{0,3},{1,2},{2,1},{3,0},{4,7},{5,6},{6,5},{7,4},{8,11},{9,10},{10,... | collective-permute-start | bytes 258056 | tf_op jit(solution)/shard_map/ppermute | solution.py:347
  32.7 9.2 %collective-permute-start.12 = (bf16[48,896]{1,0:T(8,128)(2,1)S(1)}, bf16[48,896]{1,0:T(8,128)(2,1)S(1)}, u32[]{:S(2)}, u32[]{:S(2)}) collective-permute-start(bf16[48,896]{1,0:T(8,128)(2,1)S(1)} %get-tuple-element.44), channel_id=1, source_target_pairs={{0,1},{1,0},{2,3},{3,2},{4,5},{5,4},{6,7},{7,6},{8,9},{9,8},{10,11... | collective-permute-start | bytes 258056 | tf_op jit(solution)/shard_map/ppermute | solution.py:341
  34.5 7.4 %collective-permute-start.13 = (bf16[48,896]{1,0:T(8,128)(2,1)S(1)}, bf16[48,896]{1,0:T(8,128)(2,1)S(1)}, u32[]{:S(2)}, u32[]{:S(2)}) collective-permute-start(bf16[48,896]{1,0:T(8,128)(2,1)S(1)} %get-tuple-element.45), channel_id=1, source_target_pairs={{0,2},{2,0},{4,6},{6,4},{8,10},{10,8},{12,14},{14,12},{1,3},{3,1},... | collective-permute-start | bytes 258056 | tf_op jit(solution)/shard_map/ppermute | solution.py:344
  35.3 6.6 %collective-permute-start.14 = (bf16[48,896]{1,0:T(8,128)(2,1)S(1)}, bf16[48,896]{1,0:T(8,128)(2,1)S(1)}, u32[]{:S(2)}, u32[]{:S(2)}) collective-permute-start(bf16[48,896]{1,0:T(8,128)(2,1)S(1)} %get-tuple-element.46), channel_id=1, source_target_pairs={{0,3},{1,2},{2,1},{3,0},{4,7},{5,6},{6,5},{7,4},{8,11},{9,10},{10,... | collective-permute-start | bytes 258056 | tf_op jit(solution)/shard_map/ppermute | solution.py:347
  37.2 9.8 %collective-permute-start.17 = (bf16[48,896]{1,0:T(8,128)(2,1)S(1)}, bf16[48,896]{1,0:T(8,128)(2,1)S(1)}, u32[]{:S(2)}, u32[]{:S(2)}) collective-permute-start(bf16[48,896]{1,0:T(8,128)(2,1)S(1)} %get-tuple-element.50), channel_id=1, source_target_pairs={{0,12},{2,14},{4,8},{6,10},{8,4},{10,6},{12,0},{14,2},{1,13},{3,15... | collective-permute-start | bytes 258056 | tf_op jit(solution)/shard_map/ppermute | solution.py:338
  41.8 7.7 %collective-permute-start.16 = (bf16[48,896]{1,0:T(8,128)(2,1)S(1)}, bf16[48,896]{1,0:T(8,128)(2,1)S(1)}, u32[]{:S(2)}, u32[]{:S(2)}) collective-permute-start(bf16[48,896]{1,0:T(8,128)(2,1)S(1)} %get-tuple-element.43.after), channel_id=1, source_target_pairs={{0,8},{2,10},{4,12},{6,14},{8,0},{10,2},{12,4},{14,6},{1,9},{3,11}... | collective-permute-start | bytes 258056 | tf_op jit(solution)/shard_map/ppermute | solution.py:338
  42.1 7.4 %collective-permute-start.15 = (bf16[48,896]{1,0:T(8,128)(2,1)S(1)}, bf16[48,896]{1,0:T(8,128)(2,1)S(1)}, u32[]{:S(2)}, u32[]{:S(2)}) collective-permute-start(bf16[48,896]{1,0:T(8,128)(2,1)S(1)} %get-tuple-element.49), channel_id=1, source_target_pairs={{0,4},{2,6},{4,0},{6,2},{8,12},{10,14},{12,8},{14,10},{1,5},{3,7},... | collective-permute-start | bytes 258056 | tf_op jit(solution)/shard_map/ppermute | solution.py:338

commit v5 on v4

--- a/solution.py
+++ b/solution.py
@@ -76,7 +76,7 @@
 
 
 PIECES = 8
-FETCHED = (4, 4)
+FETCHED = (2, 1, 5)
 
 
 def iota(shape, dim):
@@ -357,23 +357,31 @@
     for d in (2, 3, 1):
         landed[d] = to_chip(packed[d], d)
     arrived, got_up = [], []
-    token, begin = packed[0], 0
-    for chosen, count in zip(batches, FETCHED):
+    begin = 0
+
+    def fetch(count, after):
+        nonlocal begin
+        fetched, token = call(
+            functools.partial(fetch_kernel, begin, count, wide),
+            "fetch",
+            (pltpu.VMEM((count * wide, units), bf16), jax.ShapeDtypeStruct((8, 128), jnp.float32)),
+            [HBM] * 2, (VMEM, VMEM), [DMA((count,))], 1 * MIB, (after, w_up),
+            moved=2 * count * wide * units,
+        )
+        got_up.append(fetched)
+        begin += count
+        return token
+
+    token = fetch(FETCHED[0], packed[0])
+    for chosen, count in zip(batches, FETCHED[1:]):
         same, other = call(
             functools.partial(near_kernel, capacity, batch),
             "near", (near,) * 2, [HBM] + [VMEM] * batch, (VMEM,) * 2, [], 1 * MIB,
             (token, *[landed[d] for d in chosen]),
         )
-        arrived += [same, along(same), beside(other), across(other)]
-        fetched, token = call(
-            functools.partial(fetch_kernel, begin, count, wide),
-            "fetch",
-            (pltpu.VMEM((count * wide, units), bf16), jax.ShapeDtypeStruct((8, 128), jnp.float32)),
-            [HBM] * 2, (VMEM, VMEM), [DMA((count,))], 1 * MIB, (same, w_up),
-            moved=2 * count * wide * units,
-        )
-        got_up.append(fetched)
-        begin += count
+        core, x, diagonal = beside(other), along(same), across(other)
+        arrived += [same, x, core, diagonal]
+        token = fetch(count, same)
     n_in = len(arrived)
     rows = n_in * batch * capacity
     parts = call(
@@ -389,10 +397,14 @@
     token = parts[0]
     for b in reversed(range(len(batches))):
         own, x, core, diagonal = parts[4 * b : 4 * b + 4]
+        if b:
+            x, diagonal, core = along(x), across(diagonal), beside(core)
+        else:
+            core, x, diagonal = beside(core), along(x), across(diagonal)
         sums = call(
             functools.partial(sum_kernel, capacity, batch),
             "sums", (far,) * batch, [HBM] + [VMEM] * 4, (VMEM,) * batch, [], 1 * MIB,
-            (token, own, along(x), beside(core), across(diagonal)),
+            (token, own, x, core, diagonal),
         )
         token = sums[0]
         for d, value in zip(batches[b], sums):

time: 50.6 us -> 48.5 us (0.958)
  waiting for transfers between devices: 6.12 us -> 4.57 us
  Pallas kernels: 22.8 us -> 23.8 us
  local copies, waits for them, and re-layouts: 1.23 us -> 0.25 us
  starting transfers between devices: 19.5 us -> 18.8 us
    ppermute x6, waiting for transfers between devices: 3.65 us -> 2.08 us  [to_chip(): return lax.ppermute(x, 'ep', [(i, i ^ CORES * d) for i in range(n_ep)])]
    pallas_call x10 -> x11, Pallas kernels: 22.8 us -> 23.8 us  [call(): pl.pallas_call(kernel, name=name, out_shape=out_shape, in_specs=in_specs,...]
    unnamed x12 -> x18, local copies, waits for them, and re-layouts: 1.23 us -> 0.25 us
    ppermute x4, starting transfers between devices: 3.14 us -> 2.23 us  [beside(): return lax.ppermute(x, 'ep', [(i, i ^ 1) for i in range(n_ep)])]
    ppermute x4, starting transfers between devices: 0.85 us -> 1.74 us  [across(): return lax.ppermute(x, ('ep', 'dp'), [(i, i ^ 3) for i in range(2 * n_ep)])]
    ppermute x6, starting transfers between devices: 11.1 us -> 10.2 us  [to_chip(): return lax.ppermute(x, 'ep', [(i, i ^ CORES * d) for i in range(n_ep)])]
  transfers between devices with their start and end apart: 18 -> 18, of which waited for: 4 -> 3; matrix products, arithmetic and copies ran while one was open for 0% -> 0% of each run, Pallas kernels for 26% -> 29%
where the time goes in v5:
time: 48.5 us; the launch traced here: 48.3 us
  Pallas kernels  23.8 us (49%)
  starting transfers between devices  18.8 us (39%)
  waiting for transfers between devices  4.57 us (9%)
  between operations  0.85 us (2%)
    pallas_call x11, Pallas kernels, call(): pl.pallas_call(kernel, name=name, out_shape=out_shape, in_specs=in_specs,...  23.8 us
    ppermute x6, starting transfers between devices, to_chip(): return lax.ppermute(x, 'ep', [(i, i ^ CORES * d) for i in range(n_ep)])  10.2 us
    ppermute x4, starting transfers between devices, along(): return lax.ppermute(x, 'dp', [(0, 1), (1, 0)])  4.67 us
    ppermute x4, starting transfers between devices, beside(): return lax.ppermute(x, 'ep', [(i, i ^ 1) for i in range(n_ep)])  2.23 us
    ppermute x6, waiting for transfers between devices, to_chip(): return lax.ppermute(x, 'ep', [(i, i ^ CORES * d) for i in range(n_ep)])  2.08 us
    ppermute x4, starting transfers between devices, across(): return lax.ppermute(x, ('ep', 'dp'), [(i, i ^ 3) for i in range(2 * n_ep)])  1.74 us
    ppermute x4, waiting for transfers between devices, across(): return lax.ppermute(x, ('ep', 'dp'), [(i, i ^ 3) for i in range(2 * n_ep)])  1.67 us
  transfers between devices with their start and end apart: 18, of which 3 were waited for; matrix products, arithmetic and copies ran while one was open for 0% of the time, Pallas kernels for 29%

profile of v5, /device:TPU:0, one launch (start us, length us, event | category | flops | bytes accessed | tf_op | source)
XLA Modules:
  0.0 48.3 jit_solution(4572990749561310713)
XLA Ops:
  0.6 1.3 %pack.1 = (bf16[48,896]{1,0:T(8,128)(2,1)S(1)}, bf16[48,896]{1,0:T(8,128)(2,1)S(1)}, bf16[48,896]{1,0:T(8,128)(2,1)S(1)}, bf16[48,896]{1,0:T(8,128)(2,1)S(1)}) custom-call(s32[2,8]{1,0:T(2,128)} %bitcast.19, bf16[8,7168]{1,0:T(8,128)(2,1)} %tok_hbm.1), custom_call_target="tpu_custom_call" | custom-call | tf_op jit(solution)/shard_map/pack/pallas_call | solution.py:308
  1.9 3.1 %collective-permute-start = (bf16[48,896]{1,0:T(8,128)(2,1)S(1)}, bf16[48,896]{1,0:T(8,128)(2,1)S(1)}, u32[]{:S(2)}, u32[]{:S(2)}) collective-permute-start(bf16[48,896]{1,0:T(8,128)(2,1)S(1)} %get-tuple-element.31), channel_id=1, source_target_pairs={{0,4},{2,6},{4,0},{6,2},{8,12},{10,14},{12,8},{14,10},{1,5},{3,7},... | collective-permute-start | bytes 258056 | tf_op jit(solution)/shard_map/ppermute | solution.py:338
  5.0 2.6 %collective-permute-start.4 = (bf16[48,896]{1,0:T(8,128)(2,1)S(1)}, bf16[48,896]{1,0:T(8,128)(2,1)S(1)}, u32[]{:S(2)}, u32[]{:S(2)}) collective-permute-start(bf16[48,896]{1,0:T(8,128)(2,1)S(1)} %get-tuple-element.35), channel_id=1, source_target_pairs={{0,8},{2,10},{4,12},{6,14},{8,0},{10,2},{12,4},{14,6},{1,9},{3,11}... | collective-permute-start | bytes 258056 | tf_op jit(solution)/shard_map/ppermute | solution.py:338
  7.6 0.0 collective-permute-start.5
  7.6 0.0 slice-start.5
  7.6 2.2 %fetch.3 = (bf16[1792,1024]{1,0:T(8,128)(2,1)S(1)}, f32[8,128]{1,0:T(8,128)S(1)}) custom-call(bf16[48,896]{1,0:T(8,128)(2,1)S(1)} %get-tuple-element.29.after.refs_0_, bf16[7168,1024]{1,0:T(8,128)(2,1)} %bitcast.14), custom_call_target="tpu_custom_call" | custom-call | bytes 3670016 | tf_op jit(solution)/shard_map/fetch/pallas_call | solution.py:308
  9.9 0.0 collective-permute-done.refs_1_
  9.9 0.2 near.2
  10.1 0.4 collective-permute-start.3
  10.5 1.4 %collective-permute-start.2 = (bf16[48,896]{1,0:T(8,128)(2,1)S(1)}, bf16[48,896]{1,0:T(8,128)(2,1)S(1)}, u32[]{:S(2)}, u32[]{:S(2)}) collective-permute-start(bf16[48,896]{1,0:T(8,128)(2,1)S(1)} %get-tuple-element.33), channel_id=1, source_target_pairs={{0,2},{2,0},{4,6},{6,4},{8,10},{10,8},{12,14},{14,12},{1,3},{3,1},... | collective-permute-start | bytes 258056 | tf_op jit(solution)/shard_map/ppermute | solution.py:344
  12.0 0.3 collective-permute-start.1
  12.3 2.3 %fetch.4 = (bf16[896,1024]{1,0:T(8,128)(2,1)S(1)}, f32[8,128]{1,0:T(8,128)S(1)}) custom-call(bf16[48,896]{1,0:T(8,128)(2,1)S(1)} %get-tuple-element.32.after.refs_0_, bf16[7168,1024]{1,0:T(8,128)(2,1)} %bitcast.15), custom_call_target="tpu_custom_call" | custom-call | bytes 1835008 | tf_op jit(solution)/shard_map/fetch/pallas_call | solution.py:308
  14.6 0.0 collective-permute-done.4.refs_0_
  14.6 0.0 collective-permute-done.5.refs_1_
  14.6 0.2 near.3
  14.8 1.1 %collective-permute-start.8 = (bf16[48,896]{1,0:T(8,128)(2,1)S(1)}, bf16[48,896]{1,0:T(8,128)(2,1)S(1)}, u32[]{:S(2)}, u32[]{:S(2)}) collective-permute-start(bf16[48,896]{1,0:T(8,128)(2,1)S(1)} %get-tuple-element.38), channel_id=1, source_target_pairs={{0,3},{1,2},{2,1},{3,0},{4,7},{5,6},{6,5},{7,4},{8,11},{9,10},{10,... | collective-permute-start | bytes 258056 | tf_op jit(solution)/shard_map/ppermute | solution.py:347
  15.9 0.8 %collective-permute-start.7 = (bf16[48,896]{1,0:T(8,128)(2,1)S(1)}, bf16[48,896]{1,0:T(8,128)(2,1)S(1)}, u32[]{:S(2)}, u32[]{:S(2)}) collective-permute-start(bf16[48,896]{1,0:T(8,128)(2,1)S(1)} %get-tuple-element.38), channel_id=1, source_target_pairs={{0,2},{2,0},{4,6},{6,4},{8,10},{10,8},{12,14},{14,12},{1,3},{3,1},... | collective-permute-start | bytes 258056 | tf_op jit(solution)/shard_map/ppermute | solution.py:344
  16.7 0.0 collective-permute-done.3.refs_3_
  16.7 0.3 collective-permute-start.6
  17.0 4.4 %fetch.5 = (bf16[4480,1024]{1,0:T(8,128)(2,1)S(1)}, f32[8,128]{1,0:T(8,128)}) custom-call(bf16[48,896]{1,0:T(8,128)(2,1)S(1)} %get-tuple-element.37.after.refs_4_, bf16[7168,1024]{1,0:T(8,128)(2,1)} %bitcast.16), custom_call_target="tpu_custom_call" | custom-call | bytes 9175040 | tf_op jit(solution)/shard_map/fetch/pallas_call | solution.py:308
  21.5 0.0 collective-permute-done.2.refs_2_
  21.5 0.0 collective-permute-done.1.refs_1_
  21.5 0.0 collective-permute-done.8.refs_7_
  21.5 0.0 collective-permute-done.7.refs_6_
  21.5 0.0 collective-permute-done.6.refs_5_
  21.6 0.2 slice-done.7
  21.8 7.6 %experts.1 = (bf16[48,896]{1,0:T(8,128)(2,1)S(1)}, bf16[48,896]{1,0:T(8,128)(2,1)S(1)}, bf16[48,896]{1,0:T(8,128)(2,1)S(1)}, bf16[48,896]{1,0:T(8,128)(2,1)S(1)}...) custom-call(bf16[48,896]{1,0:T(8,128)(2,1)S(1)} %get-tuple-element.3, ...), custom_call_target="tpu_custom_call" | custom-call | flops 2113929216 | tf_op jit(solution)/shard_map/experts/pallas_call | solution.py:308
  29.5 2.1 %collective-permute-start.9 = (bf16[48,896]{1,0:T(8,128)(2,1)S(1)}, bf16[48,896]{1,0:T(8,128)(2,1)S(1)}, u32[]{:S(2)}, u32[]{:S(2)}) collective-permute-start(bf16[48,896]{1,0:T(8,128)(2,1)S(1)} %get-tuple-element.44), channel_id=1, source_target_pairs={{0,1},{1,0},{2,3},{3,2},{4,5},{5,4},{6,7},{7,6},{8,9},{9,8},{10,11... | collective-permute-start | bytes 258056 | tf_op jit(solution)/shard_map/ppermute | solution.py:341
  31.5 0.0 collective-permute-start.10
  31.5 0.2 collective-permute-start.11
  31.7 1.9 %collective-permute-start.12 = (bf16[48,896]{1,0:T(8,128)(2,1)S(1)}, bf16[48,896]{1,0:T(8,128)(2,1)S(1)}, u32[]{:S(2)}, u32[]{:S(2)}) collective-permute-start(bf16[48,896]{1,0:T(8,128)(2,1)S(1)} %get-tuple-element.48), channel_id=1, source_target_pairs={{0,1},{1,0},{2,3},{3,2},{4,5},{5,4},{6,7},{7,6},{8,9},{9,8},{10,11... | collective-permute-start | bytes 258056 | tf_op jit(solution)/shard_map/ppermute | solution.py:341
  33.7 0.0 collective-permute-start.13
  33.7 0.8 %collective-permute-done.9.along = bf16[48,896]{1,0:T(8,128)(2,1)S(1)} collective-permute-done((bf16[48,896]{1,0:T(8,128)(2,1)S(1)}, bf16[48,896]{1,0:T(8,128)(2,1)S(1)}, u32[]{:S(2)}, u32[]{:S(2)}) %collective-permute-start.9) | collective-permute-done | bytes 86048 | tf_op jit(solution)/shard_map/ppermute | solution.py:341
  34.5 0.0 collective-permute-start.14
  34.5 0.0 collective-permute-done.10.beside
  34.5 1.7 %collective-permute-done.11.across = bf16[48,896]{1,0:T(8,128)(2,1)S(1)} collective-permute-done((bf16[48,896]{1,0:T(8,128)(2,1)S(1)}, bf16[48,896]{1,0:T(8,128)(2,1)S(1)}, u32[]{:S(2)}, u32[]{:S(2)}) %collective-permute-start.11) | collective-permute-done | bytes 86048 | tf_op jit(solution)/shard_map/ppermute | solution.py:347
  36.1 0.2 sums.2
  36.4 3.7 %collective-permute-start.17 = (bf16[48,896]{1,0:T(8,128)(2,1)S(1)}, bf16[48,896]{1,0:T(8,128)(2,1)S(1)}, u32[]{:S(2)}, u32[]{:S(2)}) collective-permute-start(bf16[48,896]{1,0:T(8,128)(2,1)S(1)} %get-tuple-element.54), channel_id=1, source_target_pairs={{0,12},{2,14},{4,8},{6,10},{8,4},{10,6},{12,0},{14,2},{1,13},{3,15... | collective-permute-start | bytes 258056 | tf_op jit(solution)/shard_map/ppermute | solution.py:338
  40.0 0.0 collective-permute-start.16
  40.0 0.0 collective-permute-done.12.along
  40.1 0.0 collective-permute-done.13.beside
  40.1 0.0 collective-permute-done.14.across
  40.1 0.2 sums.3
  40.3 0.8 %collective-permute-start.15 = (bf16[48,896]{1,0:T(8,128)(2,1)S(1)}, bf16[48,896]{1,0:T(8,128)(2,1)S(1)}, u32[]{:S(2)}, u32[]{:S(2)}) collective-permute-start(bf16[48,896]{1,0:T(8,128)(2,1)S(1)} %get-tuple-element.53), channel_id=1, source_target_pairs={{0,4},{2,6},{4,0},{6,2},{8,12},{10,14},{12,8},{14,10},{1,5},{3,7},... | collective-permute-start | bytes 258056 | tf_op jit(solution)/shard_map/ppermute | solution.py:338
  41.2 4.2 %attend.1 = (bf16[2,128,512]{2,1,0:T(8,128)(2,1)}, bf16[128,192]{1,0:T(8,128)(2,1)S(1)}) custom-call(bf16[48,896]{1,0:T(8,128)(2,1)S(1)} %get-tuple-element.51.after.refs_0_, s32[2]{0:T(128)} %lengths.1, s32[2,8]{1,0:T(2,128)} %bitcast.20, bf16[2,576,128]{2,1,0:T(8,128)(2,1)} %bitcast.18, bf16[2,576,512]{2,1,0:T(8,128)(2,1)} %bitcast.17), custom_call_target="tpu_custom_call" | custom-call | bytes 1179648 | tf_op jit(solution)/shard_map/attend/pallas_call | solution.py:308
  45.3 2.1 %collective-permute-done.16.refs_2_ = bf16[48,896]{1,0:T(8,128)(2,1)S(1)} collective-permute-done((bf16[48,896]{1,0:T(8,128)(2,1)S(1)}, bf16[48,896]{1,0:T(8,128)(2,1)S(1)}, u32[]{:S(2)}, u32[]{:S(2)}) %collective-permute-start.16) | collective-permute-done | bytes 86048 | tf_op jit(solution)/shard_map/ppermute | solution.py:338
  47.4 0.0 collective-permute-done.15.refs_1_
  47.4 0.9 %combine.1 = bf16[8,7168]{1,0:T(8,128)(2,1)} custom-call(bf16[128,192]{1,0:T(8,128)(2,1)S(1)} %get-tuple-element.52.picks_ref, f32[2,8]{1,0:T(2,128)S(1)} %bitcast.13, bf16[48,896]{1,0:T(8,128)(2,1)S(1)} %get-tuple-element.51.after.refs_0_, bf16[48,896]{1,0:T(8,128)(2,1)S(1)} %collective-permute-done.15.refs_1_, ...), custom_call_target="tpu_custom_call" | custom-call | tf_op jit(solution)/shard_map/combine/pallas_call | solution.py:308
  (19 shorter events, 0.0 us)
Async XLA Ops:
  1.9 7.9 %collective-permute-start = (bf16[48,896]{1,0:T(8,128)(2,1)S(1)}, bf16[48,896]{1,0:T(8,128)(2,1)S(1)}, u32[]{:S(2)}, u32[]{:S(2)}) collective-permute-start(bf16[48,896]{1,0:T(8,128)(2,1)S(1)} %get-tuple-element.31), channel_id=1, source_target_pairs={{0,4},{2,6},{4,0},{6,2},{8,12},{10,14},{12,8},{14,10},{1,5},{3,7},... | collective-permute-start | bytes 258056 | tf_op jit(solution)/shard_map/ppermute | solution.py:338
  5.0 9.6 %collective-permute-start.4 = (bf16[48,896]{1,0:T(8,128)(2,1)S(1)}, bf16[48,896]{1,0:T(8,128)(2,1)S(1)}, u32[]{:S(2)}, u32[]{:S(2)}) collective-permute-start(bf16[48,896]{1,0:T(8,128)(2,1)S(1)} %get-tuple-element.35), channel_id=1, source_target_pairs={{0,8},{2,10},{4,12},{6,14},{8,0},{10,2},{12,4},{14,6},{1,9},{3,11}... | collective-permute-start | bytes 258056 | tf_op jit(solution)/shard_map/ppermute | solution.py:338
  7.6 7.0 %collective-permute-start.5 = (bf16[48,896]{1,0:T(8,128)(2,1)S(1)}, bf16[48,896]{1,0:T(8,128)(2,1)S(1)}, u32[]{:S(2)}, u32[]{:S(2)}) collective-permute-start(bf16[48,896]{1,0:T(8,128)(2,1)S(1)} %get-tuple-element.36), channel_id=1, source_target_pairs={{0,12},{2,14},{4,8},{6,10},{8,4},{10,6},{12,0},{14,2},{1,13},{3,15... | collective-permute-start | bytes 258056 | tf_op jit(solution)/shard_map/ppermute | solution.py:338
  7.6 14.0 %slice-start = ((s8[14680064]{0:T(1024)(128)(4,1)}), s8[4194304]{0:T(1024)(128)(4,1)S(1)}, s32[]{:S(2)}) async-start(s8[14680064]{0:T(1024)(128)(4,1)} %bitcast.7), calls=%async_computation | async-start | bytes 8388608
  7.6 14.0 %slice-start.1 = ((s8[14680064]{0:T(1024)(128)(4,1)}), s8[4194304]{0:T(1024)(128)(4,1)S(1)}, s32[]{:S(2)}) async-start(s8[14680064]{0:T(1024)(128)(4,1)} %bitcast.7), calls=%async_computation.1 | async-start | bytes 8388608
  7.6 14.0 %slice-start.4 = ((s8[14680064]{0:T(1024)(128)(4,1)}), s8[4194304]{0:T(1024)(128)(4,1)S(1)}, s32[]{:S(2)}) async-start(s8[14680064]{0:T(1024)(128)(4,1)} %bitcast.10), calls=%async_computation.4 | async-start | bytes 8388608
  7.6 14.0 %slice-start.5 = ((s8[14680064]{0:T(1024)(128)(4,1)}), s8[4194304]{0:T(1024)(128)(4,1)S(1)}, s32[]{:S(2)}) async-start(s8[14680064]{0:T(1024)(128)(4,1)} %bitcast.10), calls=%async_computation.5 | async-start | bytes 8388608
  10.1 6.6 %collective-permute-start.3 = (bf16[48,896]{1,0:T(8,128)(2,1)S(1)}, bf16[48,896]{1,0:T(8,128)(2,1)S(1)}, u32[]{:S(2)}, u32[]{:S(2)}) collective-permute-start(bf16[48,896]{1,0:T(8,128)(2,1)S(1)} %get-tuple-element.33), channel_id=1, source_target_pairs={{0,3},{1,2},{2,1},{3,0},{4,7},{5,6},{6,5},{7,4},{8,11},{9,10},{10,... | collective-permute-start | bytes 258056 | tf_op jit(solution)/shard_map/ppermute | solution.py:347
  10.5 11.0 %collective-permute-start.2 = (bf16[48,896]{1,0:T(8,128)(2,1)S(1)}, bf16[48,896]{1,0:T(8,128)(2,1)S(1)}, u32[]{:S(2)}, u32[]{:S(2)}) collective-permute-start(bf16[48,896]{1,0:T(8,128)(2,1)S(1)} %get-tuple-element.33), channel_id=1, source_target_pairs={{0,2},{2,0},{4,6},{6,4},{8,10},{10,8},{12,14},{14,12},{1,3},{3,1},... | collective-permute-start | bytes 258056 | tf_op jit(solution)/shard_map/ppermute | solution.py:344
  11.9 9.6 %slice-start.2 = ((s8[14680064]{0:T(1024)(128)(4,1)}), s8[4194304]{0:T(1024)(128)(4,1)S(1)}, s32[]{:S(2)}) async-start(s8[14680064]{0:T(1024)(128)(4,1)} %bitcast.7), calls=%async_computation.2 | async-start | bytes 8388608
  11.9 9.7 %slice-start.6 = ((s8[14680064]{0:T(1024)(128)(4,1)}), s8[4194304]{0:T(1024)(128)(4,1)S(1)}, s32[]{:S(2)}) async-start(s8[14680064]{0:T(1024)(128)(4,1)} %bitcast.10), calls=%async_computation.6 | async-start | bytes 8388608
  12.0 9.6 %collective-permute-start.1 = (bf16[48,896]{1,0:T(8,128)(2,1)S(1)}, bf16[48,896]{1,0:T(8,128)(2,1)S(1)}, u32[]{:S(2)}, u32[]{:S(2)}) collective-permute-start(bf16[48,896]{1,0:T(8,128)(2,1)S(1)} %get-tuple-element.32.after.refs_0_), channel_id=1, source_target_pairs={{0,1},{1,0},{2,3},{3,2},{4,5},{5,4},{6,7},{7,6},{8,9},{9,8},{10,11... | collective-permute-start | bytes 258056 | tf_op jit(solution)/shard_map/ppermute | solution.py:341
  14.8 6.7 %collective-permute-start.8 = (bf16[48,896]{1,0:T(8,128)(2,1)S(1)}, bf16[48,896]{1,0:T(8,128)(2,1)S(1)}, u32[]{:S(2)}, u32[]{:S(2)}) collective-permute-start(bf16[48,896]{1,0:T(8,128)(2,1)S(1)} %get-tuple-element.38), channel_id=1, source_target_pairs={{0,3},{1,2},{2,1},{3,0},{4,7},{5,6},{6,5},{7,4},{8,11},{9,10},{10,... | collective-permute-start | bytes 258056 | tf_op jit(solution)/shard_map/ppermute | solution.py:347
  15.9 5.6 %collective-permute-start.7 = (bf16[48,896]{1,0:T(8,128)(2,1)S(1)}, bf16[48,896]{1,0:T(8,128)(2,1)S(1)}, u32[]{:S(2)}, u32[]{:S(2)}) collective-permute-start(bf16[48,896]{1,0:T(8,128)(2,1)S(1)} %get-tuple-element.38), channel_id=1, source_target_pairs={{0,2},{2,0},{4,6},{6,4},{8,10},{10,8},{12,14},{14,12},{1,3},{3,1},... | collective-permute-start | bytes 258056 | tf_op jit(solution)/shard_map/ppermute | solution.py:344
  16.7 4.9 %slice-start.3 = ((s8[14680064]{0:T(1024)(128)(4,1)}), s8[2097152]{0:T(1024)(128)(4,1)S(1)}, s32[]{:S(2)}) async-start(s8[14680064]{0:T(1024)(128)(4,1)} %bitcast.7), calls=%async_computation.3 | async-start | bytes 4194304
  16.7 5.1 %slice-start.7 = ((s8[14680064]{0:T(1024)(128)(4,1)}), s8[2097152]{0:T(1024)(128)(4,1)S(1)}, s32[]{:S(2)}) async-start(s8[14680064]{0:T(1024)(128)(4,1)} %bitcast.10), calls=%async_computation.7 | async-start | bytes 4194304
  16.7 4.9 %collective-permute-start.6 = (bf16[48,896]{1,0:T(8,128)(2,1)S(1)}, bf16[48,896]{1,0:T(8,128)(2,1)S(1)}, u32[]{:S(2)}, u32[]{:S(2)}) collective-permute-start(bf16[48,896]{1,0:T(8,128)(2,1)S(1)} %get-tuple-element.37.after.refs_4_), channel_id=1, source_target_pairs={{0,1},{1,0},{2,3},{3,2},{4,5},{5,4},{6,7},{7,6},{8,9},{9,8},{10,11... | collective-permute-start | bytes 258056 | tf_op jit(solution)/shard_map/ppermute | solution.py:341
  21.8 25.6 %copy-start = (f32[8,2]{0,1:T(2,128)S(1)}, f32[8,2]{0,1:T(2,128)}, u32[]{:S(2)}) copy-start(f32[8,2]{0,1:T(2,128)} %param.11) | copy-start | bytes 196
  29.5 5.0 %collective-permute-start.9 = (bf16[48,896]{1,0:T(8,128)(2,1)S(1)}, bf16[48,896]{1,0:T(8,128)(2,1)S(1)}, u32[]{:S(2)}, u32[]{:S(2)}) collective-permute-start(bf16[48,896]{1,0:T(8,128)(2,1)S(1)} %get-tuple-element.44), channel_id=1, source_target_pairs={{0,1},{1,0},{2,3},{3,2},{4,5},{5,4},{6,7},{7,6},{8,9},{9,8},{10,11... | collective-permute-start | bytes 258056 | tf_op jit(solution)/shard_map/ppermute | solution.py:341
  31.5 2.9 %collective-permute-start.10 = (bf16[48,896]{1,0:T(8,128)(2,1)S(1)}, bf16[48,896]{1,0:T(8,128)(2,1)S(1)}, u32[]{:S(2)}, u32[]{:S(2)}) collective-permute-start(bf16[48,896]{1,0:T(8,128)(2,1)S(1)} %get-tuple-element.45), channel_id=1, source_target_pairs={{0,2},{2,0},{4,6},{6,4},{8,10},{10,8},{12,14},{14,12},{1,3},{3,1},... | collective-permute-start | bytes 258056 | tf_op jit(solution)/shard_map/ppermute | solution.py:344
  31.5 4.6 %collective-permute-start.11 = (bf16[48,896]{1,0:T(8,128)(2,1)S(1)}, bf16[48,896]{1,0:T(8,128)(2,1)S(1)}, u32[]{:S(2)}, u32[]{:S(2)}) collective-permute-start(bf16[48,896]{1,0:T(8,128)(2,1)S(1)} %get-tuple-element.46), channel_id=1, source_target_pairs={{0,3},{1,2},{2,1},{3,0},{4,7},{5,6},{6,5},{7,4},{8,11},{9,10},{10,... | collective-permute-start | bytes 258056 | tf_op jit(solution)/shard_map/ppermute | solution.py:347
  31.7 8.3 %collective-permute-start.12 = (bf16[48,896]{1,0:T(8,128)(2,1)S(1)}, bf16[48,896]{1,0:T(8,128)(2,1)S(1)}, u32[]{:S(2)}, u32[]{:S(2)}) collective-permute-start(bf16[48,896]{1,0:T(8,128)(2,1)S(1)} %get-tuple-element.48), channel_id=1, source_target_pairs={{0,1},{1,0},{2,3},{3,2},{4,5},{5,4},{6,7},{7,6},{8,9},{9,8},{10,11... | collective-permute-start | bytes 258056 | tf_op jit(solution)/shard_map/ppermute | solution.py:341
  33.7 6.4 %collective-permute-start.13 = (bf16[48,896]{1,0:T(8,128)(2,1)S(1)}, bf16[48,896]{1,0:T(8,128)(2,1)S(1)}, u32[]{:S(2)}, u32[]{:S(2)}) collective-permute-start(bf16[48,896]{1,0:T(8,128)(2,1)S(1)} %get-tuple-element.49), channel_id=1, source_target_pairs={{0,2},{2,0},{4,6},{6,4},{8,10},{10,8},{12,14},{14,12},{1,3},{3,1},... | collective-permute-start | bytes 258056 | tf_op jit(solution)/shard_map/ppermute | solution.py:344
  34.5 5.6 %collective-permute-start.14 = (bf16[48,896]{1,0:T(8,128)(2,1)S(1)}, bf16[48,896]{1,0:T(8,128)(2,1)S(1)}, u32[]{:S(2)}, u32[]{:S(2)}) collective-permute-start(bf16[48,896]{1,0:T(8,128)(2,1)S(1)} %get-tuple-element.50), channel_id=1, source_target_pairs={{0,3},{1,2},{2,1},{3,0},{4,7},{5,6},{6,5},{7,4},{8,11},{9,10},{10,... | collective-permute-start | bytes 258056 | tf_op jit(solution)/shard_map/ppermute | solution.py:347
  36.4 9.0 %collective-permute-start.17 = (bf16[48,896]{1,0:T(8,128)(2,1)S(1)}, bf16[48,896]{1,0:T(8,128)(2,1)S(1)}, u32[]{:S(2)}, u32[]{:S(2)}) collective-permute-start(bf16[48,896]{1,0:T(8,128)(2,1)S(1)} %get-tuple-element.54), channel_id=1, source_target_pairs={{0,12},{2,14},{4,8},{6,10},{8,4},{10,6},{12,0},{14,2},{1,13},{3,15... | collective-permute-start | bytes 258056 | tf_op jit(solution)/shard_map/ppermute | solution.py:338
  40.0 7.4 %collective-permute-start.16 = (bf16[48,896]{1,0:T(8,128)(2,1)S(1)}, bf16[48,896]{1,0:T(8,128)(2,1)S(1)}, u32[]{:S(2)}, u32[]{:S(2)}) collective-permute-start(bf16[48,896]{1,0:T(8,128)(2,1)S(1)} %get-tuple-element.47.after), channel_id=1, source_target_pairs={{0,8},{2,10},{4,12},{6,14},{8,0},{10,2},{12,4},{14,6},{1,9},{3,11}... | collective-permute-start | bytes 258056 | tf_op jit(solution)/shard_map/ppermute | solution.py:338
  40.3 7.1 %collective-permute-start.15 = (bf16[48,896]{1,0:T(8,128)(2,1)S(1)}, bf16[48,896]{1,0:T(8,128)(2,1)S(1)}, u32[]{:S(2)}, u32[]{:S(2)}) collective-permute-start(bf16[48,896]{1,0:T(8,128)(2,1)S(1)} %get-tuple-element.53), channel_id=1, source_target_pairs={{0,4},{2,6},{4,0},{6,2},{8,12},{10,14},{12,8},{14,10},{1,5},{3,7},... | collective-permute-start | bytes 258056 | tf_op jit(solution)/shard_map/ppermute | solution.py:338

commit v6 on v5

--- a/solution.py
+++ b/solution.py
@@ -203,7 +203,7 @@
         out[...] = back[s * rows : (s + 1) * rows]
 
 
-def sum_kernel(capacity, batch, after, own, along, beside, across, *outs):
+def sum_kernel(capacity, batch, after, own, across, along, beside, *outs):
     del after
     f32 = jnp.float32
     same = own[...].astype(f32) + along[...].astype(f32)
@@ -404,7 +404,7 @@
         sums = call(
             functools.partial(sum_kernel, capacity, batch),
             "sums", (far,) * batch, [HBM] + [VMEM] * 4, (VMEM,) * batch, [], 1 * MIB,
-            (token, own, x, core, diagonal),
+            (token, own, diagonal, x, core),
         )
         token = sums[0]
         for d, value in zip(batches[b], sums):

time: 48.5 us -> 48.3 us (level)
  waiting for transfers between devices: 4.57 us -> 3.8 us
  starting transfers between devices: 18.8 us -> 19.4 us
    ppermute x4, starting transfers between devices: 1.74 us -> 4 us  [across(): return lax.ppermute(x, ('ep', 'dp'), [(i, i ^ 3) for i in range(2 * n_ep)])]
    ppermute x4, starting transfers between devices: 4.67 us -> 2.45 us  [along(): return lax.ppermute(x, 'dp', [(0, 1), (1, 0)])]
    ppermute x4, waiting for transfers between devices: 1.67 us -> 0.1 us  [across(): return lax.ppermute(x, ('ep', 'dp'), [(i, i ^ 3) for i in range(2 * n_ep)])]
    ppermute x4, waiting for transfers between devices: 0.81 us -> 2.05 us  [along(): return lax.ppermute(x, 'dp', [(0, 1), (1, 0)])]
where the time goes in v6:
time: 48.3 us; the launch traced here: 48.1 us
  Pallas kernels  23.8 us (49%)
  starting transfers between devices  19.4 us (40%)
  waiting for transfers between devices  3.8 us (8%)
  between operations  0.85 us (2%)
    pallas_call x11, Pallas kernels, call(): pl.pallas_call(kernel, name=name, out_shape=out_shape, in_specs=in_specs,...  23.8 us
    ppermute x6, starting transfers between devices, to_chip(): return lax.ppermute(x, 'ep', [(i, i ^ CORES * d) for i in range(n_ep)])  10.3 us
    ppermute x4, starting transfers between devices, across(): return lax.ppermute(x, ('ep', 'dp'), [(i, i ^ 3) for i in range(2 * n_ep)])  4 us
    ppermute x4, starting transfers between devices, beside(): return lax.ppermute(x, 'ep', [(i, i ^ 1) for i in range(n_ep)])  2.68 us
    ppermute x4, starting transfers between devices, along(): return lax.ppermute(x, 'dp', [(0, 1), (1, 0)])  2.45 us
    ppermute x4, waiting for transfers between devices, along(): return lax.ppermute(x, 'dp', [(0, 1), (1, 0)])  2.05 us
    ppermute x6, waiting for transfers between devices, to_chip(): return lax.ppermute(x, 'ep', [(i, i ^ CORES * d) for i in range(n_ep)])  1.64 us
  transfers between devices with their start and end apart: 18, of which 3 were waited for; matrix products, arithmetic and copies ran while one was open for 0% of the time, Pallas kernels for 29%

profile of v6, /device:TPU:0, one launch (start us, length us, event | category | flops | bytes accessed | tf_op | source)
XLA Modules:
  0.0 48.1 jit_solution(11146351284395904869)
XLA Ops:
  0.6 1.3 %pack.1 = (bf16[48,896]{1,0:T(8,128)(2,1)S(1)}, bf16[48,896]{1,0:T(8,128)(2,1)S(1)}, bf16[48,896]{1,0:T(8,128)(2,1)S(1)}, bf16[48,896]{1,0:T(8,128)(2,1)S(1)}) custom-call(s32[2,8]{1,0:T(2,128)} %bitcast.19, bf16[8,7168]{1,0:T(8,128)(2,1)} %tok_hbm.1), custom_call_target="tpu_custom_call" | custom-call | tf_op jit(solution)/shard_map/pack/pallas_call | solution.py:308
  1.9 3.1 %collective-permute-start = (bf16[48,896]{1,0:T(8,128)(2,1)S(1)}, bf16[48,896]{1,0:T(8,128)(2,1)S(1)}, u32[]{:S(2)}, u32[]{:S(2)}) collective-permute-start(bf16[48,896]{1,0:T(8,128)(2,1)S(1)} %get-tuple-element.31), channel_id=1, source_target_pairs={{0,4},{2,6},{4,0},{6,2},{8,12},{10,14},{12,8},{14,10},{1,5},{3,7},... | collective-permute-start | bytes 258056 | tf_op jit(solution)/shard_map/ppermute | solution.py:338
  5.0 2.6 %collective-permute-start.4 = (bf16[48,896]{1,0:T(8,128)(2,1)S(1)}, bf16[48,896]{1,0:T(8,128)(2,1)S(1)}, u32[]{:S(2)}, u32[]{:S(2)}) collective-permute-start(bf16[48,896]{1,0:T(8,128)(2,1)S(1)} %get-tuple-element.35), channel_id=1, source_target_pairs={{0,8},{2,10},{4,12},{6,14},{8,0},{10,2},{12,4},{14,6},{1,9},{3,11}... | collective-permute-start | bytes 258056 | tf_op jit(solution)/shard_map/ppermute | solution.py:338
  7.6 0.0 collective-permute-start.5
  7.6 0.0 slice-start.5
  7.6 2.2 %fetch.3 = (bf16[1792,1024]{1,0:T(8,128)(2,1)S(1)}, f32[8,128]{1,0:T(8,128)S(1)}) custom-call(bf16[48,896]{1,0:T(8,128)(2,1)S(1)} %get-tuple-element.29.after.refs_0_, bf16[7168,1024]{1,0:T(8,128)(2,1)} %bitcast.14), custom_call_target="tpu_custom_call" | custom-call | bytes 3670016 | tf_op jit(solution)/shard_map/fetch/pallas_call | solution.py:308
  9.9 0.0 collective-permute-done.refs_1_
  9.9 0.2 near.2
  10.1 0.4 collective-permute-start.3
  10.5 1.4 %collective-permute-start.2 = (bf16[48,896]{1,0:T(8,128)(2,1)S(1)}, bf16[48,896]{1,0:T(8,128)(2,1)S(1)}, u32[]{:S(2)}, u32[]{:S(2)}) collective-permute-start(bf16[48,896]{1,0:T(8,128)(2,1)S(1)} %get-tuple-element.33), channel_id=1, source_target_pairs={{0,2},{2,0},{4,6},{6,4},{8,10},{10,8},{12,14},{14,12},{1,3},{3,1},... | collective-permute-start | bytes 258056 | tf_op jit(solution)/shard_map/ppermute | solution.py:344
  12.0 0.3 collective-permute-start.1
  12.3 2.3 %fetch.4 = (bf16[896,1024]{1,0:T(8,128)(2,1)S(1)}, f32[8,128]{1,0:T(8,128)S(1)}) custom-call(bf16[48,896]{1,0:T(8,128)(2,1)S(1)} %get-tuple-element.32.after.refs_0_, bf16[7168,1024]{1,0:T(8,128)(2,1)} %bitcast.15), custom_call_target="tpu_custom_call" | custom-call | bytes 1835008 | tf_op jit(solution)/shard_map/fetch/pallas_call | solution.py:308
  14.6 0.0 collective-permute-done.4.refs_0_
  14.6 0.0 collective-permute-done.5.refs_1_
  14.6 0.2 near.3
  14.8 1.1 %collective-permute-start.8 = (bf16[48,896]{1,0:T(8,128)(2,1)S(1)}, bf16[48,896]{1,0:T(8,128)(2,1)S(1)}, u32[]{:S(2)}, u32[]{:S(2)}) collective-permute-start(bf16[48,896]{1,0:T(8,128)(2,1)S(1)} %get-tuple-element.38), channel_id=1, source_target_pairs={{0,3},{1,2},{2,1},{3,0},{4,7},{5,6},{6,5},{7,4},{8,11},{9,10},{10,... | collective-permute-start | bytes 258056 | tf_op jit(solution)/shard_map/ppermute | solution.py:347
  15.9 0.8 %collective-permute-start.7 = (bf16[48,896]{1,0:T(8,128)(2,1)S(1)}, bf16[48,896]{1,0:T(8,128)(2,1)S(1)}, u32[]{:S(2)}, u32[]{:S(2)}) collective-permute-start(bf16[48,896]{1,0:T(8,128)(2,1)S(1)} %get-tuple-element.38), channel_id=1, source_target_pairs={{0,2},{2,0},{4,6},{6,4},{8,10},{10,8},{12,14},{14,12},{1,3},{3,1},... | collective-permute-start | bytes 258056 | tf_op jit(solution)/shard_map/ppermute | solution.py:344
  16.7 0.0 collective-permute-done.3.refs_3_
  16.7 0.3 collective-permute-start.6
  17.0 4.4 %fetch.5 = (bf16[4480,1024]{1,0:T(8,128)(2,1)S(1)}, f32[8,128]{1,0:T(8,128)}) custom-call(bf16[48,896]{1,0:T(8,128)(2,1)S(1)} %get-tuple-element.37.after.refs_4_, bf16[7168,1024]{1,0:T(8,128)(2,1)} %bitcast.16), custom_call_target="tpu_custom_call" | custom-call | bytes 9175040 | tf_op jit(solution)/shard_map/fetch/pallas_call | solution.py:308
  21.5 0.0 collective-permute-done.2.refs_2_
  21.5 0.0 collective-permute-done.1.refs_1_
  21.5 0.0 collective-permute-done.8.refs_7_
  21.5 0.0 collective-permute-done.7.refs_6_
  21.5 0.0 collective-permute-done.6.refs_5_
  21.6 0.2 slice-done.7
  21.8 7.6 %experts.1 = (bf16[48,896]{1,0:T(8,128)(2,1)S(1)}, bf16[48,896]{1,0:T(8,128)(2,1)S(1)}, bf16[48,896]{1,0:T(8,128)(2,1)S(1)}, bf16[48,896]{1,0:T(8,128)(2,1)S(1)}...) custom-call(bf16[48,896]{1,0:T(8,128)(2,1)S(1)} %get-tuple-element.3, ...), custom_call_target="tpu_custom_call" | custom-call | flops 2113929216 | tf_op jit(solution)/shard_map/experts/pallas_call | solution.py:308
  29.5 1.1 %collective-permute-start.9 = (bf16[48,896]{1,0:T(8,128)(2,1)S(1)}, bf16[48,896]{1,0:T(8,128)(2,1)S(1)}, u32[]{:S(2)}, u32[]{:S(2)}) collective-permute-start(bf16[48,896]{1,0:T(8,128)(2,1)S(1)} %get-tuple-element.44), channel_id=1, source_target_pairs={{0,3},{1,2},{2,1},{3,0},{4,7},{5,6},{6,5},{7,4},{8,11},{9,10},{10,... | collective-permute-start | bytes 258056 | tf_op jit(solution)/shard_map/ppermute | solution.py:347
  30.6 1.0 %collective-permute-start.10 = (bf16[48,896]{1,0:T(8,128)(2,1)S(1)}, bf16[48,896]{1,0:T(8,128)(2,1)S(1)}, u32[]{:S(2)}, u32[]{:S(2)}) collective-permute-start(bf16[48,896]{1,0:T(8,128)(2,1)S(1)} %get-tuple-element.45), channel_id=1, source_target_pairs={{0,1},{1,0},{2,3},{3,2},{4,5},{5,4},{6,7},{7,6},{8,9},{9,8},{10,11... | collective-permute-start | bytes 258056 | tf_op jit(solution)/shard_map/ppermute | solution.py:341
  31.6 0.0 collective-permute-start.11
  31.7 1.4 %collective-permute-start.12 = (bf16[48,896]{1,0:T(8,128)(2,1)S(1)}, bf16[48,896]{1,0:T(8,128)(2,1)S(1)}, u32[]{:S(2)}, u32[]{:S(2)}) collective-permute-start(bf16[48,896]{1,0:T(8,128)(2,1)S(1)} %get-tuple-element.48), channel_id=1, source_target_pairs={{0,3},{1,2},{2,1},{3,0},{4,7},{5,6},{6,5},{7,4},{8,11},{9,10},{10,... | collective-permute-start | bytes 258056 | tf_op jit(solution)/shard_map/ppermute | solution.py:347
  33.0 0.8 %collective-permute-start.13 = (bf16[48,896]{1,0:T(8,128)(2,1)S(1)}, bf16[48,896]{1,0:T(8,128)(2,1)S(1)}, u32[]{:S(2)}, u32[]{:S(2)}) collective-permute-start(bf16[48,896]{1,0:T(8,128)(2,1)S(1)} %get-tuple-element.49), channel_id=1, source_target_pairs={{0,1},{1,0},{2,3},{3,2},{4,5},{5,4},{6,7},{7,6},{8,9},{9,8},{10,11... | collective-permute-start | bytes 258056 | tf_op jit(solution)/shard_map/ppermute | solution.py:341
  33.8 0.1 collective-permute-done.9.across
  33.9 0.4 collective-permute-start.14
  34.3 2.0 %collective-permute-done.10.along = bf16[48,896]{1,0:T(8,128)(2,1)S(1)} collective-permute-done((bf16[48,896]{1,0:T(8,128)(2,1)S(1)}, bf16[48,896]{1,0:T(8,128)(2,1)S(1)}, u32[]{:S(2)}, u32[]{:S(2)}) %collective-permute-start.10) | collective-permute-done | bytes 86048 | tf_op jit(solution)/shard_map/ppermute | solution.py:341
  36.3 0.0 collective-permute-done.11.beside
  36.3 0.2 sums.2
  36.5 3.9 %collective-permute-start.17 = (bf16[48,896]{1,0:T(8,128)(2,1)S(1)}, bf16[48,896]{1,0:T(8,128)(2,1)S(1)}, u32[]{:S(2)}, u32[]{:S(2)}) collective-permute-start(bf16[48,896]{1,0:T(8,128)(2,1)S(1)} %get-tuple-element.54), channel_id=1, source_target_pairs={{0,12},{2,14},{4,8},{6,10},{8,4},{10,6},{12,0},{14,2},{1,13},{3,15... | collective-permute-start | bytes 258056 | tf_op jit(solution)/shard_map/ppermute | solution.py:338
  40.4 0.0 collective-permute-start.16
  40.4 0.0 collective-permute-done.12.across
  40.4 0.0 collective-permute-done.13.along
  40.4 0.0 collective-permute-done.14.beside
  40.4 0.2 sums.3
  40.7 0.7 %collective-permute-start.15 = (bf16[48,896]{1,0:T(8,128)(2,1)S(1)}, bf16[48,896]{1,0:T(8,128)(2,1)S(1)}, u32[]{:S(2)}, u32[]{:S(2)}) collective-permute-start(bf16[48,896]{1,0:T(8,128)(2,1)S(1)} %get-tuple-element.53), channel_id=1, source_target_pairs={{0,4},{2,6},{4,0},{6,2},{8,12},{10,14},{12,8},{14,10},{1,5},{3,7},... | collective-permute-start | bytes 258056 | tf_op jit(solution)/shard_map/ppermute | solution.py:338
  41.4 4.2 %attend.1 = (bf16[2,128,512]{2,1,0:T(8,128)(2,1)}, bf16[128,192]{1,0:T(8,128)(2,1)S(1)}) custom-call(bf16[48,896]{1,0:T(8,128)(2,1)S(1)} %get-tuple-element.51.after.refs_0_, s32[2]{0:T(128)} %lengths.1, s32[2,8]{1,0:T(2,128)} %bitcast.20, bf16[2,576,128]{2,1,0:T(8,128)(2,1)} %bitcast.18, bf16[2,576,512]{2,1,0:T(8,128)(2,1)} %bitcast.17), custom_call_target="tpu_custom_call" | custom-call | bytes 1179648 | tf_op jit(solution)/shard_map/attend/pallas_call | solution.py:308
  45.6 0.0 collective-permute-done.17.refs_3_
  45.6 1.6 %collective-permute-done.16.refs_2_ = bf16[48,896]{1,0:T(8,128)(2,1)S(1)} collective-permute-done((bf16[48,896]{1,0:T(8,128)(2,1)S(1)}, bf16[48,896]{1,0:T(8,128)(2,1)S(1)}, u32[]{:S(2)}, u32[]{:S(2)}) %collective-permute-start.16) | collective-permute-done | bytes 86048 | tf_op jit(solution)/shard_map/ppermute | solution.py:338
  47.2 0.9 %combine.1 = bf16[8,7168]{1,0:T(8,128)(2,1)} custom-call(bf16[128,192]{1,0:T(8,128)(2,1)S(1)} %get-tuple-element.52.picks_ref, f32[2,8]{1,0:T(2,128)S(1)} %bitcast.13, bf16[48,896]{1,0:T(8,128)(2,1)S(1)} %get-tuple-element.51.after.refs_0_, bf16[48,896]{1,0:T(8,128)(2,1)S(1)} %collective-permute-done.15.refs_1_, ...), custom_call_target="tpu_custom_call" | custom-call | tf_op jit(solution)/shard_map/combine/pallas_call | solution.py:308
  (19 shorter events, 0.0 us)
Async XLA Ops:
  1.9 7.9 %collective-permute-start = (bf16[48,896]{1,0:T(8,128)(2,1)S(1)}, bf16[48,896]{1,0:T(8,128)(2,1)S(1)}, u32[]{:S(2)}, u32[]{:S(2)}) collective-permute-start(bf16[48,896]{1,0:T(8,128)(2,1)S(1)} %get-tuple-element.31), channel_id=1, source_target_pairs={{0,4},{2,6},{4,0},{6,2},{8,12},{10,14},{12,8},{14,10},{1,5},{3,7},... | collective-permute-start | bytes 258056 | tf_op jit(solution)/shard_map/ppermute | solution.py:338
  5.0 9.6 %collective-permute-start.4 = (bf16[48,896]{1,0:T(8,128)(2,1)S(1)}, bf16[48,896]{1,0:T(8,128)(2,1)S(1)}, u32[]{:S(2)}, u32[]{:S(2)}) collective-permute-start(bf16[48,896]{1,0:T(8,128)(2,1)S(1)} %get-tuple-element.35), channel_id=1, source_target_pairs={{0,8},{2,10},{4,12},{6,14},{8,0},{10,2},{12,4},{14,6},{1,9},{3,11}... | collective-permute-start | bytes 258056 | tf_op jit(solution)/shard_map/ppermute | solution.py:338
  7.6 7.0 %collective-permute-start.5 = (bf16[48,896]{1,0:T(8,128)(2,1)S(1)}, bf16[48,896]{1,0:T(8,128)(2,1)S(1)}, u32[]{:S(2)}, u32[]{:S(2)}) collective-permute-start(bf16[48,896]{1,0:T(8,128)(2,1)S(1)} %get-tuple-element.36), channel_id=1, source_target_pairs={{0,12},{2,14},{4,8},{6,10},{8,4},{10,6},{12,0},{14,2},{1,13},{3,15... | collective-permute-start | bytes 258056 | tf_op jit(solution)/shard_map/ppermute | solution.py:338
  7.6 14.0 %slice-start = ((s8[14680064]{0:T(1024)(128)(4,1)}), s8[4194304]{0:T(1024)(128)(4,1)S(1)}, s32[]{:S(2)}) async-start(s8[14680064]{0:T(1024)(128)(4,1)} %bitcast.7), calls=%async_computation | async-start | bytes 8388608
  7.6 14.0 %slice-start.1 = ((s8[14680064]{0:T(1024)(128)(4,1)}), s8[4194304]{0:T(1024)(128)(4,1)S(1)}, s32[]{:S(2)}) async-start(s8[14680064]{0:T(1024)(128)(4,1)} %bitcast.7), calls=%async_computation.1 | async-start | bytes 8388608
  7.6 14.0 %slice-start.4 = ((s8[14680064]{0:T(1024)(128)(4,1)}), s8[4194304]{0:T(1024)(128)(4,1)S(1)}, s32[]{:S(2)}) async-start(s8[14680064]{0:T(1024)(128)(4,1)} %bitcast.10), calls=%async_computation.4 | async-start | bytes 8388608
  7.6 14.0 %slice-start.5 = ((s8[14680064]{0:T(1024)(128)(4,1)}), s8[4194304]{0:T(1024)(128)(4,1)S(1)}, s32[]{:S(2)}) async-start(s8[14680064]{0:T(1024)(128)(4,1)} %bitcast.10), calls=%async_computation.5 | async-start | bytes 8388608
  10.1 6.6 %collective-permute-start.3 = (bf16[48,896]{1,0:T(8,128)(2,1)S(1)}, bf16[48,896]{1,0:T(8,128)(2,1)S(1)}, u32[]{:S(2)}, u32[]{:S(2)}) collective-permute-start(bf16[48,896]{1,0:T(8,128)(2,1)S(1)} %get-tuple-element.33), channel_id=1, source_target_pairs={{0,3},{1,2},{2,1},{3,0},{4,7},{5,6},{6,5},{7,4},{8,11},{9,10},{10,... | collective-permute-start | bytes 258056 | tf_op jit(solution)/shard_map/ppermute | solution.py:347
  10.5 11.0 %collective-permute-start.2 = (bf16[48,896]{1,0:T(8,128)(2,1)S(1)}, bf16[48,896]{1,0:T(8,128)(2,1)S(1)}, u32[]{:S(2)}, u32[]{:S(2)}) collective-permute-start(bf16[48,896]{1,0:T(8,128)(2,1)S(1)} %get-tuple-element.33), channel_id=1, source_target_pairs={{0,2},{2,0},{4,6},{6,4},{8,10},{10,8},{12,14},{14,12},{1,3},{3,1},... | collective-permute-start | bytes 258056 | tf_op jit(solution)/shard_map/ppermute | solution.py:344
  11.9 9.6 %slice-start.2 = ((s8[14680064]{0:T(1024)(128)(4,1)}), s8[4194304]{0:T(1024)(128)(4,1)S(1)}, s32[]{:S(2)}) async-start(s8[14680064]{0:T(1024)(128)(4,1)} %bitcast.7), calls=%async_computation.2 | async-start | bytes 8388608
  11.9 9.7 %slice-start.6 = ((s8[14680064]{0:T(1024)(128)(4,1)}), s8[4194304]{0:T(1024)(128)(4,1)S(1)}, s32[]{:S(2)}) async-start(s8[14680064]{0:T(1024)(128)(4,1)} %bitcast.10), calls=%async_computation.6 | async-start | bytes 8388608
  12.0 9.6 %collective-permute-start.1 = (bf16[48,896]{1,0:T(8,128)(2,1)S(1)}, bf16[48,896]{1,0:T(8,128)(2,1)S(1)}, u32[]{:S(2)}, u32[]{:S(2)}) collective-permute-start(bf16[48,896]{1,0:T(8,128)(2,1)S(1)} %get-tuple-element.32.after.refs_0_), channel_id=1, source_target_pairs={{0,1},{1,0},{2,3},{3,2},{4,5},{5,4},{6,7},{7,6},{8,9},{9,8},{10,11... | collective-permute-start | bytes 258056 | tf_op jit(solution)/shard_map/ppermute | solution.py:341
  14.8 6.7 %collective-permute-start.8 = (bf16[48,896]{1,0:T(8,128)(2,1)S(1)}, bf16[48,896]{1,0:T(8,128)(2,1)S(1)}, u32[]{:S(2)}, u32[]{:S(2)}) collective-permute-start(bf16[48,896]{1,0:T(8,128)(2,1)S(1)} %get-tuple-element.38), channel_id=1, source_target_pairs={{0,3},{1,2},{2,1},{3,0},{4,7},{5,6},{6,5},{7,4},{8,11},{9,10},{10,... | collective-permute-start | bytes 258056 | tf_op jit(solution)/shard_map/ppermute | solution.py:347
  15.9 5.6 %collective-permute-start.7 = (bf16[48,896]{1,0:T(8,128)(2,1)S(1)}, bf16[48,896]{1,0:T(8,128)(2,1)S(1)}, u32[]{:S(2)}, u32[]{:S(2)}) collective-permute-start(bf16[48,896]{1,0:T(8,128)(2,1)S(1)} %get-tuple-element.38), channel_id=1, source_target_pairs={{0,2},{2,0},{4,6},{6,4},{8,10},{10,8},{12,14},{14,12},{1,3},{3,1},... | collective-permute-start | bytes 258056 | tf_op jit(solution)/shard_map/ppermute | solution.py:344
  16.7 4.9 %slice-start.3 = ((s8[14680064]{0:T(1024)(128)(4,1)}), s8[2097152]{0:T(1024)(128)(4,1)S(1)}, s32[]{:S(2)}) async-start(s8[14680064]{0:T(1024)(128)(4,1)} %bitcast.7), calls=%async_computation.3 | async-start | bytes 4194304
  16.7 5.1 %slice-start.7 = ((s8[14680064]{0:T(1024)(128)(4,1)}), s8[2097152]{0:T(1024)(128)(4,1)S(1)}, s32[]{:S(2)}) async-start(s8[14680064]{0:T(1024)(128)(4,1)} %bitcast.10), calls=%async_computation.7 | async-start | bytes 4194304
  16.7 4.9 %collective-permute-start.6 = (bf16[48,896]{1,0:T(8,128)(2,1)S(1)}, bf16[48,896]{1,0:T(8,128)(2,1)S(1)}, u32[]{:S(2)}, u32[]{:S(2)}) collective-permute-start(bf16[48,896]{1,0:T(8,128)(2,1)S(1)} %get-tuple-element.37.after.refs_4_), channel_id=1, source_target_pairs={{0,1},{1,0},{2,3},{3,2},{4,5},{5,4},{6,7},{7,6},{8,9},{9,8},{10,11... | collective-permute-start | bytes 258056 | tf_op jit(solution)/shard_map/ppermute | solution.py:341
  21.8 25.4 %copy-start = (f32[8,2]{0,1:T(2,128)S(1)}, f32[8,2]{0,1:T(2,128)}, u32[]{:S(2)}) copy-start(f32[8,2]{0,1:T(2,128)} %param.11) | copy-start | bytes 196
  29.5 4.4 %collective-permute-start.9 = (bf16[48,896]{1,0:T(8,128)(2,1)S(1)}, bf16[48,896]{1,0:T(8,128)(2,1)S(1)}, u32[]{:S(2)}, u32[]{:S(2)}) collective-permute-start(bf16[48,896]{1,0:T(8,128)(2,1)S(1)} %get-tuple-element.44), channel_id=1, source_target_pairs={{0,3},{1,2},{2,1},{3,0},{4,7},{5,6},{6,5},{7,4},{8,11},{9,10},{10,... | collective-permute-start | bytes 258056 | tf_op jit(solution)/shard_map/ppermute | solution.py:347
  30.6 5.7 %collective-permute-start.10 = (bf16[48,896]{1,0:T(8,128)(2,1)S(1)}, bf16[48,896]{1,0:T(8,128)(2,1)S(1)}, u32[]{:S(2)}, u32[]{:S(2)}) collective-permute-start(bf16[48,896]{1,0:T(8,128)(2,1)S(1)} %get-tuple-element.45), channel_id=1, source_target_pairs={{0,1},{1,0},{2,3},{3,2},{4,5},{5,4},{6,7},{7,6},{8,9},{9,8},{10,11... | collective-permute-start | bytes 258056 | tf_op jit(solution)/shard_map/ppermute | solution.py:341
  31.6 4.7 %collective-permute-start.11 = (bf16[48,896]{1,0:T(8,128)(2,1)S(1)}, bf16[48,896]{1,0:T(8,128)(2,1)S(1)}, u32[]{:S(2)}, u32[]{:S(2)}) collective-permute-start(bf16[48,896]{1,0:T(8,128)(2,1)S(1)} %get-tuple-element.46), channel_id=1, source_target_pairs={{0,2},{2,0},{4,6},{6,4},{8,10},{10,8},{12,14},{14,12},{1,3},{3,1},... | collective-permute-start | bytes 258056 | tf_op jit(solution)/shard_map/ppermute | solution.py:344
  31.7 8.8 %collective-permute-start.12 = (bf16[48,896]{1,0:T(8,128)(2,1)S(1)}, bf16[48,896]{1,0:T(8,128)(2,1)S(1)}, u32[]{:S(2)}, u32[]{:S(2)}) collective-permute-start(bf16[48,896]{1,0:T(8,128)(2,1)S(1)} %get-tuple-element.48), channel_id=1, source_target_pairs={{0,3},{1,2},{2,1},{3,0},{4,7},{5,6},{6,5},{7,4},{8,11},{9,10},{10,... | collective-permute-start | bytes 258056 | tf_op jit(solution)/shard_map/ppermute | solution.py:347
  33.0 7.4 %collective-permute-start.13 = (bf16[48,896]{1,0:T(8,128)(2,1)S(1)}, bf16[48,896]{1,0:T(8,128)(2,1)S(1)}, u32[]{:S(2)}, u32[]{:S(2)}) collective-permute-start(bf16[48,896]{1,0:T(8,128)(2,1)S(1)} %get-tuple-element.49), channel_id=1, source_target_pairs={{0,1},{1,0},{2,3},{3,2},{4,5},{5,4},{6,7},{7,6},{8,9},{9,8},{10,11... | collective-permute-start | bytes 258056 | tf_op jit(solution)/shard_map/ppermute | solution.py:341
  33.9 6.6 %collective-permute-start.14 = (bf16[48,896]{1,0:T(8,128)(2,1)S(1)}, bf16[48,896]{1,0:T(8,128)(2,1)S(1)}, u32[]{:S(2)}, u32[]{:S(2)}) collective-permute-start(bf16[48,896]{1,0:T(8,128)(2,1)S(1)} %get-tuple-element.50), channel_id=1, source_target_pairs={{0,2},{2,0},{4,6},{6,4},{8,10},{10,8},{12,14},{14,12},{1,3},{3,1},... | collective-permute-start | bytes 258056 | tf_op jit(solution)/shard_map/ppermute | solution.py:344
  36.5 9.1 %collective-permute-start.17 = (bf16[48,896]{1,0:T(8,128)(2,1)S(1)}, bf16[48,896]{1,0:T(8,128)(2,1)S(1)}, u32[]{:S(2)}, u32[]{:S(2)}) collective-permute-start(bf16[48,896]{1,0:T(8,128)(2,1)S(1)} %get-tuple-element.54), channel_id=1, source_target_pairs={{0,12},{2,14},{4,8},{6,10},{8,4},{10,6},{12,0},{14,2},{1,13},{3,15... | collective-permute-start | bytes 258056 | tf_op jit(solution)/shard_map/ppermute | solution.py:338
  40.4 6.8 %collective-permute-start.16 = (bf16[48,896]{1,0:T(8,128)(2,1)S(1)}, bf16[48,896]{1,0:T(8,128)(2,1)S(1)}, u32[]{:S(2)}, u32[]{:S(2)}) collective-permute-start(bf16[48,896]{1,0:T(8,128)(2,1)S(1)} %get-tuple-element.47.after), channel_id=1, source_target_pairs={{0,8},{2,10},{4,12},{6,14},{8,0},{10,2},{12,4},{14,6},{1,9},{3,11}... | collective-permute-start | bytes 258056 | tf_op jit(solution)/shard_map/ppermute | solution.py:338
  40.7 6.6 %collective-permute-start.15 = (bf16[48,896]{1,0:T(8,128)(2,1)S(1)}, bf16[48,896]{1,0:T(8,128)(2,1)S(1)}, u32[]{:S(2)}, u32[]{:S(2)}) collective-permute-start(bf16[48,896]{1,0:T(8,128)(2,1)S(1)} %get-tuple-element.53), channel_id=1, source_target_pairs={{0,4},{2,6},{4,0},{6,2},{8,12},{10,14},{12,8},{14,10},{1,5},{3,7},... | collective-permute-start | bytes 258056 | tf_op jit(solution)/shard_map/ppermute | solution.py:338

commit v7 on v6

--- a/solution.py
+++ b/solution.py
@@ -76,7 +76,8 @@
 
 
 PIECES = 8
-FETCHED = (2, 1, 5)
+CUTS = 4
+FETCHED = (1, 1, 6)
 
 
 def iota(shape, dim):
@@ -239,11 +240,14 @@
 
 def fetch_kernel(start, count, wide, after, weights, got, done, sems):
     del after
+    rows = wide // CUTS
     copies = [
         pltpu.make_async_copy(
-            weights.at[pl.ds((start + p) * wide, wide)], got.at[pl.ds(p * wide, wide)], sems.at[p]
+            weights.at[pl.ds(start * wide + p * rows, rows)],
+            got.at[pl.ds(p * rows, rows)],
+            sems.at[p],
         )
-        for p in range(count)
+        for p in range(count * CUTS)
     ]
     for copy in copies:
         copy.start()
@@ -365,7 +369,7 @@
             functools.partial(fetch_kernel, begin, count, wide),
             "fetch",
             (pltpu.VMEM((count * wide, units), bf16), jax.ShapeDtypeStruct((8, 128), jnp.float32)),
-            [HBM] * 2, (VMEM, VMEM), [DMA((count,))], 1 * MIB, (after, w_up),
+            [HBM] * 2, (VMEM, VMEM), [DMA((count * CUTS,))], 1 * MIB, (after, w_up),
             moved=2 * count * wide * units,
         )
         got_up.append(fetched)

time: 48.3 us -> 48.8 us (1.010)
  waiting for transfers between devices: 3.8 us -> 4.91 us
    ppermute x4, starting transfers between devices: 4 us -> 3.02 us  [across(): return lax.ppermute(x, ('ep', 'dp'), [(i, i ^ 3) for i in range(2 * n_ep)])]
    ppermute x4, waiting for transfers between devices: 0.1 us -> 0.67 us  [across(): return lax.ppermute(x, ('ep', 'dp'), [(i, i ^ 3) for i in range(2 * n_ep)])]
    ppermute x6, waiting for transfers between devices: 1.64 us -> 2.19 us  [to_chip(): return lax.ppermute(x, 'ep', [(i, i ^ CORES * d) for i in range(n_ep)])]
  transfers between devices with their start and end apart: 18 -> 18, of which waited for: 3 -> 4; matrix products, arithmetic and copies ran while one was open for 0% -> 0% of each run, Pallas kernels for 29% -> 29%
where the time goes in v7:
time: 48.8 us; the launch traced here: 48.6 us
  Pallas kernels  23.8 us (49%)
  starting transfers between devices  19 us (39%)
  waiting for transfers between devices  4.91 us (10%)
  between operations  0.88 us (2%)
    pallas_call x11, Pallas kernels, call(): pl.pallas_call(kernel, name=name, out_shape=out_shape, in_specs=in_specs,...  23.8 us
    ppermute x6, starting transfers between devices, to_chip(): return lax.ppermute(x, 'ep', [(i, i ^ CORES * d) for i in range(n_ep)])  10.3 us
    ppermute x4, starting transfers between devices, across(): return lax.ppermute(x, ('ep', 'dp'), [(i, i ^ 3) for i in range(2 * n_ep)])  3.02 us
    ppermute x4, starting transfers between devices, beside(): return lax.ppermute(x, 'ep', [(i, i ^ 1) for i in range(n_ep)])  2.91 us
    ppermute x4, starting transfers between devices, along(): return lax.ppermute(x, 'dp', [(0, 1), (1, 0)])  2.76 us
    ppermute x6, waiting for transfers between devices, to_chip(): return lax.ppermute(x, 'ep', [(i, i ^ CORES * d) for i in range(n_ep)])  2.19 us
    ppermute x4, waiting for transfers between devices, along(): return lax.ppermute(x, 'dp', [(0, 1), (1, 0)])  2.03 us
  transfers between devices with their start and end apart: 18, of which 4 were waited for; matrix products, arithmetic and copies ran while one was open for 0% of the time, Pallas kernels for 29%

profile of v7, /device:TPU:0, one launch (start us, length us, event | category | flops | bytes accessed | tf_op | source)
XLA Modules:
  0.0 48.6 jit_solution(1402211903869704838)
XLA Ops:
  0.6 1.3 %pack.1 = (bf16[48,896]{1,0:T(8,128)(2,1)S(1)}, bf16[48,896]{1,0:T(8,128)(2,1)S(1)}, bf16[48,896]{1,0:T(8,128)(2,1)S(1)}, bf16[48,896]{1,0:T(8,128)(2,1)S(1)}) custom-call(s32[2,8]{1,0:T(2,128)} %bitcast.19, bf16[8,7168]{1,0:T(8,128)(2,1)} %tok_hbm.1), custom_call_target="tpu_custom_call" | custom-call | tf_op jit(solution)/shard_map/pack/pallas_call | solution.py:312
  1.9 3.1 %collective-permute-start = (bf16[48,896]{1,0:T(8,128)(2,1)S(1)}, bf16[48,896]{1,0:T(8,128)(2,1)S(1)}, u32[]{:S(2)}, u32[]{:S(2)}) collective-permute-start(bf16[48,896]{1,0:T(8,128)(2,1)S(1)} %get-tuple-element.31), channel_id=1, source_target_pairs={{0,4},{2,6},{4,0},{6,2},{8,12},{10,14},{12,8},{14,10},{1,5},{3,7},... | collective-permute-start | bytes 258056 | tf_op jit(solution)/shard_map/ppermute | solution.py:342
  5.0 2.6 %collective-permute-start.4 = (bf16[48,896]{1,0:T(8,128)(2,1)S(1)}, bf16[48,896]{1,0:T(8,128)(2,1)S(1)}, u32[]{:S(2)}, u32[]{:S(2)}) collective-permute-start(bf16[48,896]{1,0:T(8,128)(2,1)S(1)} %get-tuple-element.35), channel_id=1, source_target_pairs={{0,8},{2,10},{4,12},{6,14},{8,0},{10,2},{12,4},{14,6},{1,9},{3,11}... | collective-permute-start | bytes 258056 | tf_op jit(solution)/shard_map/ppermute | solution.py:342
  7.6 0.0 collective-permute-start.5
  7.6 0.0 slice-start.5
  7.6 1.6 %fetch.3 = (bf16[896,1024]{1,0:T(8,128)(2,1)S(1)}, f32[8,128]{1,0:T(8,128)S(1)}) custom-call(bf16[48,896]{1,0:T(8,128)(2,1)S(1)} %get-tuple-element.29.after.refs_0_, bf16[7168,1024]{1,0:T(8,128)(2,1)} %bitcast.14), custom_call_target="tpu_custom_call" | custom-call | bytes 1835008 | tf_op jit(solution)/shard_map/fetch/pallas_call | solution.py:312
  9.3 0.0 collective-permute-done.refs_1_
  9.3 0.2 near.2
  9.5 0.4 collective-permute-start.3
  9.9 1.4 %collective-permute-start.2 = (bf16[48,896]{1,0:T(8,128)(2,1)S(1)}, bf16[48,896]{1,0:T(8,128)(2,1)S(1)}, u32[]{:S(2)}, u32[]{:S(2)}) collective-permute-start(bf16[48,896]{1,0:T(8,128)(2,1)S(1)} %get-tuple-element.33), channel_id=1, source_target_pairs={{0,2},{2,0},{4,6},{6,4},{8,10},{10,8},{12,14},{14,12},{1,3},{3,1},... | collective-permute-start | bytes 258056 | tf_op jit(solution)/shard_map/ppermute | solution.py:348
  11.4 0.3 collective-permute-start.1
  11.7 2.3 %fetch.4 = (bf16[896,1024]{1,0:T(8,128)(2,1)S(1)}, f32[8,128]{1,0:T(8,128)S(1)}) custom-call(bf16[48,896]{1,0:T(8,128)(2,1)S(1)} %get-tuple-element.32.after.refs_0_, bf16[7168,1024]{1,0:T(8,128)(2,1)} %bitcast.15), custom_call_target="tpu_custom_call" | custom-call | bytes 1835008 | tf_op jit(solution)/shard_map/fetch/pallas_call | solution.py:312
  13.9 0.6 %collective-permute-done.4.refs_0_ = bf16[48,896]{1,0:T(8,128)(2,1)S(1)} collective-permute-done((bf16[48,896]{1,0:T(8,128)(2,1)S(1)}, bf16[48,896]{1,0:T(8,128)(2,1)S(1)}, u32[]{:S(2)}, u32[]{:S(2)}) %collective-permute-start.4) | collective-permute-done | bytes 86048 | tf_op jit(solution)/shard_map/ppermute | solution.py:342
  14.5 0.0 collective-permute-done.5.refs_1_
  14.5 0.2 near.3
  14.7 0.6 %collective-permute-start.8 = (bf16[48,896]{1,0:T(8,128)(2,1)S(1)}, bf16[48,896]{1,0:T(8,128)(2,1)S(1)}, u32[]{:S(2)}, u32[]{:S(2)}) collective-permute-start(bf16[48,896]{1,0:T(8,128)(2,1)S(1)} %get-tuple-element.38), channel_id=1, source_target_pairs={{0,3},{1,2},{2,1},{3,0},{4,7},{5,6},{6,5},{7,4},{8,11},{9,10},{10,... | collective-permute-start | bytes 258056 | tf_op jit(solution)/shard_map/ppermute | solution.py:351
  15.3 1.1 %collective-permute-start.7 = (bf16[48,896]{1,0:T(8,128)(2,1)S(1)}, bf16[48,896]{1,0:T(8,128)(2,1)S(1)}, u32[]{:S(2)}, u32[]{:S(2)}) collective-permute-start(bf16[48,896]{1,0:T(8,128)(2,1)S(1)} %get-tuple-element.38), channel_id=1, source_target_pairs={{0,2},{2,0},{4,6},{6,4},{8,10},{10,8},{12,14},{14,12},{1,3},{3,1},... | collective-permute-start | bytes 258056 | tf_op jit(solution)/shard_map/ppermute | solution.py:348
  16.4 0.0 collective-permute-done.3.refs_3_
  16.4 0.5 %collective-permute-start.6 = (bf16[48,896]{1,0:T(8,128)(2,1)S(1)}, bf16[48,896]{1,0:T(8,128)(2,1)S(1)}, u32[]{:S(2)}, u32[]{:S(2)}) collective-permute-start(bf16[48,896]{1,0:T(8,128)(2,1)S(1)} %get-tuple-element.37.after.refs_4_), channel_id=1, source_target_pairs={{0,1},{1,0},{2,3},{3,2},{4,5},{5,4},{6,7},{7,6},{8,9},{9,8},{10,11... | collective-permute-start | bytes 258056 | tf_op jit(solution)/shard_map/ppermute | solution.py:345
  16.9 5.1 %fetch.5 = (bf16[5376,1024]{1,0:T(8,128)(2,1)S(1)}, f32[8,128]{1,0:T(8,128)}) custom-call(bf16[48,896]{1,0:T(8,128)(2,1)S(1)} %get-tuple-element.37.after.refs_4_, bf16[7168,1024]{1,0:T(8,128)(2,1)} %bitcast.16), custom_call_target="tpu_custom_call" | custom-call | bytes 11010048 | tf_op jit(solution)/shard_map/fetch/pallas_call | solution.py:312
  22.1 0.0 collective-permute-done.2.refs_2_
  22.1 0.0 collective-permute-done.1.refs_1_
  22.1 0.0 collective-permute-done.8.refs_7_
  22.1 0.0 collective-permute-done.7.refs_6_
  22.1 0.0 collective-permute-done.6.refs_5_
  22.2 0.0 copy-start
  22.2 7.6 %experts.1 = (bf16[48,896]{1,0:T(8,128)(2,1)S(1)}, bf16[48,896]{1,0:T(8,128)(2,1)S(1)}, bf16[48,896]{1,0:T(8,128)(2,1)S(1)}, bf16[48,896]{1,0:T(8,128)(2,1)S(1)}...) custom-call(bf16[48,896]{1,0:T(8,128)(2,1)S(1)} %get-tuple-element.3, ...), custom_call_target="tpu_custom_call" | custom-call | flops 2113929216 | tf_op jit(solution)/shard_map/experts/pallas_call | solution.py:312
  29.9 0.7 %collective-permute-start.9 = (bf16[48,896]{1,0:T(8,128)(2,1)S(1)}, bf16[48,896]{1,0:T(8,128)(2,1)S(1)}, u32[]{:S(2)}, u32[]{:S(2)}) collective-permute-start(bf16[48,896]{1,0:T(8,128)(2,1)S(1)} %get-tuple-element.44), channel_id=1, source_target_pairs={{0,3},{1,2},{2,1},{3,0},{4,7},{5,6},{6,5},{7,4},{8,11},{9,10},{10,... | collective-permute-start | bytes 258056 | tf_op jit(solution)/shard_map/ppermute | solution.py:351
  30.6 1.1 %collective-permute-start.10 = (bf16[48,896]{1,0:T(8,128)(2,1)S(1)}, bf16[48,896]{1,0:T(8,128)(2,1)S(1)}, u32[]{:S(2)}, u32[]{:S(2)}) collective-permute-start(bf16[48,896]{1,0:T(8,128)(2,1)S(1)} %get-tuple-element.45), channel_id=1, source_target_pairs={{0,1},{1,0},{2,3},{3,2},{4,5},{5,4},{6,7},{7,6},{8,9},{9,8},{10,11... | collective-permute-start | bytes 258056 | tf_op jit(solution)/shard_map/ppermute | solution.py:345
  31.7 0.1 collective-permute-start.11
  31.8 1.3 %collective-permute-start.12 = (bf16[48,896]{1,0:T(8,128)(2,1)S(1)}, bf16[48,896]{1,0:T(8,128)(2,1)S(1)}, u32[]{:S(2)}, u32[]{:S(2)}) collective-permute-start(bf16[48,896]{1,0:T(8,128)(2,1)S(1)} %get-tuple-element.48), channel_id=1, source_target_pairs={{0,3},{1,2},{2,1},{3,0},{4,7},{5,6},{6,5},{7,4},{8,11},{9,10},{10,... | collective-permute-start | bytes 258056 | tf_op jit(solution)/shard_map/ppermute | solution.py:351
  33.1 0.8 %collective-permute-start.13 = (bf16[48,896]{1,0:T(8,128)(2,1)S(1)}, bf16[48,896]{1,0:T(8,128)(2,1)S(1)}, u32[]{:S(2)}, u32[]{:S(2)}) collective-permute-start(bf16[48,896]{1,0:T(8,128)(2,1)S(1)} %get-tuple-element.49), channel_id=1, source_target_pairs={{0,1},{1,0},{2,3},{3,2},{4,5},{5,4},{6,7},{7,6},{8,9},{9,8},{10,11... | collective-permute-start | bytes 258056 | tf_op jit(solution)/shard_map/ppermute | solution.py:345
  33.9 0.7 %collective-permute-done.9.across = bf16[48,896]{1,0:T(8,128)(2,1)S(1)} collective-permute-done((bf16[48,896]{1,0:T(8,128)(2,1)S(1)}, bf16[48,896]{1,0:T(8,128)(2,1)S(1)}, u32[]{:S(2)}, u32[]{:S(2)}) %collective-permute-start.9) | collective-permute-done | bytes 86048 | tf_op jit(solution)/shard_map/ppermute | solution.py:351
  34.5 0.3 collective-permute-start.14
  34.8 2.0 %collective-permute-done.10.along = bf16[48,896]{1,0:T(8,128)(2,1)S(1)} collective-permute-done((bf16[48,896]{1,0:T(8,128)(2,1)S(1)}, bf16[48,896]{1,0:T(8,128)(2,1)S(1)}, u32[]{:S(2)}, u32[]{:S(2)}) %collective-permute-start.10) | collective-permute-done | bytes 86048 | tf_op jit(solution)/shard_map/ppermute | solution.py:345
  36.8 0.0 collective-permute-done.11.beside
  36.8 0.2 sums.2
  37.1 3.4 %collective-permute-start.17 = (bf16[48,896]{1,0:T(8,128)(2,1)S(1)}, bf16[48,896]{1,0:T(8,128)(2,1)S(1)}, u32[]{:S(2)}, u32[]{:S(2)}) collective-permute-start(bf16[48,896]{1,0:T(8,128)(2,1)S(1)} %get-tuple-element.54), channel_id=1, source_target_pairs={{0,12},{2,14},{4,8},{6,10},{8,4},{10,6},{12,0},{14,2},{1,13},{3,15... | collective-permute-start | bytes 258056 | tf_op jit(solution)/shard_map/ppermute | solution.py:342
  40.4 0.0 collective-permute-start.16
  40.4 0.0 collective-permute-done.12.across
  40.4 0.0 collective-permute-done.13.along
  40.4 0.2 sums.3
  40.7 1.2 %collective-permute-start.15 = (bf16[48,896]{1,0:T(8,128)(2,1)S(1)}, bf16[48,896]{1,0:T(8,128)(2,1)S(1)}, u32[]{:S(2)}, u32[]{:S(2)}) collective-permute-start(bf16[48,896]{1,0:T(8,128)(2,1)S(1)} %get-tuple-element.53), channel_id=1, source_target_pairs={{0,4},{2,6},{4,0},{6,2},{8,12},{10,14},{12,8},{14,10},{1,5},{3,7},... | collective-permute-start | bytes 258056 | tf_op jit(solution)/shard_map/ppermute | solution.py:342
  41.9 4.2 %attend.1 = (bf16[2,128,512]{2,1,0:T(8,128)(2,1)}, bf16[128,192]{1,0:T(8,128)(2,1)S(1)}) custom-call(bf16[48,896]{1,0:T(8,128)(2,1)S(1)} %get-tuple-element.51.after.refs_0_, s32[2]{0:T(128)} %lengths.1, s32[2,8]{1,0:T(2,128)} %bitcast.20, bf16[2,576,128]{2,1,0:T(8,128)(2,1)} %bitcast.18, bf16[2,576,512]{2,1,0:T(8,128)(2,1)} %bitcast.17), custom_call_target="tpu_custom_call" | custom-call | bytes 1179648 | tf_op jit(solution)/shard_map/attend/pallas_call | solution.py:312
  46.1 0.0 collective-permute-done.17.refs_3_
  46.1 1.6 %collective-permute-done.16.refs_2_ = bf16[48,896]{1,0:T(8,128)(2,1)S(1)} collective-permute-done((bf16[48,896]{1,0:T(8,128)(2,1)S(1)}, bf16[48,896]{1,0:T(8,128)(2,1)S(1)}, u32[]{:S(2)}, u32[]{:S(2)}) %collective-permute-start.16) | collective-permute-done | bytes 86048 | tf_op jit(solution)/shard_map/ppermute | solution.py:342
  47.7 0.0 collective-permute-done.15.refs_1_
  47.8 0.9 %combine.1 = bf16[8,7168]{1,0:T(8,128)(2,1)} custom-call(bf16[128,192]{1,0:T(8,128)(2,1)S(1)} %get-tuple-element.52.picks_ref, f32[2,8]{1,0:T(2,128)S(1)} %bitcast.13, bf16[48,896]{1,0:T(8,128)(2,1)S(1)} %get-tuple-element.51.after.refs_0_, bf16[48,896]{1,0:T(8,128)(2,1)S(1)} %collective-permute-done.15.refs_1_, ...), custom_call_target="tpu_custom_call" | custom-call | tf_op jit(solution)/shard_map/combine/pallas_call | solution.py:312
  (19 shorter events, 0.0 us)
Async XLA Ops:
  1.9 7.3 %collective-permute-start = (bf16[48,896]{1,0:T(8,128)(2,1)S(1)}, bf16[48,896]{1,0:T(8,128)(2,1)S(1)}, u32[]{:S(2)}, u32[]{:S(2)}) collective-permute-start(bf16[48,896]{1,0:T(8,128)(2,1)S(1)} %get-tuple-element.31), channel_id=1, source_target_pairs={{0,4},{2,6},{4,0},{6,2},{8,12},{10,14},{12,8},{14,10},{1,5},{3,7},... | collective-permute-start | bytes 258056 | tf_op jit(solution)/shard_map/ppermute | solution.py:342
  5.0 9.5 %collective-permute-start.4 = (bf16[48,896]{1,0:T(8,128)(2,1)S(1)}, bf16[48,896]{1,0:T(8,128)(2,1)S(1)}, u32[]{:S(2)}, u32[]{:S(2)}) collective-permute-start(bf16[48,896]{1,0:T(8,128)(2,1)S(1)} %get-tuple-element.35), channel_id=1, source_target_pairs={{0,8},{2,10},{4,12},{6,14},{8,0},{10,2},{12,4},{14,6},{1,9},{3,11}... | collective-permute-start | bytes 258056 | tf_op jit(solution)/shard_map/ppermute | solution.py:342
  7.6 6.9 %collective-permute-start.5 = (bf16[48,896]{1,0:T(8,128)(2,1)S(1)}, bf16[48,896]{1,0:T(8,128)(2,1)S(1)}, u32[]{:S(2)}, u32[]{:S(2)}) collective-permute-start(bf16[48,896]{1,0:T(8,128)(2,1)S(1)} %get-tuple-element.36), channel_id=1, source_target_pairs={{0,12},{2,14},{4,8},{6,10},{8,4},{10,6},{12,0},{14,2},{1,13},{3,15... | collective-permute-start | bytes 258056 | tf_op jit(solution)/shard_map/ppermute | solution.py:342
  7.6 14.5 %slice-start = ((s8[14680064]{0:T(1024)(128)(4,1)}), s8[4194304]{0:T(1024)(128)(4,1)S(1)}, s32[]{:S(2)}) async-start(s8[14680064]{0:T(1024)(128)(4,1)} %bitcast.7), calls=%async_computation | async-start | bytes 8388608
  7.6 14.5 %slice-start.1 = ((s8[14680064]{0:T(1024)(128)(4,1)}), s8[4194304]{0:T(1024)(128)(4,1)S(1)}, s32[]{:S(2)}) async-start(s8[14680064]{0:T(1024)(128)(4,1)} %bitcast.7), calls=%async_computation.1 | async-start | bytes 8388608
  7.6 14.5 %slice-start.4 = ((s8[14680064]{0:T(1024)(128)(4,1)}), s8[4194304]{0:T(1024)(128)(4,1)S(1)}, s32[]{:S(2)}) async-start(s8[14680064]{0:T(1024)(128)(4,1)} %bitcast.10), calls=%async_computation.4 | async-start | bytes 8388608
  7.6 14.5 %slice-start.5 = ((s8[14680064]{0:T(1024)(128)(4,1)}), s8[4194304]{0:T(1024)(128)(4,1)S(1)}, s32[]{:S(2)}) async-start(s8[14680064]{0:T(1024)(128)(4,1)} %bitcast.10), calls=%async_computation.5 | async-start | bytes 8388608
  9.5 6.9 %collective-permute-start.3 = (bf16[48,896]{1,0:T(8,128)(2,1)S(1)}, bf16[48,896]{1,0:T(8,128)(2,1)S(1)}, u32[]{:S(2)}, u32[]{:S(2)}) collective-permute-start(bf16[48,896]{1,0:T(8,128)(2,1)S(1)} %get-tuple-element.33), channel_id=1, source_target_pairs={{0,3},{1,2},{2,1},{3,0},{4,7},{5,6},{6,5},{7,4},{8,11},{9,10},{10,... | collective-permute-start | bytes 258056 | tf_op jit(solution)/shard_map/ppermute | solution.py:351
  9.9 12.2 %collective-permute-start.2 = (bf16[48,896]{1,0:T(8,128)(2,1)S(1)}, bf16[48,896]{1,0:T(8,128)(2,1)S(1)}, u32[]{:S(2)}, u32[]{:S(2)}) collective-permute-start(bf16[48,896]{1,0:T(8,128)(2,1)S(1)} %get-tuple-element.33), channel_id=1, source_target_pairs={{0,2},{2,0},{4,6},{6,4},{8,10},{10,8},{12,14},{14,12},{1,3},{3,1},... | collective-permute-start | bytes 258056 | tf_op jit(solution)/shard_map/ppermute | solution.py:348
  11.3 10.8 %slice-start.2 = ((s8[14680064]{0:T(1024)(128)(4,1)}), s8[4194304]{0:T(1024)(128)(4,1)S(1)}, s32[]{:S(2)}) async-start(s8[14680064]{0:T(1024)(128)(4,1)} %bitcast.7), calls=%async_computation.2 | async-start | bytes 8388608
  11.3 10.8 %slice-start.6 = ((s8[14680064]{0:T(1024)(128)(4,1)}), s8[4194304]{0:T(1024)(128)(4,1)S(1)}, s32[]{:S(2)}) async-start(s8[14680064]{0:T(1024)(128)(4,1)} %bitcast.10), calls=%async_computation.6 | async-start | bytes 8388608
  11.4 10.7 %collective-permute-start.1 = (bf16[48,896]{1,0:T(8,128)(2,1)S(1)}, bf16[48,896]{1,0:T(8,128)(2,1)S(1)}, u32[]{:S(2)}, u32[]{:S(2)}) collective-permute-start(bf16[48,896]{1,0:T(8,128)(2,1)S(1)} %get-tuple-element.32.after.refs_0_), channel_id=1, source_target_pairs={{0,1},{1,0},{2,3},{3,2},{4,5},{5,4},{6,7},{7,6},{8,9},{9,8},{10,11... | collective-permute-start | bytes 258056 | tf_op jit(solution)/shard_map/ppermute | solution.py:345
  14.7 7.4 %collective-permute-start.8 = (bf16[48,896]{1,0:T(8,128)(2,1)S(1)}, bf16[48,896]{1,0:T(8,128)(2,1)S(1)}, u32[]{:S(2)}, u32[]{:S(2)}) collective-permute-start(bf16[48,896]{1,0:T(8,128)(2,1)S(1)} %get-tuple-element.38), channel_id=1, source_target_pairs={{0,3},{1,2},{2,1},{3,0},{4,7},{5,6},{6,5},{7,4},{8,11},{9,10},{10,... | collective-permute-start | bytes 258056 | tf_op jit(solution)/shard_map/ppermute | solution.py:351
  15.3 6.8 %collective-permute-start.7 = (bf16[48,896]{1,0:T(8,128)(2,1)S(1)}, bf16[48,896]{1,0:T(8,128)(2,1)S(1)}, u32[]{:S(2)}, u32[]{:S(2)}) collective-permute-start(bf16[48,896]{1,0:T(8,128)(2,1)S(1)} %get-tuple-element.38), channel_id=1, source_target_pairs={{0,2},{2,0},{4,6},{6,4},{8,10},{10,8},{12,14},{14,12},{1,3},{3,1},... | collective-permute-start | bytes 258056 | tf_op jit(solution)/shard_map/ppermute | solution.py:348
  16.4 5.8 %slice-start.3 = ((s8[14680064]{0:T(1024)(128)(4,1)}), s8[2097152]{0:T(1024)(128)(4,1)S(1)}, s32[]{:S(2)}) async-start(s8[14680064]{0:T(1024)(128)(4,1)} %bitcast.7), calls=%async_computation.3 | async-start | bytes 4194304
  16.4 5.8 %slice-start.7 = ((s8[14680064]{0:T(1024)(128)(4,1)}), s8[2097152]{0:T(1024)(128)(4,1)S(1)}, s32[]{:S(2)}) async-start(s8[14680064]{0:T(1024)(128)(4,1)} %bitcast.10), calls=%async_computation.7 | async-start | bytes 4194304
  16.4 5.7 %collective-permute-start.6 = (bf16[48,896]{1,0:T(8,128)(2,1)S(1)}, bf16[48,896]{1,0:T(8,128)(2,1)S(1)}, u32[]{:S(2)}, u32[]{:S(2)}) collective-permute-start(bf16[48,896]{1,0:T(8,128)(2,1)S(1)} %get-tuple-element.37.after.refs_4_), channel_id=1, source_target_pairs={{0,1},{1,0},{2,3},{3,2},{4,5},{5,4},{6,7},{7,6},{8,9},{9,8},{10,11... | collective-permute-start | bytes 258056 | tf_op jit(solution)/shard_map/ppermute | solution.py:345
  22.2 25.5 %copy-start = (f32[8,2]{0,1:T(2,128)S(1)}, f32[8,2]{0,1:T(2,128)}, u32[]{:S(2)}) copy-start(f32[8,2]{0,1:T(2,128)} %param.11) | copy-start | bytes 196
  29.9 4.7 %collective-permute-start.9 = (bf16[48,896]{1,0:T(8,128)(2,1)S(1)}, bf16[48,896]{1,0:T(8,128)(2,1)S(1)}, u32[]{:S(2)}, u32[]{:S(2)}) collective-permute-start(bf16[48,896]{1,0:T(8,128)(2,1)S(1)} %get-tuple-element.44), channel_id=1, source_target_pairs={{0,3},{1,2},{2,1},{3,0},{4,7},{5,6},{6,5},{7,4},{8,11},{9,10},{10,... | collective-permute-start | bytes 258056 | tf_op jit(solution)/shard_map/ppermute | solution.py:351
  30.6 6.2 %collective-permute-start.10 = (bf16[48,896]{1,0:T(8,128)(2,1)S(1)}, bf16[48,896]{1,0:T(8,128)(2,1)S(1)}, u32[]{:S(2)}, u32[]{:S(2)}) collective-permute-start(bf16[48,896]{1,0:T(8,128)(2,1)S(1)} %get-tuple-element.45), channel_id=1, source_target_pairs={{0,1},{1,0},{2,3},{3,2},{4,5},{5,4},{6,7},{7,6},{8,9},{9,8},{10,11... | collective-permute-start | bytes 258056 | tf_op jit(solution)/shard_map/ppermute | solution.py:345
  31.7 5.1 %collective-permute-start.11 = (bf16[48,896]{1,0:T(8,128)(2,1)S(1)}, bf16[48,896]{1,0:T(8,128)(2,1)S(1)}, u32[]{:S(2)}, u32[]{:S(2)}) collective-permute-start(bf16[48,896]{1,0:T(8,128)(2,1)S(1)} %get-tuple-element.46), channel_id=1, source_target_pairs={{0,2},{2,0},{4,6},{6,4},{8,10},{10,8},{12,14},{14,12},{1,3},{3,1},... | collective-permute-start | bytes 258056 | tf_op jit(solution)/shard_map/ppermute | solution.py:348
  31.8 8.7 %collective-permute-start.12 = (bf16[48,896]{1,0:T(8,128)(2,1)S(1)}, bf16[48,896]{1,0:T(8,128)(2,1)S(1)}, u32[]{:S(2)}, u32[]{:S(2)}) collective-permute-start(bf16[48,896]{1,0:T(8,128)(2,1)S(1)} %get-tuple-element.48), channel_id=1, source_target_pairs={{0,3},{1,2},{2,1},{3,0},{4,7},{5,6},{6,5},{7,4},{8,11},{9,10},{10,... | collective-permute-start | bytes 258056 | tf_op jit(solution)/shard_map/ppermute | solution.py:351
  33.1 7.4 %collective-permute-start.13 = (bf16[48,896]{1,0:T(8,128)(2,1)S(1)}, bf16[48,896]{1,0:T(8,128)(2,1)S(1)}, u32[]{:S(2)}, u32[]{:S(2)}) collective-permute-start(bf16[48,896]{1,0:T(8,128)(2,1)S(1)} %get-tuple-element.49), channel_id=1, source_target_pairs={{0,1},{1,0},{2,3},{3,2},{4,5},{5,4},{6,7},{7,6},{8,9},{9,8},{10,11... | collective-permute-start | bytes 258056 | tf_op jit(solution)/shard_map/ppermute | solution.py:345
  34.5 5.9 %collective-permute-start.14 = (bf16[48,896]{1,0:T(8,128)(2,1)S(1)}, bf16[48,896]{1,0:T(8,128)(2,1)S(1)}, u32[]{:S(2)}, u32[]{:S(2)}) collective-permute-start(bf16[48,896]{1,0:T(8,128)(2,1)S(1)} %get-tuple-element.50), channel_id=1, source_target_pairs={{0,2},{2,0},{4,6},{6,4},{8,10},{10,8},{12,14},{14,12},{1,3},{3,1},... | collective-permute-start | bytes 258056 | tf_op jit(solution)/shard_map/ppermute | solution.py:348
  37.1 9.0 %collective-permute-start.17 = (bf16[48,896]{1,0:T(8,128)(2,1)S(1)}, bf16[48,896]{1,0:T(8,128)(2,1)S(1)}, u32[]{:S(2)}, u32[]{:S(2)}) collective-permute-start(bf16[48,896]{1,0:T(8,128)(2,1)S(1)} %get-tuple-element.54), channel_id=1, source_target_pairs={{0,12},{2,14},{4,8},{6,10},{8,4},{10,6},{12,0},{14,2},{1,13},{3,15... | collective-permute-start | bytes 258056 | tf_op jit(solution)/shard_map/ppermute | solution.py:342
  40.4 7.3 %collective-permute-start.16 = (bf16[48,896]{1,0:T(8,128)(2,1)S(1)}, bf16[48,896]{1,0:T(8,128)(2,1)S(1)}, u32[]{:S(2)}, u32[]{:S(2)}) collective-permute-start(bf16[48,896]{1,0:T(8,128)(2,1)S(1)} %get-tuple-element.47.after), channel_id=1, source_target_pairs={{0,8},{2,10},{4,12},{6,14},{8,0},{10,2},{12,4},{14,6},{1,9},{3,11}... | collective-permute-start | bytes 258056 | tf_op jit(solution)/shard_map/ppermute | solution.py:342
  40.7 7.1 %collective-permute-start.15 = (bf16[48,896]{1,0:T(8,128)(2,1)S(1)}, bf16[48,896]{1,0:T(8,128)(2,1)S(1)}, u32[]{:S(2)}, u32[]{:S(2)}) collective-permute-start(bf16[48,896]{1,0:T(8,128)(2,1)S(1)} %get-tuple-element.53), channel_id=1, source_target_pairs={{0,4},{2,6},{4,0},{6,2},{8,12},{10,14},{12,8},{14,10},{1,5},{3,7},... | collective-permute-start | bytes 258056 | tf_op jit(solution)/shard_map/ppermute | solution.py:342
